TPU v7x, 32 devices: a whole 2x2x4 slice. The times are simulated.
32 devices in a mesh: seq: 8 (over y, x, core), batch: 4 (over z).
Axes of the slice: x: 2, y: 2, z: 4, core: 2. Of those that a mesh axis runs over, the one named last changes fastest.
Arguments:
- layer_input: bfloat16 [4, 2048, 768], P('batch', 'seq'), may hold values from -6 to 6
- segments: int32 [4, 2048], P('batch', 'seq'), may hold values from 0 to 7, never falling along the last dimension, each value on 1 to 800 neighbouring positions
- rand_blocks: int32 [4, 32, 12, 3], P('batch', 'seq'), may hold values from 0 to 31, as said below
- w_qkv: bfloat16 [2, 768, 2304], P(None, ('seq', 'batch')), may hold values from -0.21875 to 0.21875
- w_out: bfloat16 [2, 768, 768], P(None, ('seq', 'batch')), may hold values from -2.5 to 2.5
- w_up: bfloat16 [2, 768, 3072], P(None, ('seq', 'batch')), may hold values from -0.21875 to 0.21875
- w_down: bfloat16 [2, 3072, 768], P(None, ('seq', 'batch')), may hold values from -0.109375 to 0.109375
- gains: bfloat16 [2, 2, 768], P(None, None, ('seq', 'batch')), may hold values from 0.5 to 1.5
- biases: bfloat16 [2, 6, 768], P(None, None, ('seq', 'batch')), may hold values from -2 to 2
- up_bias: bfloat16 [2, 3072], P(None, ('seq', 'batch')), may hold values from -2 to 2
- d_out: bfloat16 [4, 2048, 768], P('batch', 'seq'), may hold values from -6 to 6
Outputs:
- output: bfloat16 [4, 2048, 768], P('batch', 'seq')
- d_input: float32 [4, 2048, 768], P('batch', 'seq')
- grad_w_qkv: float32 [2, 768, 2304], P(None, ('seq', 'batch'))
- grad_w_out: float32 [2, 768, 768], P(None, ('seq', 'batch'))
- grad_w_up: float32 [2, 768, 3072], P(None, ('seq', 'batch'))
- grad_w_down: float32 [2, 3072, 768], P(None, ('seq', 'batch'))
- grad_gains: float32 [2, 2, 768], P(None, None, ('seq', 'batch'))
- grad_biases: float32 [2, 6, 768], P(None, None, ('seq', 'batch'))
- grad_up_bias: float32 [2, 3072], P(None, ('seq', 'batch'))
Inputs may be any that keep to these rules, and one draw needn't show every extreme that they name: `rand_blocks`: for each sequence and each index of seq, the entries of the 4 query blocks held there (all heads and draws) name blocks held by each index of seq between 17 and 18 times, and some index exactly 18 times.
All inputs are finite; a program needn't handle non-finite values.
Results may differ from a plain program's by a relative error of at most 0.02.
Values may be sent and summed in bfloat16 or wider, within the bound.
A program may use at most 256 MiB of HBM per device.

v0:
```python
from functools import partial

import jax
import jax.numpy as jnp
from jax import lax
from jax.sharding import PartitionSpec as P

D = 768
H = 12
DH = 64
BLK = 64
R = 3
GLOB = 2
L = 2


layer_eps = 1e-06
masked_score = -1e30


def padded(x, sides, width):
    for axis, dim in sides:
        devices, length = (lax.axis_size(axis), x.shape[dim])
        up = [(i, (i + 1) % devices) for i in range(devices - 1)]
        down = [(j, i) for i, j in up]
        last = lax.slice_in_dim(x, length - width, length, axis=dim)
        first = lax.slice_in_dim(x, 0, width, axis=dim)
        before = lax.ppermute(last, axis, up)
        after = lax.ppermute(first, axis, down)
        x = jnp.concatenate([before, x, after], axis=dim)
    return x


def from_root(value, axis, source):
    kept = jnp.where(lax.axis_index(axis) == source, value, 0).astype(value.dtype)
    return lax.psum(kept, axis)


def combined_all(x, axis, combine):
    everything = jax.tree.map(lambda part: lax.all_gather(part, axis), x)
    first = jax.tree.map(lambda part: part[0], everything)

    def step(k, so_far):
        return combine(so_far, jax.tree.map(lambda part: part[k], everything))

    return lax.fori_loop(1, lax.axis_size(axis), step, first)


def norm_rows(resid, gain, shift):
    center = resid - jnp.mean(resid, axis=-1, keepdims=True)
    inv_std = lax.rsqrt(jnp.mean(center * center, axis=-1, keepdims=True) + layer_eps)
    normed = center * inv_std
    return (normed * gain + shift, normed, inv_std)


def norm_back(grad_rows, normed, inv_std, gain):
    scaled = grad_rows * gain
    return (
        scaled
        - jnp.mean(scaled, axis=-1, keepdims=True)
        - normed * jnp.mean(scaled * normed, axis=-1, keepdims=True)
    ) * inv_std


def window_view(blocked, block_axis, blocks_here):
    return jnp.concatenate(
        [
            lax.slice_in_dim(blocked, offset, offset + blocks_here, axis=block_axis)
            for offset in range(3)
        ],
        axis=block_axis + 1,
    )


def combine_stats(earlier, latter):
    joint_max = jnp.maximum(earlier[0], latter[0])
    return (
        joint_max,
        earlier[1] * jnp.exp(earlier[0] - joint_max) + latter[1] * jnp.exp(latter[0] - joint_max),
    )


def fetch_layer(layer_index, w_qkv, w_out, w_up, w_down, gains, biases, up_bias):
    return (
        lax.all_gather(w_qkv[layer_index], ("seq", "batch"), axis=0, tiled=True),
        lax.all_gather(w_out[layer_index], ("seq", "batch"), axis=0, tiled=True),
        lax.all_gather(w_up[layer_index], ("seq", "batch"), axis=0, tiled=True),
        lax.all_gather(w_down[layer_index], ("seq", "batch"), axis=0, tiled=True),
        lax.all_gather(gains[layer_index], ("seq", "batch"), axis=1, tiled=True),
        lax.all_gather(biases[layer_index], ("seq", "batch"), axis=1, tiled=True),
        lax.all_gather(up_bias[layer_index], ("seq", "batch"), axis=0, tiled=True),
    )


def decode(codes, blocks_here):
    flat_codes = codes.reshape(-1)
    return (flat_codes // (blocks_here * H), flat_codes // H % blocks_here, flat_codes % H)


def on_device(
    layer_input, segments, rand_blocks, w_qkv, w_out, w_up, w_down, gains, biases, up_bias, d_out
):
    seq_count = lax.axis_size("seq")
    own_index = lax.axis_index("seq")
    groups = layer_input.shape[0]
    local_len = layer_input.shape[1]
    blocks_here = local_len // BLK
    length = local_len * seq_count
    global_width = GLOB * BLK
    rows_total = groups * local_len
    score_scale = DH ** (-0.5)
    per_group = blocks_here * H * R
    capacity = -(-per_group // seq_count)
    slot_total = seq_count * groups * capacity
    pad_rows = ((0, 0), (0, local_len - global_width), (0, 0))
    owners = (rand_blocks // blocks_here).reshape(groups, per_group)
    owner_hits = (owners[:, :, None] == jnp.arange(seq_count)[None, None, :]).astype(jnp.int32)
    ranks = jnp.sum((jnp.cumsum(owner_hits, axis=1) - 1) * owner_hits, axis=2)
    slot_index = jnp.arange(groups)[:, None] * capacity + ranks
    request_code = (
        (jnp.arange(groups)[:, None, None, None] * blocks_here + rand_blocks % blocks_here) * H
        + jnp.arange(H)[None, None, :, None]
    ).reshape(groups, per_group)
    requests = (
        jnp.zeros((seq_count, groups * capacity), jnp.int32)
        .at[owners, slot_index]
        .set(request_code)
    )
    landing = (owners * (groups * capacity) + slot_index).reshape(-1)
    seg_shifted = segments + 1
    seg_extended = padded(seg_shifted, (("seq", 1),), BLK)
    positions = own_index * local_len - BLK + jnp.arange(local_len + 2 * BLK)
    pos_window = window_view(positions.reshape(blocks_here + 2, BLK), 0, blocks_here)
    seg_window = window_view(seg_extended.reshape(groups, blocks_here + 2, BLK), 1, blocks_here)
    seg_query = seg_shifted.reshape(groups, blocks_here, BLK)
    inside = (pos_window >= global_width) & (pos_window < length)
    window_allowed = inside[None, :, None, :] & (
        seg_window[:, :, None, :] == seg_query[:, :, :, None]
    )
    allowed = jnp.concatenate(
        [
            jnp.ones((groups, blocks_here, BLK, global_width), jnp.bool_),
            window_allowed,
            jnp.ones((groups, blocks_here, BLK, R * BLK), jnp.bool_),
        ],
        axis=-1,
    )
    global_rows = ((own_index == 0) & (jnp.arange(local_len) < global_width))[None, :, None]

    def head_view(queries, extended, shared, drawn, head_index):
        q_head = jnp.take(queries.reshape(groups, blocks_here, BLK, H, DH), head_index, axis=3)
        beside_all = jnp.take(
            extended.reshape(groups, blocks_here + 2, BLK, 2, H, DH), head_index, axis=4
        )
        window = window_view(beside_all, 1, blocks_here)
        common = jnp.take(
            shared[:, :, D:].reshape(groups, global_width, 2, H, DH), head_index, axis=3
        )
        common = jnp.broadcast_to(common[:, None], (groups, blocks_here, global_width, 2, DH))
        picked = jnp.take(drawn, head_index, axis=2).reshape(groups, blocks_here, R * BLK, 2, DH)
        key_rows = jnp.concatenate([common, window, picked], axis=2)
        return (q_head, key_rows[:, :, :, 0], key_rows[:, :, :, 1])

    def head_forward(queries, extended, shared, drawn, head_index):
        q_head, key_head, value_head = head_view(queries, extended, shared, drawn, head_index)
        scores = (
            jnp.einsum("sbqd,sbkd->sbqk", q_head, key_head, preferred_element_type=jnp.float32)
            * score_scale
        )
        probs = jax.nn.softmax(jnp.where(allowed, scores, masked_score), axis=-1)
        return jnp.einsum(
            "sbqk,sbkd->sbqd",
            probs.astype(jnp.bfloat16),
            value_head,
            preferred_element_type=jnp.float32,
        )

    def head_backward(queries, extended, shared, drawn, generic_grad, head_index):
        q_head, key_head, value_head = head_view(queries, extended, shared, drawn, head_index)
        grad_head = jnp.take(
            generic_grad.reshape(groups, blocks_here, BLK, H, DH), head_index, axis=3
        )
        scores = (
            jnp.einsum("sbqd,sbkd->sbqk", q_head, key_head, preferred_element_type=jnp.float32)
            * score_scale
        )
        probs = jax.nn.softmax(jnp.where(allowed, scores, masked_score), axis=-1)
        prob_grads = jnp.einsum(
            "sbqd,sbkd->sbqk", grad_head, value_head, preferred_element_type=jnp.float32
        )
        score_grads = (
            probs * (prob_grads - jnp.sum(probs * prob_grads, axis=-1, keepdims=True)) * score_scale
        ).astype(jnp.bfloat16)
        query_grad = jnp.einsum(
            "sbqk,sbkd->sbqd", score_grads, key_head, preferred_element_type=jnp.float32
        )
        key_grad = jnp.einsum(
            "sbqk,sbqd->sbkd", score_grads, q_head, preferred_element_type=jnp.float32
        )
        value_grad = jnp.einsum(
            "sbqk,sbqd->sbkd",
            probs.astype(jnp.bfloat16),
            grad_head,
            preferred_element_type=jnp.float32,
        )
        pair_grad = jnp.stack([key_grad, value_grad], axis=3)
        to_shared = jnp.sum(pair_grad[:, :, :global_width], axis=1)
        window_part = pair_grad[:, :, global_width : global_width + 3 * BLK].reshape(
            groups, blocks_here, 3, BLK, 2, DH
        )
        to_extended = sum(
            (
                jnp.pad(
                    window_part[:, :, offset],
                    ((0, 0), (offset, 2 - offset), (0, 0), (0, 0), (0, 0)),
                )
                for offset in range(3)
            )
        )
        to_drawn = pair_grad[:, :, global_width + 3 * BLK :].reshape(
            groups, blocks_here, R, BLK, 2, DH
        )
        return (query_grad, to_shared, to_extended, to_drawn)

    resid = layer_input.astype(jnp.float32).reshape(rows_total, D)
    inputs_low = layer_input
    saved_layers = []
    kept_weights = []
    for layer_index in range(L):
        weights_now = fetch_layer(layer_index, w_qkv, w_out, w_up, w_down, gains, biases, up_bias)
        (
            forward_mat_qkv,
            forward_mat_out,
            forward_mat_up,
            forward_mat_down,
            forward_gain_rows,
            forward_bias_rows,
            forward_up_shift,
        ) = weights_now
        forward_gain_rows = forward_gain_rows.astype(jnp.float32)
        forward_bias_rows = forward_bias_rows.astype(jnp.float32)
        projected = jnp.dot(
            inputs_low.reshape(rows_total, D), forward_mat_qkv, preferred_element_type=jnp.float32
        )
        forward_queries = (
            (projected[:, :D] + forward_bias_rows[0])
            .astype(jnp.bfloat16)
            .reshape(groups, local_len, D)
        )
        forward_keys_values = (
            jnp.concatenate(
                [projected[:, D : 2 * D], projected[:, 2 * D :] + forward_bias_rows[1]], axis=-1
            )
            .astype(jnp.bfloat16)
            .reshape(groups, local_len, 2 * D)
        )
        forward_extended = padded(forward_keys_values, (("seq", 1),), BLK)
        forward_shared = from_root(
            jnp.concatenate(
                [forward_queries[:, :global_width], forward_keys_values[:, :global_width]], axis=-1
            ),
            "seq",
            0,
        )
        tile_table = forward_keys_values.reshape(groups, blocks_here, BLK, 2, H, DH)
        codes = lax.all_to_all(requests, "seq", split_axis=0, concat_axis=0, tiled=True)
        group_ids, block_ids, head_ids = decode(codes, blocks_here)
        serve_picked = tile_table[group_ids, block_ids, :, :, head_ids, :]
        serve_picked = serve_picked.reshape(codes.shape[0], codes.shape[1], BLK, 2 * DH)
        arrived = lax.all_to_all(serve_picked, "seq", split_axis=0, concat_axis=0, tiled=True)
        placed = arrived.reshape(slot_total, BLK, 2 * DH)[landing]
        forward_drawn = placed.reshape(groups, blocks_here, H, R, BLK, 2 * DH)
        generic = lax.map(
            lambda head_index: head_forward(
                forward_queries, forward_extended, forward_shared, forward_drawn, head_index
            ),
            jnp.arange(H),
        )
        generic = jnp.moveaxis(generic, 0, 3).reshape(groups, local_len, D)
        forward_shared_q = forward_shared[:, :, :D].reshape(groups, global_width, H, DH)
        forward_local_k = forward_keys_values[:, :, :D].reshape(groups, local_len, H, DH)
        forward_local_v = forward_keys_values[:, :, D:].reshape(groups, local_len, H, DH)
        forward_global_scores = (
            jnp.einsum(
                "sqhd,skhd->shqk",
                forward_shared_q,
                forward_local_k,
                preferred_element_type=jnp.float32,
            )
            * score_scale
        )
        forward_row_max = jnp.max(forward_global_scores, axis=-1)
        forward_exp_total = jnp.sum(
            jnp.exp(forward_global_scores - forward_row_max[..., None]), axis=-1
        )
        forward_row_max, forward_exp_total = combined_all(
            (forward_row_max, forward_exp_total), "seq", combine_stats
        )
        forward_global_probs = (
            jnp.exp(forward_global_scores - forward_row_max[..., None])
            / forward_exp_total[..., None]
        ).astype(jnp.bfloat16)
        partial_out = jnp.einsum(
            "shqk,skhd->sqhd",
            forward_global_probs,
            forward_local_v,
            preferred_element_type=jnp.float32,
        ).reshape(groups, global_width, D)
        global_out = lax.psum(partial_out, "seq")
        attended = jnp.where(global_rows, jnp.pad(global_out, pad_rows), generic)
        forward_attended_low = attended.astype(jnp.bfloat16).reshape(rows_total, D)
        resid_one = (
            resid
            + jnp.dot(forward_attended_low, forward_mat_out, preferred_element_type=jnp.float32)
            + forward_bias_rows[2]
        )
        middle, forward_normed_one, forward_inv_one = norm_rows(
            resid_one, forward_gain_rows[0], forward_bias_rows[3]
        )
        forward_middle_low = middle.astype(jnp.bfloat16)
        forward_hidden = jnp.dot(
            forward_middle_low, forward_mat_up, preferred_element_type=jnp.float32
        ) + forward_up_shift.astype(jnp.float32)
        forward_active_low = jax.nn.gelu(forward_hidden, approximate=False).astype(jnp.bfloat16)
        resid_two = (
            middle
            + jnp.dot(forward_active_low, forward_mat_down, preferred_element_type=jnp.float32)
            + forward_bias_rows[4]
        )
        result, forward_normed_two, forward_inv_two = norm_rows(
            resid_two, forward_gain_rows[1], forward_bias_rows[5]
        )
        forward_saved = (
            inputs_low,
            forward_queries,
            forward_keys_values,
            forward_extended,
            forward_shared,
            forward_drawn,
            codes,
            forward_row_max,
            forward_exp_total,
            forward_attended_low,
            forward_normed_one,
            forward_inv_one,
            forward_middle_low,
            forward_hidden,
            forward_active_low,
            forward_normed_two,
            forward_inv_two,
        )
        resid = result
        saved_layers.append(forward_saved)
        kept_weights.append(weights_now)
        inputs_low = resid.astype(jnp.bfloat16).reshape(groups, local_len, D)
    grad_rows = d_out.astype(jnp.float32).reshape(rows_total, D)
    owned_layers = []
    for layer_index in reversed(range(L)):
        weights_now = fetch_layer(layer_index, w_qkv, w_out, w_up, w_down, gains, biases, up_bias)
        (
            backward_inputs_low,
            backward_queries,
            keys_values,
            backward_extended,
            backward_shared,
            backward_drawn,
            backward_served,
            row_max,
            exp_total,
            attended_low,
            normed_one,
            inv_one,
            middle_low,
            hidden,
            active_low,
            normed_two,
            inv_two,
        ) = saved_layers[layer_index]
        mat_qkv, mat_out, mat_up, mat_down, gain_rows, bias_rows, up_shift = weights_now
        gain_rows = gain_rows.astype(jnp.float32)
        gain_two_grad = jnp.sum(grad_rows * normed_two, axis=0)
        shift_two_grad = jnp.sum(grad_rows, axis=0)
        grad_two = norm_back(grad_rows, normed_two, inv_two, gain_rows[1])
        down_shift_grad = jnp.sum(grad_two, axis=0)
        grad_two_low = grad_two.astype(jnp.bfloat16)
        down_grad = jnp.einsum(
            "mf,md->fd", active_low, grad_two_low, preferred_element_type=jnp.float32
        )
        active_grad = jnp.einsum(
            "md,fd->mf", grad_two_low, mat_down, preferred_element_type=jnp.float32
        )
        hidden_grad = jax.vjp(partial(jax.nn.gelu, approximate=False), hidden)[1](active_grad)[0]
        up_shift_grad = jnp.sum(hidden_grad, axis=0)
        hidden_grad_low = hidden_grad.astype(jnp.bfloat16)
        up_grad = jnp.einsum(
            "md,mf->df", middle_low, hidden_grad_low, preferred_element_type=jnp.float32
        )
        middle_grad = grad_two + jnp.einsum(
            "mf,df->md", hidden_grad_low, mat_up, preferred_element_type=jnp.float32
        )
        gain_one_grad = jnp.sum(middle_grad * normed_one, axis=0)
        shift_one_grad = jnp.sum(middle_grad, axis=0)
        grad_one = norm_back(middle_grad, normed_one, inv_one, gain_rows[0])
        out_shift_grad = jnp.sum(grad_one, axis=0)
        grad_one_low = grad_one.astype(jnp.bfloat16)
        out_grad = jnp.einsum(
            "md,me->de", attended_low, grad_one_low, preferred_element_type=jnp.float32
        )
        attended_grad = (
            jnp.einsum("me,de->md", grad_one_low, mat_out, preferred_element_type=jnp.float32)
            .astype(jnp.bfloat16)
            .reshape(groups, local_len, D)
        )
        cotangent = from_root(attended_grad[:, :global_width], "seq", 0)
        backward_generic_grad = jnp.where(global_rows, jnp.zeros((), jnp.bfloat16), attended_grad)
        query_grads, backward_to_shared, backward_to_extended, backward_to_drawn = lax.map(
            lambda head_index: head_backward(
                backward_queries,
                backward_extended,
                backward_shared,
                backward_drawn,
                backward_generic_grad,
                head_index,
            ),
            jnp.arange(H),
        )
        query_grads = jnp.moveaxis(query_grads, 0, 3).reshape(groups, local_len, D)
        backward_to_shared = jnp.moveaxis(backward_to_shared, 0, 3).reshape(
            groups, global_width, 2 * D
        )
        window_grads = jnp.moveaxis(backward_to_extended, 0, 4).reshape(
            groups, local_len + 2 * BLK, 2 * D
        )
        backward_drawn_grads = jnp.moveaxis(backward_to_drawn, 0, 2)
        shared_q = backward_shared[:, :, :D].reshape(groups, global_width, H, DH)
        local_k = keys_values[:, :, :D].reshape(groups, local_len, H, DH)
        local_v = keys_values[:, :, D:].reshape(groups, local_len, H, DH)
        cot_heads = cotangent.reshape(groups, global_width, H, DH)
        global_scores = (
            jnp.einsum("sqhd,skhd->shqk", shared_q, local_k, preferred_element_type=jnp.float32)
            * score_scale
        )
        global_probs = jnp.exp(global_scores - row_max[..., None]) / exp_total[..., None]
        global_prob_grads = jnp.einsum(
            "sqhd,skhd->shqk", cot_heads, local_v, preferred_element_type=jnp.float32
        )
        row_delta = lax.psum(jnp.sum(global_probs * global_prob_grads, axis=-1), "seq")
        global_score_grads = (
            global_probs * (global_prob_grads - row_delta[..., None]) * score_scale
        ).astype(jnp.bfloat16)
        query_part = jnp.einsum(
            "shqk,skhd->sqhd", global_score_grads, local_k, preferred_element_type=jnp.float32
        ).reshape(groups, global_width, D)
        key_from_global = jnp.einsum(
            "shqk,sqhd->skhd", global_score_grads, shared_q, preferred_element_type=jnp.float32
        ).reshape(groups, local_len, D)
        value_from_global = jnp.einsum(
            "shqk,sqhd->skhd",
            global_probs.astype(jnp.bfloat16),
            cot_heads,
            preferred_element_type=jnp.float32,
        ).reshape(groups, local_len, D)
        shared_q_grad, shared_kv_grad = lax.psum((query_part, backward_to_shared), "seq")
        rims = jnp.concatenate([window_grads[:, :BLK], window_grads[:, local_len + BLK :]], axis=1)
        returned = padded(rims, (("seq", 1),), BLK)
        from_sides = jnp.pad(returned[:, :BLK], ((0, 0), (0, local_len - BLK), (0, 0))) + jnp.pad(
            returned[:, 3 * BLK :], ((0, 0), (local_len - BLK, 0), (0, 0))
        )
        shared_kv_rows = jnp.where(global_rows, jnp.pad(shared_kv_grad, pad_rows), 0.0)
        outgoing = (
            jnp.zeros((slot_total, BLK, 2 * DH), jnp.float32)
            .at[landing]
            .set(backward_drawn_grads.reshape(-1, BLK, 2 * DH))
        )
        incoming = lax.all_to_all(
            outgoing.reshape(seq_count, groups * capacity, BLK, 2 * DH),
            "seq",
            split_axis=0,
            concat_axis=0,
            tiled=True,
        )
        return_group_ids, return_block_ids, return_head_ids = decode(backward_served, blocks_here)
        summed = (
            jnp.zeros((groups, blocks_here, BLK, 2, H, DH), jnp.float32)
            .at[return_group_ids, return_block_ids, :, :, return_head_ids, :]
            .add(incoming.reshape(-1, BLK, 2, DH))
        )
        grad_kv_local = (
            window_grads[:, BLK : BLK + local_len]
            + from_sides
            + summed.reshape(groups, local_len, 2 * D)
            + jnp.concatenate([key_from_global, value_from_global], axis=-1)
            + shared_kv_rows
        )
        grad_queries = query_grads + jnp.where(global_rows, jnp.pad(shared_q_grad, pad_rows), 0.0)
        proj_grad = jnp.concatenate([grad_queries, grad_kv_local], axis=-1).reshape(
            rows_total, 3 * D
        )
        bias_grads = jnp.stack(
            [
                jnp.sum(proj_grad[:, :D], axis=0),
                jnp.sum(proj_grad[:, 2 * D :], axis=0),
                out_shift_grad,
                shift_one_grad,
                down_shift_grad,
                shift_two_grad,
            ]
        )
        proj_grad_low = proj_grad.astype(jnp.bfloat16)
        qkv_grad = jnp.einsum(
            "md,me->de",
            backward_inputs_low.reshape(rows_total, D),
            proj_grad_low,
            preferred_element_type=jnp.float32,
        )
        input_grad = grad_one + jnp.einsum(
            "me,de->md", proj_grad_low, mat_qkv, preferred_element_type=jnp.float32
        )
        owned = (
            lax.psum_scatter(qkv_grad, ("seq", "batch"), scatter_dimension=0, tiled=True),
            lax.psum_scatter(out_grad, ("seq", "batch"), scatter_dimension=0, tiled=True),
            lax.psum_scatter(up_grad, ("seq", "batch"), scatter_dimension=0, tiled=True),
            lax.psum_scatter(down_grad, ("seq", "batch"), scatter_dimension=0, tiled=True),
            lax.psum_scatter(
                jnp.stack([gain_one_grad, gain_two_grad]),
                ("seq", "batch"),
                scatter_dimension=1,
                tiled=True,
            ),
            lax.psum_scatter(bias_grads, ("seq", "batch"), scatter_dimension=1, tiled=True),
            lax.psum_scatter(up_shift_grad, ("seq", "batch"), scatter_dimension=0, tiled=True),
        )
        grad_rows, owned = (input_grad, owned)
        owned_layers.insert(0, owned)
    stacked = tuple((jnp.stack([owned[member] for owned in owned_layers]) for member in range(7)))
    return (
        inputs_low,
        grad_rows.reshape(groups, local_len, D),
        stacked[0],
        stacked[1],
        stacked[2],
        stacked[3],
        stacked[4],
        stacked[5],
        stacked[6],
    )


def solution(mesh):
    placed = (
        P("batch", "seq", None),
        P("batch", "seq"),
        P("batch", "seq", None, None),
        P(None, ("seq", "batch"), None),
        P(None, ("seq", "batch"), None),
        P(None, ("seq", "batch"), None),
        P(None, ("seq", "batch"), None),
        P(None, None, ("seq", "batch")),
        P(None, None, ("seq", "batch")),
        P(None, ("seq", "batch")),
        P("batch", "seq", None),
    )
    return jax.shard_map(
        on_device,
        mesh=mesh,
        in_specs=placed,
        out_specs=(
            P("batch", "seq", None),
            P("batch", "seq", None),
            P(None, ("seq", "batch"), None),
            P(None, ("seq", "batch"), None),
            P(None, ("seq", "batch"), None),
            P(None, ("seq", "batch"), None),
            P(None, None, ("seq", "batch")),
            P(None, None, ("seq", "batch")),
            P(None, ("seq", "batch")),
        ),
        check_vma=False,
    )
```

profile of v0, /device:TPU:0, one launch (start us, length us, event | category | flops | bytes accessed | tf_op | source)
XLA Modules:
  0.0 3416.3 jit_solution(12134670326372136293)
XLA Ops:
  10.5 74.1 %all-gather.1 = bf16[1,6,768]{1,0,2:T(2,128)(2,1)S(1)} all-gather(bf16[1,6,24]{1,0,2:T(2,128)(2,1)S(1)} %copy.453), channel_id=3, replica_groups=mesh['seq'=8,'batch'=4] {'seq','batch'}, dimensions={2}, use_global_device_ids=true | all-gather | bytes 9504 | tf_op jit(solution)/shard_map/all_gather | solution.py:90
  111.3 22.2 scatter_fusion
  152.9 68.5 %all-gather.5 = bf16[1,2,768]{1,0,2:T(2,128)(2,1)S(1)} all-gather(bf16[1,2,24]{1,0,2:T(2,128)(2,1)} %copy.454), channel_id=7, replica_groups=mesh['seq'=8,'batch'=4] {'seq','batch'}, dimensions={2}, use_global_device_ids=true | all-gather | bytes 3168 | tf_op jit(solution)/shard_map/all_gather | solution.py:89
  227.9 70.0 %all-gather.10 = bf16[1,6,768]{1,0,2:T(2,128)(2,1)S(1)} all-gather(bf16[1,6,24]{1,0,2:T(2,128)(2,1)} %copy.455), channel_id=12, replica_groups=mesh['seq'=8,'batch'=4] {'seq','batch'}, dimensions={2}, use_global_device_ids=true | all-gather | bytes 9504 | tf_op jit(solution)/shard_map/all_gather | solution.py:90
  316.3 41.8 %all-reduce.28 = (bf16[3072]{0:T(1024)(128)(2,1)}, bf16[3072]{0:T(1024)(128)(2,1)}) all-reduce(bf16[3072]{0:T(1024)(128)(2,1)} %dynamic-update-slice.5, bf16[3072]{0:T(1024)(128)(2,1)} %dynamic-update-slice.4), channel_id=18, replica_groups=mesh['seq'=8,'batch'=4] {'seq','batch'}, use_global_device_ids=true, to_apply=%add.18 | all-reduce | flops 6144 | bytes 24576
  390.0 14.0 copy.352
  426.6 27.4 all-gather.19
  467.3 28.8 all-reduce.52
  504.1 190.6 %while.95 = (s32[]{:T(128)}, bf16[12,1,4,64,64]{4,3,2,1,0:T(8,128)(2,1)}, pred[1,4,64,512]{3,2,1,0:T(32,128)(4,1)}, bf16[256,768]{0,1:T(8,128)(2,1)S(1)}, s32[12...) while((s32[]{:T(128)}, ...), condition=%wide.region_13.18_spmd, body=%wide.region_10.17_spmd.sunk | while | flops 51709192 | bytes 10391245 | solution.py:273
  725.6 68.3 %all-gather.14 = bf16[1,2,768]{1,0,2:T(2,128)(2,1)S(1)} all-gather(bf16[1,2,24]{1,0,2:T(2,128)(2,1)S(1)} %copy.456), channel_id=16, replica_groups=mesh['seq'=8,'batch'=4] {'seq','batch'}, dimensions={2}, use_global_device_ids=true | all-gather | bytes 3168 | tf_op jit(solution)/shard_map/all_gather | solution.py:89
  823.5 14.1 copy.367
  858.6 34.8 %all-gather.21 = f32[8,12,128]{2,1,0:T(8,128)S(1)} all-gather(f32[1,12,128]{2,1,0:T(8,128)S(1)} %bitcast.864), channel_id=14, replica_groups=mesh['seq'=8,'batch'=4] {'seq'}, dimensions={0}, use_global_device_ids=true | all-gather | bytes 55296 | tf_op jit(solution)/shard_map/all_gather | solution.py:40
  907.7 32.0 all-reduce.53
  947.8 190.8 %while.97 = (s32[]{:T(128)}, bf16[12,1,4,64,64]{4,3,2,1,0:T(8,128)(2,1)}, pred[1,4,64,512]{3,2,1,0:T(32,128)(4,1)}, bf16[256,768]{0,1:T(8,128)(2,1)S(1)}, s32[12...) while((s32[]{:T(128)}, ...), condition=%wide.region_27.32_spmd, body=%wide.region_24.31_spmd.sunk | while | flops 51709192 | bytes 10391245 | solution.py:273
  1184.4 351.1 %while.98 = (s32[]{:T(128)}, f32[12,1,4,64,64]{4,3,2,1,0:T(8,128)}, f32[12,1,128,2,64]{2,4,0,3,1:T(8,128)}, f32[12,1,6,64,2,64]{5,3,4,2,1,0:T(8,128)}, f32[12,1,...) while((s32[]{:T(128)}, f32[12,1,4,64,64]{4,3,2,1,0:T(8,128)}, ...), condition=%wide.region_41.46_spmd, body=%wide.region_36.45_spmd.sunk | while | flops 87148552 | bytes 34387376 | solution.py:416
  1535.5 17.1 copy.380
  1565.2 21.7 scatter_fusion.1
  1607.4 54.5 %all-reduce.43.cloned.1.call-done = bf16[128,12,64]{0,2,1:T(8,128)(2,1)} async-done(((bf16[128,12,64]{0,2,1:T(8,128)(2,1)}), bf16[128,12,64]{0,2,1:T(8,128)(2,1)}) %all-reduce.43.cloned.1.call-update) | async-done | bytes 196624 | tf_op jit(solution)/shard_map/psum | solution.py:36
  1695.7 42.2 %all-reduce.51.cloned.1.call-done = (f32[1,128,1536]{2,1,0:T(8,128)}, f32[1,128,768]{1,2,0:T(8,128)}) async-done(((f32[1,128,1536]{2,1,0:T(8,128)}, f32[1,128,768]{1,2,0:T(8,128)}), (f32[1,128,1536]{2,1,0:T(8,128)}, f32[1,128,768]{1,2,0:T(8,128)})) %all-reduce.51.cloned.1.call-update) | async-done | bytes 1179664 | tf_op jit(solution)/shard_map/psum | solution.py:463
  1759.6 22.5 scatter_fusion.2
  1821.2 352.0 %while.99 = (s32[]{:T(128)}, f32[12,1,4,64,64]{4,3,2,1,0:T(8,128)}, f32[12,1,128,2,64]{2,4,0,3,1:T(8,128)}, f32[12,1,6,64,2,64]{5,3,4,2,1,0:T(8,128)}, f32[12,1,...) while((s32[]{:T(128)}, f32[12,1,4,64,64]{4,3,2,1,0:T(8,128)}, ...), condition=%wide.region_58.63_spmd, body=%wide.region_53.62_spmd.sunk | while | flops 87148552 | bytes 32814492 | solution.py:416
  2198.3 17.1 copy.396
  2228.1 21.8 scatter_fusion.3
  2331.5 22.6 scatter_fusion.4
  2415.7 47.5 %reduce-scatter.17.cloned.1.call-done = f32[24,768]{1,0:T(8,128)} async-done(((f32[768,768]{1,0:T(8,128)}), f32[24,768]{1,0:T(8,128)}) %reduce-scatter.17.cloned.1.call-update) | async-done | bytes 73744 | tf_op jit(solution)/shard_map/reduce_scatter | solution.py:521
  2468.7 123.4 %all-reduce.47.cloned.1.call-done = (f32[2,768]{1,0:T(2,128)}, f32[2,768]{1,0:T(2,128)}, f32[6,768]{1,0:T(8,128)}, f32[6,768]{1,0:T(8,128)}, f32[3072]{0:T(1024)}, /*index=5*/f32[3072]{0:T(1024)}) async-done(((f32[2,768]{1,0:T(2,128)}, f32[2,768]{1,0:T(2,128)}, f32[6,768]{1,0:T(8,128)}, f32[6,768]{1,0:T(8,128)}, f32[3072]{0:T(1024)}, /*index=5*/f32[3072]{0:T(1024)}), (f32[2,768]{1,0:T(2,128)}, ...) | async-done | bytes 73744
  2598.4 119.6 %reduce-scatter.31.cloned.1.call-done = f32[24,2304]{1,0:T(8,128)} async-done(((f32[768,2304]{1,0:T(8,128)}), f32[24,2304]{1,0:T(8,128)}) %reduce-scatter.31.cloned.1.call-update) | async-done | bytes 221200
  2719.6 140.2 %reduce-scatter.27.cloned.1.call-done = f32[96,768]{1,0:T(8,128)} async-done(((f32[3072,768]{1,0:T(8,128)}), f32[96,768]{1,0:T(8,128)}) %reduce-scatter.27.cloned.1.call-update) | async-done | bytes 294928 | tf_op jit(solution)/shard_map/reduce_scatter | solution.py:523
  2859.8 140.3 %reduce-scatter.25.cloned.1.call-done = f32[96,768]{1,0:T(8,128)} async-done(((f32[3072,768]{1,0:T(8,128)}), f32[96,768]{1,0:T(8,128)}) %reduce-scatter.25.cloned.1.call-update) | async-done | bytes 294928 | tf_op jit(solution)/shard_map/reduce_scatter | solution.py:523
  3002.0 139.7 %reduce-scatter.23.cloned.1.call-done = f32[24,3072]{1,0:T(8,128)} async-done(((f32[768,3072]{1,0:T(8,128)}), f32[24,3072]{1,0:T(8,128)}) %reduce-scatter.23.cloned.1.call-update) | async-done | bytes 294928 | tf_op jit(solution)/shard_map/reduce_scatter | solution.py:522
  3141.7 140.5 %reduce-scatter.21.cloned.1.call-done = f32[24,3072]{1,0:T(8,128)} async-done(((f32[768,3072]{1,0:T(8,128)}), f32[24,3072]{1,0:T(8,128)}) %reduce-scatter.21.cloned.1.call-update) | async-done | bytes 294928 | tf_op jit(solution)/shard_map/reduce_scatter | solution.py:522
  3284.1 122.9 %reduce-scatter.29.cloned.1.call-done = f32[24,2304]{1,0:T(8,128)} async-done(((f32[768,2304]{1,0:T(8,128)}), f32[24,2304]{1,0:T(8,128)}) %reduce-scatter.29.cloned.1.call-update) | async-done | bytes 221200
  (2219 shorter events, 1608.6 us)
Async XLA Ops:
  7.2 91.2 %all-gather.31.cloned.1.call-start = ((), (), s32[]{:S(2)}) async-start(), calls=%async_computation.23 | async-start | bytes 3649536 | tf_op jit(solution)/shard_map/all_gather | solution.py:85
  8.9 414.5 %all-reduce.39.cloned.1.call-start = ((), (), s32[]{:S(2)}) async-start(), calls=%async_computation.13 | async-start | bytes 1179648 | tf_op jit(solution)/shard_map/psum | solution.py:36
  102.6 595.6 %all-gather.33.cloned.1.call-start = ((), (), s32[]{:S(2)}) async-start(), calls=%async_computation.24 | async-start | bytes 1216512 | tf_op jit(solution)/shard_map/all_gather | solution.py:86
  104.2 596.4 %all-gather.35.cloned.1.call-start = ((), (), s32[]{:S(2)}) async-start(), calls=%async_computation.25 | async-start | bytes 4866048 | tf_op jit(solution)/shard_map/all_gather | solution.py:87
  106.0 606.4 %all-gather.37.cloned.1.call-start = ((), (), s32[]{:S(2)}) async-start(), calls=%async_computation.26 | async-start | bytes 4866048 | tf_op jit(solution)/shard_map/all_gather | solution.py:88
  133.5 232.0 %all-to-all-start = ((s32[8,1,18]{2,1,0:T(1,128)}), s32[8,1,18]{2,1,0:T(1,128)S(1)}, u32[]{:S(2)}, u32[]{:S(2)}) async-start(s32[8,1,18]{2,1,0:T(1,128)} %bitcast.108), calls=%async_computation | async-start | bytes 8192 | tf_op jit(solution)/shard_map/all_to_all | solution.py:266
  136.8 580.2 %all-gather.39.cloned.1.call-start = ((), (), s32[]{:S(2)}) async-start(), calls=%async_computation.27 | async-start | bytes 3649536 | tf_op jit(solution)/shard_map/all_gather | solution.py:85
  138.8 223.6 %collective-permute-start = (s32[1,64]{1,0:T(1,128)}, s32[1,64]{1,0:T(1,128)}, u32[]{:S(2)}, u32[]{:S(2)}) collective-permute-start(s32[1,64]{1,0:T(1,128)} %get-tuple-element.1191), channel_id=1, source_target_pairs={{0,4},{4,8},{8,12},{12,16},{16,20},{20,24},{24,28},{1,5},{5,9},{9,... | collective-permute-start | bytes 776 | tf_op jit(solution)/shard_map/ppermute | solution.py:28
  141.6 220.8 %collective-permute-start.1 = (s32[1,64]{1,0:T(1,128)}, s32[1,64]{1,0:T(1,128)}, u32[]{:S(2)}, u32[]{:S(2)}) collective-permute-start(s32[1,64]{1,0:T(1,128)} %get-tuple-element.1192), channel_id=1, source_target_pairs={{4,0},{8,4},{12,8},{16,12},{20,16},{24,20},{28,24},{5,1},{9,5},{13... | collective-permute-start | bytes 776 | tf_op jit(solution)/shard_map/ppermute | solution.py:29
  412.6 83.5 %all-to-all-start.1 = ((bf16[8,18,64,128]{3,2,1,0:T(8,128)(2,1)}), bf16[8,18,64,128]{3,2,1,0:T(8,128)(2,1)}, u32[]{:S(2)}, u32[]{:S(2)}) async-start(bf16[8,18,64,128]{3,2,1,0:T(8,128)(2,1)} %reshape.1400), calls=%async_computation.1 | async-start | bytes 4718592 | tf_op jit(solution)/shard_map/all_to_all | solution.py:270
  421.1 434.2 %all-reduce.41.cloned.1.call-start = ((), (), s32[]{:S(2)}) async-start(), calls=%async_computation.14 | async-start | bytes 1179648 | tf_op jit(solution)/shard_map/psum | solution.py:36
  722.2 420.5 %all-gather.41.cloned.1.call-start = ((), (), s32[]{:S(2)}) async-start(), calls=%async_computation.28 | async-start | bytes 1216512 | tf_op jit(solution)/shard_map/all_gather | solution.py:86
  722.9 422.0 %all-gather.43.cloned.1.call-start = ((), (), s32[]{:S(2)}) async-start(), calls=%async_computation.29 | async-start | bytes 4866048 | tf_op jit(solution)/shard_map/all_gather | solution.py:87
  723.6 433.6 %all-gather.45.cloned.1.call-start = ((), (), s32[]{:S(2)}) async-start(), calls=%async_computation.30 | async-start | bytes 4866048 | tf_op jit(solution)/shard_map/all_gather | solution.py:88
  846.2 93.5 %all-to-all-start.2 = ((bf16[8,18,64,128]{3,2,1,0:T(8,128)(2,1)}), bf16[8,18,64,128]{3,2,1,0:T(8,128)(2,1)}, u32[]{:S(2)}, u32[]{:S(2)}) async-start(bf16[8,18,64,128]{3,2,1,0:T(8,128)(2,1)} %reshape.1410), calls=%async_computation.2 | async-start | bytes 4718592 | tf_op jit(solution)/shard_map/all_to_all | solution.py:270
  1586.9 153.2 %all-to-all-start.3 = ((f32[8,18,64,128]{3,2,1,0:T(8,128)}), f32[8,18,64,128]{3,2,1,0:T(8,128)}, u32[]{:S(2)}, u32[]{:S(2)}) async-start(f32[8,18,64,128]{3,2,1,0:T(8,128)} %bitcast.779), calls=%async_computation.3 | async-start | bytes 9437184 | tf_op jit(solution)/shard_map/all_to_all | solution.py:475
  1592.6 145.3 %all-reduce.51.cloned.1.call-start = ((), (), s32[]{:S(2)}) async-start(), calls=%async_computation.35 | async-start | bytes 2359296 | tf_op jit(solution)/shard_map/psum | solution.py:463
  1680.1 495.4 %all-reduce.45.cloned.1.call-start = ((), (), s32[]{:S(2)}) async-start(), calls=%async_computation.16 | async-start | bytes 393216 | tf_op jit(solution)/shard_map/psum | solution.py:36
  1687.0 103.8 %collective-permute-start.6 = (f32[1,64,1536]{2,1,0:T(8,128)}, f32[1,64,1536]{2,1,0:T(8,128)S(1)}, u32[]{:S(2)}, u32[]{:S(2)}) collective-permute-start(f32[1,64,1536]{2,1,0:T(8,128)} %get-tuple-element.1159), channel_id=1, source_target_pairs={{0,4},{4,8},{8,12},{12,16},{16,20},{20,24},{24,28},{1,5},{5,9},{9,... | collective-permute-start | bytes 1179656 | tf_op jit(solution)/shard_map/ppermute | solution.py:28
  1689.1 101.8 %collective-permute-start.7 = (f32[1,64,1536]{2,1,0:T(8,128)}, f32[1,64,1536]{2,1,0:T(8,128)}, u32[]{:S(2)}, u32[]{:S(2)}) collective-permute-start(f32[1,64,1536]{2,1,0:T(8,128)} %get-tuple-element.1160), channel_id=1, source_target_pairs={{4,0},{8,4},{12,8},{16,12},{20,16},{24,20},{28,24},{5,1},{9,5},{13... | collective-permute-start | bytes 1179656 | tf_op jit(solution)/shard_map/ppermute | solution.py:29
  1809.8 489.4 %all-reduce.49.cloned.1.call-start = ((), (), s32[]{:S(2)}) async-start(), calls=%async_computation.34 | async-start | bytes 2359296 | tf_op jit(solution)/shard_map/psum | solution.py:463
  2195.3 220.4 %reduce-scatter.19.cloned.1.call-start = ((), (), s32[]{:S(2)}) async-start(), calls=%async_computation.18 | async-start | bytes 2433024 | tf_op jit(solution)/shard_map/reduce_scatter | solution.py:521
  2254.6 208.6 %reduce-scatter.17.cloned.1.call-start = ((), (), s32[]{:S(2)}) async-start(), calls=%async_computation.17 | async-start | bytes 2433024 | tf_op jit(solution)/shard_map/reduce_scatter | solution.py:521
  2282.5 309.6 %all-reduce.47.cloned.1.call-start = ((), (), s32[]{:S(2)}) async-start(), calls=%async_computation.33 | async-start | bytes 172032
  2284.6 78.0 %collective-permute-start.8 = (f32[1,64,1536]{2,1,0:T(8,128)}, f32[1,64,1536]{2,1,0:T(8,128)}, u32[]{:S(2)}, u32[]{:S(2)}) collective-permute-start(f32[1,64,1536]{2,1,0:T(8,128)} %get-tuple-element.1157), channel_id=1, source_target_pairs={{0,4},{4,8},{8,12},{12,16},{16,20},{20,24},{24,28},{1,5},{5,9},{9,... | collective-permute-start | bytes 1179656 | tf_op jit(solution)/shard_map/ppermute | solution.py:28
  2287.6 75.0 %collective-permute-start.9 = (f32[1,64,1536]{2,1,0:T(8,128)}, f32[1,64,1536]{2,1,0:T(8,128)}, u32[]{:S(2)}, u32[]{:S(2)}) collective-permute-start(f32[1,64,1536]{2,1,0:T(8,128)} %get-tuple-element.1158), channel_id=1, source_target_pairs={{4,0},{8,4},{12,8},{16,12},{20,16},{24,20},{28,24},{5,1},{9,5},{13... | collective-permute-start | bytes 1179656 | tf_op jit(solution)/shard_map/ppermute | solution.py:29
  2369.9 348.0 %reduce-scatter.31.cloned.1.call-start = ((), (), s32[]{:S(2)}) async-start(), calls=%async_computation.32 | async-start | bytes 7299072
  2374.9 484.9 %reduce-scatter.27.cloned.1.call-start = ((), (), s32[]{:S(2)}) async-start(), calls=%async_computation.22 | async-start | bytes 9732096 | tf_op jit(solution)/shard_map/reduce_scatter | solution.py:523
  2381.7 618.5 %reduce-scatter.25.cloned.1.call-start = ((), (), s32[]{:S(2)}) async-start(), calls=%async_computation.21 | async-start | bytes 9732096 | tf_op jit(solution)/shard_map/reduce_scatter | solution.py:523
  2388.5 753.3 %reduce-scatter.23.cloned.1.call-start = ((), (), s32[]{:S(2)}) async-start(), calls=%async_computation.20 | async-start | bytes 9732096 | tf_op jit(solution)/shard_map/reduce_scatter | solution.py:522
  2395.4 886.8 %reduce-scatter.21.cloned.1.call-start = ((), (), s32[]{:S(2)}) async-start(), calls=%async_computation.19 | async-start | bytes 9732096 | tf_op jit(solution)/shard_map/reduce_scatter | solution.py:522
  2402.3 1004.7 %reduce-scatter.29.cloned.1.call-start = ((), (), s32[]{:S(2)}) async-start(), calls=%async_computation.31 | async-start | bytes 7299072
  (313 other events, 4376.4 us)
Sparse Core Ops, SparseCore 0:
  11.4 63.7 all-gather.30
  102.8 50.9 all-reduce.38
  157.0 53.6 all-gather.32
  214.3 63.6 all-gather.34
  281.6 63.3 all-gather.36
  348.1 59.0 all-gather.38
  722.3 53.3 all-reduce.40
  778.5 53.7 all-gather.40
  835.1 67.8 all-gather.42
  905.7 62.5 all-gather.44
  1596.1 65.7 all-reduce.42
  1680.2 57.5 all-reduce.50
  1809.9 52.3 all-reduce.44
  2195.5 56.2 all-reduce.48
  2256.9 102.2 reduce-scatter.18
  2365.1 98.0 reduce-scatter.16
  2470.1 121.9 all-reduce.46
  2597.6 120.3 reduce-scatter.30
  2724.9 134.9 reduce-scatter.26
  2865.6 134.5 reduce-scatter.24
  3007.0 134.6 reduce-scatter.22
  3147.6 134.5 reduce-scatter.20
  3288.9 118.0 reduce-scatter.28
where the time goes:
time: 3440 us; the launch traced here: 3420 us
  local copies, waits for them, and re-layouts  1130 us (33%)
  waiting for transfers between devices  1080 us (31%)
  blocking collectives  489 us (14%)
  matrix products  359 us (10%)
  other arithmetic  191 us (6%)
  loops' own time  102 us (3%)
  starting transfers between devices  47.6 us (1%)
    unnamed x26, waiting for transfers between devices  368 us
    reduce_scatter x2, waiting for transfers between devices, on_device(): lax.psum_scatter(down_grad, ('seq', 'batch'), scatter_dimension=0, tiled=...  281 us
    reduce_scatter x2, waiting for transfers between devices, on_device(): lax.psum_scatter(up_grad, ('seq', 'batch'), scatter_dimension=0, tiled=True)  280 us
    reshape x48, local copies, waits for them, and re-layouts, head_view(): extended.reshape(groups, blocks_here + 2, BLK, 2, H, DH)  182 us
    all_gather x2, blocking collectives, fetch_layer(): lax.all_gather(biases[layer_index], ('seq', 'batch'), axis=1, tiled=True)  144 us
    all_gather x2, blocking collectives, fetch_layer(): lax.all_gather(gains[layer_index], ('seq', 'batch'), axis=1, tiled=True)  137 us
    another operation x48, local copies, waits for them, and re-layouts, head_view(): jnp.take(extended.reshape(groups, blocks_here + 2, BLK, 2, H, DH), head_i...  87.1 us
    all_gather x4, blocking collectives, combined_all(): everything = jax.tree.map(lambda part: lax.all_gather(part, axis), x)  80 us
  transfers between devices with their start and end apart: 38, of which 11 were waited for; matrix products, arithmetic and copies ran while one was open for 36% of the time, Pallas kernels for 0%

commit v1 on v0

v1 whole, which is shorter than its diff:
```python
import functools
import itertools
from functools import partial

import jax
import jax.numpy as jnp
from jax import lax
from jax.experimental import pallas as pl
from jax.experimental.pallas import tpu as pltpu
from jax.sharding import PartitionSpec as P

MESH = pl.DeviceIdType.MESH


def place():
    s = lax.axis_index("seq")
    return {"y": s // 4, "x": (s // 2) % 2, "c": s % 2, "z": lax.axis_index("batch")}


def device_of(p):
    return ((p["y"] * 2 + p["x"]) * 2 + p["c"], p["z"])


def moved(p, axis, d):
    p = dict(p)
    if d:
        p[axis] = p[axis] + d if axis == "z" else 1 - p[axis]
    return p


def holds(p, depth):
    return (p["z"] >= 0) & (p["z"] < depth)


def when(cond, action):
    if cond is None:
        action()
    else:
        pl.when(cond)(action)


def both(one, other):
    return other if one is None else one if other is None else one & other


def offsets(order, depth):
    return list(
        itertools.product(*[range(1 - depth, depth) if a == "z" else (0, 1) for a in order])
    )


def last_move(offset):
    return max([-1] + [i for i, d in enumerate(offset) if d])


def onward(order, offset):
    last = last_move(offset)
    moves = []
    if last >= 0 and order[last] == "z":
        moves.append(("on", "z", -1 if offset[last] > 0 else 1))
    for axis in order[last + 1 :]:
        moves += [("start", axis, d) for d in ((1, -1) if axis == "z" else (1,))]
    moves.append(("core", "c", 1))
    return moves


def greet(axes, depth, from_first=0):
    me = place()
    barrier = pltpu.get_barrier_semaphore()
    count = 0
    for axis in axes + ("c",):
        for d in (1, -1) if axis == "z" else (1,):
            peer = moved(me, axis, d)
            cond = holds(peer, depth) if axis == "z" else None
            when(
                cond,
                lambda peer=peer: pl.semaphore_signal(
                    barrier, inc=1, device_id=device_of(peer), device_id_type=MESH
                ),
            )
            count = count + (1 if cond is None else cond.astype(jnp.int32))
    if from_first:
        seq = lax.axis_index("seq")

        @pl.when(seq != 0)
        def _():
            pl.semaphore_signal(
                barrier, inc=1, device_id=(0, lax.axis_index("batch")), device_id_type=MESH
            )

        count = count + jnp.where(seq == 0, from_first, 0)
    pl.semaphore_wait(barrier, count)


class Gather:
    def __init__(self, source, target, number, order, depth, send, recv, send_at):
        self.source, self.target, self.number = source, target, number
        self.order, self.depth, self.send, self.recv = order, depth, send, recv
        self.send_at = send_at
        self.me = place()
        self.sent = []

    @staticmethod
    def sends(order, depth):
        return sum(len(onward(order, t)) for t in offsets(order, depth))

    def origin(self, offset):
        p = self.me
        for axis, d in zip(self.order, offset):
            p = moved(p, axis, d)
        cond = None
        if "z" in self.order and offset[self.order.index("z")]:
            cond = holds(p, self.depth)
        return p, cond

    def arrival(self, p):
        ref = self.target(p)
        return pltpu.make_async_remote_copy(
            src_ref=ref, dst_ref=ref, send_sem=self.send.at[self.send_at],
            recv_sem=self.recv.at[self.number(p)], device_id=device_of(self.me), device_id_type=MESH,
        )

    def handle(self, offset):
        p, cond = self.origin(offset)
        own = not any(offset)
        plans = []
        for kind, axis, d in onward(self.order, offset):
            peer = moved(self.me, axis, d)
            also = holds(peer, self.depth) if axis == "z" else None
            plans.append((peer, also, self.send_at))
            self.send_at += 1

        def act():
            if not own:
                self.arrival(p).wait_recv()
            for peer, also, slot in plans:
                copy = pltpu.make_async_remote_copy(
                    src_ref=self.source if own else self.target(p), dst_ref=self.target(p),
                    send_sem=self.send.at[slot], recv_sem=self.recv.at[self.number(p)],
                    device_id=device_of(peer), device_id_type=MESH,
                )
                when(also, copy.start)

        when(cond, act)
        for peer, also, slot in plans:
            self.sent.append((both(cond, also), slot))

    def events(self):
        marks = sorted(
            (t for t in offsets(self.order, self.depth) if any(t)),
            key=lambda t: (sum(abs(d) for d in t), t),
        )
        return [(sum(abs(d) for d in t), partial(self.handle, t)) for t in marks]

    def siblings(self):
        for t in offsets(self.order, self.depth):
            p, cond = self.origin(t)
            p = moved(p, "c", 1)
            when(cond, lambda p=p: self.arrival(p).wait_recv())

    def drain(self):
        for cond, slot in self.sent:
            copy = pltpu.make_async_remote_copy(
                src_ref=self.source, dst_ref=self.target(self.me), send_sem=self.send.at[slot],
                recv_sem=self.recv.at[self.number(self.me)], device_id=device_of(self.me), device_id_type=MESH,
            )
            when(cond, copy.wait_send)


def run_gathers(jobs):
    for job in jobs:
        job.handle((0,) * len(job.order))
    todo = []
    for i, job in enumerate(jobs):
        todo += [(when_, i, k, act) for k, (when_, act) in enumerate(job.events())]
    for _, _, _, act in sorted(todo, key=lambda e: e[:3]):
        act()
    for job in jobs:
        job.siblings()
    for job in jobs:
        job.drain()


class Reduce:
    def __init__(self, partial_of, inbox, number, order, depth, send, recv):
        self.partial_of, self.inbox, self.number = partial_of, inbox, number
        self.order, self.depth, self.send, self.recv = order, depth, send, recv
        self.me = place()
        self.edges = self.edge_table(order, depth)
        self.sent = []

    @staticmethod
    def edge_table(order, depth):
        table = {}
        for t in offsets(order, depth):
            for move in onward(order, t):
                table[(t, move)] = len(table)
        return table

    def owner(self, offset):
        p = self.me
        for axis, d in zip(self.order, offset):
            p = moved(p, axis, d)
        cond = None
        if "z" in self.order and offset[self.order.index("z")]:
            cond = holds(p, self.depth)
        return p, cond

    def copy(self, source, edge, slot, peer):
        return pltpu.make_async_remote_copy(
            src_ref=source, dst_ref=self.inbox.at[edge], send_sem=self.send.at[slot],
            recv_sem=self.recv.at[edge], device_id=device_of(peer), device_id_type=MESH,
        )

    def slots(self):
        return {t: i for i, t in enumerate(offsets(self.order, self.depth))}

    def start(self, offset):
        p, cond = self.owner(offset)
        q = moved(p, "c", 1)
        slot = self.slots()[offset]
        edge = self.edges[(offset, ("core", "c", 1))]
        when(cond, lambda: self.copy(self.partial_of(q), edge, slot, moved(self.me, "c", 1)).start())
        self.sent.append((cond, slot))

    def children(self, offset):
        found = []
        for kind, axis, d in onward(self.order, offset):
            cond = None
            if axis == "z":
                cond = holds(moved(self.me, "z", d), self.depth)
            found.append((self.edges[(offset, (kind, axis, d))], cond, kind))
        return found

    def upward(self, offset):
        k = last_move(offset)
        axis, d = self.order[k], offset[k]
        step = 1 if d > 0 else -1
        parent = list(offset)
        parent[k] = d - step if axis == "z" else 0
        if axis == "z" and parent[k]:
            kind, back = "on", -step
        else:
            kind, back = "start", -step if axis == "z" else 1
        edge = self.edges[(tuple(parent), (kind, axis, back))]
        return edge, moved(self.me, axis, step)

    def handle(self, offset, add, finish):
        p, cond = self.owner(offset)
        kids = self.children(offset)
        core = [e for e, c, kind in kids if kind == "core"][0]
        slot = len(self.slots()) + self.slots()[offset]

        def act():
            for edge, also, _ in kids:
                when(also, lambda edge=edge: self.copy(self.inbox.at[edge], edge, slot, self.me).wait_recv())
            if any(offset):
                add(self.partial_of(p), [(self.inbox.at[e], c) for e, c, _ in kids], self.inbox.at[core])
                edge, peer = self.upward(offset)
                self.copy(self.inbox.at[core], edge, slot, peer).start()
            else:
                finish(self.partial_of(p), [(self.inbox.at[e], c) for e, c, _ in kids])

        when(cond, act)
        if any(offset):
            self.sent.append((cond, slot))

    def marks(self):
        return sorted(offsets(self.order, self.depth), key=lambda t: (-sum(abs(d) for d in t), t))

    def drain(self):
        for cond, slot in self.sent:
            when(cond, self.copy(self.inbox.at[0], 0, slot, self.me).wait_send)

D = 768
H = 12
DH = 64
BLK = 64
R = 3
GLOB = 2
L = 2
PAIRS = H // 2
WIDE = 2 * DH
SHARED = GLOB * BLK
SHARE = 16
HELPERS = SHARED // SHARE
VMEM_LIMIT = 60 * 1024 * 1024

layer_eps = 1e-06
masked_score = -1e30

Z_Y_X, Z_X_Y, X_Y_Z, Y_X_Z = ("z", "y", "x"), ("z", "x", "y"), ("x", "y", "z"), ("y", "x", "z")
Y_X, X_Y = ("y", "x"), ("x", "y")
ANYWHERE = pl.BlockSpec(memory_space=pl.ANY)
IN_VMEM = pl.BlockSpec(memory_space=pltpu.VMEM)


def number_in(depth):
    return lambda p: device_of(p)[0] * depth + p["z"]


def dma(*shape):
    return pltpu.SemaphoreType.DMA(shape)


def gather_weights_kernel(depth, orders, *refs):
    n = len(orders)
    sources, targets = refs[:n], refs[n : 2 * n]
    send, recv, local = refs[2 * n :]
    greet(("y", "x", "z"), depth)
    me = place()
    number = number_in(depth)
    jobs, own, at = [], [], 0
    for i, order in enumerate(orders):
        copy = pltpu.make_async_copy(sources[i], targets[i].at[number(me)], local.at[i])
        copy.start()
        own.append(copy)
        jobs.append(
            Gather(
                sources[i], lambda p, i=i: targets[i].at[number(p)], number, order, depth,
                send, recv.at[i], at,
            )
        )
        at += Gather.sends(order, depth)
    run_gathers(jobs)
    for copy in own:
        copy.wait()


def gather_weights(arrays, orders, depth, n_dev, cid):
    total = sum(Gather.sends(order, depth) for order in orders)
    n = len(arrays)
    return pl.pallas_call(
        partial(gather_weights_kernel, depth, orders),
        out_shape=[jax.ShapeDtypeStruct((n_dev,) + a.shape, a.dtype) for a in arrays],
        in_specs=[ANYWHERE] * n,
        out_specs=[ANYWHERE] * n,
        scratch_shapes=[dma(total), dma(n, n_dev), dma(n)],
        compiler_params=pltpu.CompilerParams(collective_id=cid, has_side_effects=True),
        name="gather_weights",
    )(*arrays)


def fetch_layer(layer, w_qkv, w_out, w_up, w_down, seq_count, depth):
    if seq_count != 8:
        gathered = [
            lax.all_gather(w[layer], ("seq", "batch"), axis=0, tiled=True)
            for w in (w_qkv, w_out, w_up, w_down)
        ]
        return tuple(gathered)
    n_dev = seq_count * depth
    rows = w_down.shape[1] * 2 // 3
    got = gather_weights(
        [w_qkv[layer], w_out[layer], w_up[layer], w_down[layer]],
        [Z_Y_X, Z_X_Y, Z_X_Y, X_Y_Z],
        depth, n_dev, layer,
    )
    return tuple(g.reshape(-1, g.shape[-1]) for g in got)


def to_helpers(depth, source, target, send, recv):
    seq, z = lax.axis_index("seq"), lax.axis_index("batch")

    def copy(j):
        return pltpu.make_async_remote_copy(
            src_ref=source.at[pl.ds(j * SHARE, SHARE)], dst_ref=target, send_sem=send.at[j],
            recv_sem=recv, device_id=(j, z), device_id_type=MESH,
        )

    def begin():
        for j in range(1, HELPERS):
            copy(j).start()

    def own():
        pltpu.sync_copy(source.at[pl.ds(0, SHARE)], target)
        for j in range(1, HELPERS):
            copy(j).wait_send()

    def end():
        pl.when(seq == 0)(own)
        pl.when(seq != 0)(lambda: copy(1).wait_recv())

    pl.when(seq == 0)(begin)
    return end


def to_first(source, target, send, recv):
    seq, z = lax.axis_index("seq"), lax.axis_index("batch")

    def copy(j):
        return pltpu.make_async_remote_copy(
            src_ref=source, dst_ref=target.at[pl.ds(j * SHARE, SHARE)], send_sem=send,
            recv_sem=recv.at[j], device_id=(0, z), device_id_type=MESH,
        )

    for j in range(1, HELPERS):
        pl.when(seq == j)(copy(j).start)

    def end():
        def mine():
            pltpu.sync_copy(source, target.at[pl.ds(0, SHARE)])
            for j in range(1, HELPERS):
                copy(j).wait_recv()

        pl.when(seq == 0)(mine)
        pl.when(seq != 0)(lambda: copy(1).wait_send())

    return end


def greet_first():
    seq, z = lax.axis_index("seq"), lax.axis_index("batch")
    barrier = pltpu.get_barrier_semaphore()

    @pl.when(seq != 0)
    def _():
        pl.semaphore_signal(barrier, inc=1, device_id=(0, z), device_id_type=MESH)

    @pl.when(seq == 0)
    def _():
        pl.semaphore_wait(barrier, HELPERS - 1)


def greet_helpers():
    seq, z = lax.axis_index("seq"), lax.axis_index("batch")
    barrier = pltpu.get_barrier_semaphore()

    @pl.when(seq == 0)
    def _():
        for j in range(1, HELPERS):
            pl.semaphore_signal(barrier, inc=1, device_id=(j, z), device_id_type=MESH)

    @pl.when(seq != 0)
    def _():
        pl.semaphore_wait(barrier, 1)


def number_in_sequence(p):
    return device_of(p)[0]


def gather_rows_kernel(depth, kv_ref, q_ref, all_ref, part_ref, send, recv, local, give, take):
    greet(("y", "x"), depth, HELPERS - 1)
    me = place()
    end = to_helpers(depth, q_ref, part_ref, give, take)
    own = pltpu.make_async_copy(kv_ref, all_ref.at[number_in_sequence(me)], local)
    own.start()
    rows, half = kv_ref.shape[0] // 2, kv_ref.shape[1] // 2
    jobs, at = [], 0
    for i in range(4):
        window = (pl.ds(i // 2 * rows, rows), pl.ds(i % 2 * half, half))
        order = (X_Y, Y_X)[i % 2]
        jobs.append(
            Gather(
                kv_ref.at[window], lambda p, window=window: all_ref.at[(number_in_sequence(p),) + window],
                number_in_sequence, order, depth, send, recv.at[i], at,
            )
        )
        at += Gather.sends(order, depth)
    run_gathers(jobs)
    own.wait()
    end()


def gather_rows(kv, queries, seq_count, depth, cid):
    if seq_count != 8:
        every = lax.all_gather(kv, "seq", axis=0, tiled=True)
        first = lax.all_gather(queries[:SHARED], "seq", axis=0)[0]
        own = jnp.minimum(lax.axis_index("seq"), HELPERS - 1) * SHARE
        return every, lax.dynamic_slice_in_dim(first, own, SHARE, axis=0)
    every, share = pl.pallas_call(
        partial(gather_rows_kernel, depth),
        out_shape=[
            jax.ShapeDtypeStruct((seq_count,) + kv.shape, kv.dtype),
            jax.ShapeDtypeStruct((SHARE, D), queries.dtype),
        ],
        in_specs=[ANYWHERE] * 2,
        out_specs=[ANYWHERE] * 2,
        scratch_shapes=[
            dma(4 * Gather.sends(Y_X, depth)), dma(4, seq_count), dma(), dma(HELPERS), dma(),
        ],
        compiler_params=pltpu.CompilerParams(collective_id=cid, has_side_effects=True),
        name="gather_rows",
    )(kv, queries)
    return every.reshape(-1, kv.shape[1]), share


def spread_kernel(depth, source, target, give, take):
    greet_first()
    to_helpers(depth, source, target, give, take)()


def spread(rows, seq_count, depth, cid):
    if seq_count != 8:
        first = lax.all_gather(rows[:SHARED], "seq", axis=0)[0]
        own = jnp.minimum(lax.axis_index("seq"), HELPERS - 1) * SHARE
        return lax.dynamic_slice_in_dim(first, own, SHARE, axis=0)
    return pl.pallas_call(
        partial(spread_kernel, depth),
        out_shape=jax.ShapeDtypeStruct((SHARE, D), rows.dtype),
        in_specs=[ANYWHERE], out_specs=ANYWHERE,
        scratch_shapes=[dma(HELPERS), dma()],
        compiler_params=pltpu.CompilerParams(collective_id=cid, has_side_effects=True),
        name="spread",
    )(rows)


def collect_kernel(source, target, send, recv):
    greet_helpers()
    to_first(source, target, send, recv)()


def collect(part, rows, seq_count, cid):
    own_index = lax.axis_index("seq")
    if seq_count != 8:
        first = lax.all_gather(part, "seq", axis=0)[:HELPERS].reshape(SHARED, D)
    else:
        first = pl.pallas_call(
            collect_kernel,
            out_shape=jax.ShapeDtypeStruct((SHARED, D), part.dtype),
            in_specs=[ANYWHERE], out_specs=ANYWHERE,
            scratch_shapes=[dma(), dma(HELPERS)],
            compiler_params=pltpu.CompilerParams(collective_id=cid, has_side_effects=True),
            name="collect",
        )(part)
    head = jnp.where(own_index == 0, first.astype(rows.dtype), rows[:SHARED])
    return jnp.concatenate([head, rows[SHARED:]], axis=0)


def chunked(shape):
    rows, columns = shape
    width = columns
    while rows * width > 24 * 1024 and width % 256 == 0:
        width //= 2
    if rows * width > 24 * 1024 and width % 384 == 0:
        width //= 3
    return width, columns // width


def total_of(own, kids, window):
    total = own[window].astype(jnp.float32)
    for ref, cond in kids:
        if cond is None:
            total = total + ref[window].astype(jnp.float32)
        else:
            total = total + lax.cond(
                cond,
                lambda ref=ref: ref[window].astype(jnp.float32),
                lambda total=total: jnp.zeros_like(total),
            )
    return total


def over_chunks(shape, act):
    width, count = chunked(shape)

    def step(i, carry):
        act((slice(None), pl.ds(pl.multiple_of(i * width, width), width)))
        return carry

    lax.fori_loop(0, count, step, 0)


def add_up(own, kids, into):
    def act(window):
        into[window] = total_of(own, kids, window).astype(into.dtype)

    over_chunks(into.shape, act)


def write_total(target):
    def finish(own, kids):
        def act(window):
            target[window] = total_of(own, kids, window).astype(target.dtype)

        over_chunks(target.shape, act)

    return finish


def run_reduces(jobs):
    marks = [(k, i, t) for i, (job, _) in enumerate(jobs) for k, t in enumerate(job.marks())]
    marks.sort()
    for _, i, t in marks:
        jobs[i][0].start(t)
    for _, i, t in marks:
        jobs[i][0].handle(t, add_up, write_total(jobs[i][1]))
    for job, _ in jobs:
        job.drain()


def reduce_rows_kernel(depth, dk_ref, dv_ref, out_ref, *scratch):
    inboxes, (send, recv) = scratch[:4], scratch[4:]
    greet(("y", "x"), depth)
    rows, half = out_ref.shape[0] // 2, out_ref.shape[1] // 2
    jobs = []
    for i in range(4):
        source = (dk_ref, dv_ref)[i % 2]
        window = pl.ds(i // 2 * rows, rows)
        order = (X_Y, Y_X)[i % 2]
        jobs.append(
            (
                Reduce(
                    lambda p, source=source, window=window: source.at[number_in_sequence(p), window],
                    inboxes[i], number_in_sequence, order, depth, send.at[i], recv.at[i],
                ),
                out_ref.at[window, pl.ds(i % 2 * half, half)],
            )
        )
    run_reduces(jobs)


def reduce_rows(dk, dv, seq_count, depth, cid):
    if seq_count != 8:
        both_parts = jnp.concatenate([dk, dv], axis=1).astype(jnp.float32)
        return lax.psum_scatter(both_parts, "seq", scatter_dimension=0, tiled=True)
    rows = dk.shape[0] // seq_count
    edges = len(Reduce.edge_table(Y_X, depth))
    slots = 2 * len(offsets(Y_X, depth))
    return pl.pallas_call(
        partial(reduce_rows_kernel, depth),
        out_shape=jax.ShapeDtypeStruct((rows, 2 * D), jnp.float32),
        in_specs=[IN_VMEM] * 2,
        out_specs=IN_VMEM,
        scratch_shapes=[pltpu.VMEM((edges, rows // 2, D), dk.dtype) for _ in range(4)]
        + [dma(4, slots), dma(4, edges)],
        compiler_params=pltpu.CompilerParams(
            collective_id=cid, has_side_effects=True, vmem_limit_bytes=VMEM_LIMIT
        ),
        name="reduce_rows",
    )(dk.reshape(seq_count, rows, D), dv.reshape(seq_count, rows, D))


def reduce_weights_kernel(depth, orders, *refs):
    n = len(orders)
    sources, targets, inboxes = refs[:n], refs[n : 2 * n], refs[2 * n : 3 * n]
    send, recv = refs[3 * n : 4 * n], refs[4 * n :]
    greet(("y", "x", "z"), depth)
    number = number_in(depth)
    run_reduces(
        [
            (
                Reduce(
                    lambda p, i=i: sources[i].at[number(p)], inboxes[i], number, orders[i], depth,
                    send[i], recv[i],
                ),
                targets[i],
            )
            for i in range(n)
        ]
    )


def reduce_weights(parts, orders, depth, cid):
    n = len(parts)
    edges = [len(Reduce.edge_table(order, depth)) for order in orders]
    slots = [2 * len(offsets(order, depth)) for order in orders]
    return pl.pallas_call(
        partial(reduce_weights_kernel, depth, orders),
        out_shape=[jax.ShapeDtypeStruct(a.shape[1:], jnp.float32) for a in parts],
        in_specs=[IN_VMEM] * n,
        out_specs=[IN_VMEM] * n,
        scratch_shapes=[pltpu.VMEM((e,) + a.shape[1:], a.dtype) for e, a in zip(edges, parts)]
        + [dma(s) for s in slots]
        + [dma(e) for e in edges],
        compiler_params=pltpu.CompilerParams(
            collective_id=cid, has_side_effects=True, vmem_limit_bytes=VMEM_LIMIT
        ),
        name="reduce_weights",
    )(*parts)


def own_layer(parts, seq_count, depth, cid):
    n_dev = seq_count * depth
    if seq_count != 8:
        *matrices, small = parts
        return [
            lax.psum_scatter(a.astype(jnp.float32), ("seq", "batch"), scatter_dimension=0, tiled=True)
            for a in matrices
        ] + [lax.psum_scatter(small, ("seq", "batch"), scatter_dimension=0, tiled=True)[0]]
    cut = [a.astype(jnp.bfloat16).reshape(n_dev, -1, a.shape[-1]) for a in parts[:4]] + [parts[4]]
    return reduce_weights(cut, [Z_Y_X, Z_X_Y, Z_X_Y, X_Y_Z, Z_Y_X], depth, cid)


def product(a, b):
    return lax.dot_general(a, b, (((1,), (0,)), ((), ())), preferred_element_type=jnp.float32)


def product_nt(a, b):
    return lax.dot_general(a, b, (((1,), (1,)), ((), ())), preferred_element_type=jnp.float32)


def product_tn(a, b):
    return lax.dot_general(a, b, (((0,), (0,)), ((), ())), preferred_element_type=jnp.float32)


def head_masks(dtype):
    lane = lax.broadcasted_iota(jnp.int32, (1, WIDE), 1)
    return [(lane < DH).astype(dtype), (lane >= DH).astype(dtype)]


def key_places(picks_ref, first, block, head, blocks_all):
    def row(index):
        return pl.multiple_of(index * BLK, BLK)

    drawn = [row(picks_ref[(block * H + head) * R + r]) for r in range(R)]
    window = [row(jnp.clip(first + block + j - 1, 0, blocks_all - 1)) for j in range(3)]
    return [drawn[0], drawn[1]] + window + [drawn[2]]


def bring(picks_ref, first_ref, pair, pairs, blocks_here):
    for block in range(blocks_here):
        for side in range(2):
            places = key_places(
                picks_ref, first_ref[0], block, 2 * pair + side, pairs[0][0].shape[0] // BLK
            )
            for source, target in pairs:
                for i, at in enumerate(places):
                    target[2 * block + side, i * BLK : (i + 1) * BLK] = source[pl.ds(at, BLK)]


def with_shared(ref, near):
    return jnp.concatenate([ref[0:SHARED], near], axis=0)


def soft(scores):
    top = jnp.max(scores, axis=1, keepdims=True)
    weight = jnp.exp(scores - top)
    return weight * (1.0 / jnp.sum(weight, axis=1, keepdims=True))


def local_scores(q_head, keys, shut):
    scores = product_nt(q_head, keys)
    half = scores.shape[1] // 2
    return jnp.concatenate([scores[:, :half], scores[:, half:] + shut], axis=1)


def attend_kernel(
    picks_ref, first_ref, q_ref, k_ref, v_ref, shut_ref, part_ref, o_ref, po_ref, near_k, near_v
):
    pair = pl.program_id(0)
    blocks_here = q_ref.shape[0] // BLK
    bring(picks_ref, first_ref, pair, [(k_ref, near_k), (v_ref, near_v)], blocks_here)
    masks = head_masks(jnp.bfloat16)
    low_lanes = lax.broadcasted_iota(jnp.int32, (1, WIDE), 1) < DH
    scale = jnp.bfloat16(DH ** (-0.5))
    part = part_ref[...] * scale
    both_heads = jnp.concatenate([part * masks[0], part * masks[1]], axis=0)
    weight = soft(product_nt(both_heads, k_ref[...])).astype(jnp.bfloat16)
    mixed = product(weight, v_ref[...])
    po_ref[...] = jnp.where(low_lanes, mixed[:SHARE], mixed[SHARE:]).astype(po_ref.dtype)
    for block in range(blocks_here):
        q = q_ref[block * BLK : (block + 1) * BLK] * scale
        mixed = []
        for side in range(2):
            at = 2 * block + side
            scores = local_scores(q * masks[side], with_shared(k_ref, near_k[at]), shut_ref[block])
            weight = soft(scores).astype(jnp.bfloat16)
            mixed.append(product(weight, with_shared(v_ref, near_v[at])))
        o_ref[block * BLK : (block + 1) * BLK] = jnp.where(low_lanes, mixed[0], mixed[1]).astype(o_ref.dtype)


def near_rows(rows, dtype):
    return pltpu.VMEM((2 * (rows // BLK), 6 * BLK, WIDE), dtype)


def columns(rows, shift=0):
    return pl.BlockSpec((rows, WIDE), lambda p, *_: (0, p + shift))


def attend(picks, first, queries, kv, shut, part):
    rows, length = queries.shape[0], kv.shape[0]
    return pl.pallas_call(
        attend_kernel,
        grid_spec=pltpu.PrefetchScalarGridSpec(
            num_scalar_prefetch=2,
            grid=(PAIRS,),
            in_specs=[
                columns(rows), columns(length), columns(length, PAIRS),
                pl.BlockSpec(shut.shape, lambda p, *_: (0, 0, 0)), columns(SHARE),
            ],
            out_specs=[columns(rows), columns(SHARE)],
            scratch_shapes=[near_rows(rows, jnp.bfloat16)] * 2,
        ),
        out_shape=[
            jax.ShapeDtypeStruct((rows, D), jnp.bfloat16),
            jax.ShapeDtypeStruct((SHARE, D), jnp.bfloat16),
        ],
        compiler_params=pltpu.CompilerParams(vmem_limit_bytes=VMEM_LIMIT),
        name="attend",
    )(picks, first, queries, kv, kv, shut, part)


def score_grads(weight, cot_head, values):
    grads = product_nt(cot_head, values)
    mean = jnp.sum(weight * grads, axis=1, keepdims=True)
    return (weight * (grads - mean)).astype(jnp.bfloat16)


def attend_back_kernel(
    picks_ref, first_ref, q_ref, k_ref, v_ref, shut_ref, do_ref, part_ref, pdo_ref,
    dq_ref, dk_ref, dv_ref, pdq_ref, sum_k, sum_v, near_k, near_v, grad_k, grad_v,
):
    pair = pl.program_id(0)
    blocks_here, blocks_all = q_ref.shape[0] // BLK, k_ref.shape[0] // BLK
    bring(picks_ref, first_ref, pair, [(k_ref, near_k), (v_ref, near_v)], blocks_here)
    masks = head_masks(jnp.bfloat16)
    low_lanes = lax.broadcasted_iota(jnp.int32, (1, WIDE), 1) < DH
    step = DH ** (-0.5)
    scale = jnp.bfloat16(step)
    part = part_ref[...] * scale
    part = jnp.concatenate([part * masks[0], part * masks[1]], axis=0)
    cot = pdo_ref[...]
    cot = jnp.concatenate([cot * masks[0], cot * masks[1]], axis=0)
    weight = soft(product_nt(part, k_ref[...]))
    grads = score_grads(weight, cot, v_ref[...])
    mixed = product(grads, k_ref[...]) * step
    pdq_ref[...] = jnp.where(low_lanes, mixed[:SHARE], mixed[SHARE:]).astype(pdq_ref.dtype)
    sum_k[...] = product_tn(grads, part)
    sum_v[...] = product_tn(weight.astype(jnp.bfloat16), cot)
    shared_k = jnp.zeros((SHARED, WIDE), jnp.float32)
    shared_v = jnp.zeros((SHARED, WIDE), jnp.float32)
    for block in range(blocks_here):
        here = slice(block * BLK, (block + 1) * BLK)
        q, do = q_ref[here] * scale, do_ref[here]
        mixed = []
        for side in range(2):
            near = 2 * block + side
            keys, values = with_shared(k_ref, near_k[near]), with_shared(v_ref, near_v[near])
            q_head, do_head = q * masks[side], do * masks[side]
            weight = soft(local_scores(q_head, keys, shut_ref[block]))
            grads = score_grads(weight, do_head, values)
            mixed.append(product(grads, keys))
            key_grad = product_tn(grads, q_head)
            value_grad = product_tn(weight.astype(jnp.bfloat16), do_head)
            shared_k = shared_k + key_grad[:SHARED]
            shared_v = shared_v + value_grad[:SHARED]
            grad_k[near] = key_grad[SHARED:]
            grad_v[near] = value_grad[SHARED:]
        dq_ref[here] = (jnp.where(low_lanes, mixed[0], mixed[1]) * step).astype(dq_ref.dtype)
    sum_k[0:SHARED] += shared_k
    sum_v[0:SHARED] += shared_v
    for block in range(blocks_here):
        for side in range(2):
            places = key_places(picks_ref, first_ref[0], block, 2 * pair + side, blocks_all)
            for i, at in enumerate(places):
                source = slice(i * BLK, (i + 1) * BLK)
                sum_k[pl.ds(at, BLK)] += grad_k[2 * block + side, source]
                sum_v[pl.ds(at, BLK)] += grad_v[2 * block + side, source]
    dk_ref[...] = sum_k[...].astype(dk_ref.dtype)
    dv_ref[...] = sum_v[...].astype(dv_ref.dtype)


def attend_back(picks, first, queries, kv, shut, cot, part, part_cot):
    rows, length = queries.shape[0], kv.shape[0]
    return pl.pallas_call(
        attend_back_kernel,
        grid_spec=pltpu.PrefetchScalarGridSpec(
            num_scalar_prefetch=2,
            grid=(PAIRS,),
            in_specs=[
                columns(rows), columns(length), columns(length, PAIRS),
                pl.BlockSpec(shut.shape, lambda p, *_: (0, 0, 0)), columns(rows), columns(SHARE), columns(SHARE),
            ],
            out_specs=[columns(rows), columns(length), columns(length), columns(SHARE)],
            scratch_shapes=[pltpu.VMEM((length, WIDE), jnp.float32)] * 2
            + [near_rows(rows, jnp.bfloat16)] * 2
            + [near_rows(rows, jnp.float32)] * 2,
        ),
        out_shape=[
            jax.ShapeDtypeStruct((rows, D), jnp.bfloat16),
            jax.ShapeDtypeStruct((length, D), jnp.bfloat16),
            jax.ShapeDtypeStruct((length, D), jnp.bfloat16),
            jax.ShapeDtypeStruct((SHARE, D), jnp.bfloat16),
        ],
        compiler_params=pltpu.CompilerParams(vmem_limit_bytes=VMEM_LIMIT),
        name="attend_back",
    )(picks, first, queries, kv, kv, shut, cot, part, part_cot)


def norm_rows(resid, gain, shift):
    center = resid - jnp.mean(resid, axis=-1, keepdims=True)
    inv_std = lax.rsqrt(jnp.mean(center * center, axis=-1, keepdims=True) + layer_eps)
    normed = center * inv_std
    return (normed * gain + shift, normed, inv_std)


def norm_back(grad_rows, normed, inv_std, gain):
    scaled = grad_rows * gain
    return (
        scaled
        - jnp.mean(scaled, axis=-1, keepdims=True)
        - normed * jnp.mean(scaled * normed, axis=-1, keepdims=True)
    ) * inv_std


def dot32(a, b):
    return jnp.dot(a, b, preferred_element_type=jnp.float32)


def on_device(
    layer_input, segments, rand_blocks, w_qkv, w_out, w_up, w_down, gains, biases, up_bias, d_out
):
    seq_count, depth = lax.axis_size("seq"), lax.axis_size("batch")
    n_dev = seq_count * depth
    own_index = lax.axis_index("seq")
    rows = layer_input.shape[1]
    blocks_here, length = rows // BLK, rows * seq_count
    picks = rand_blocks.reshape(-1)
    first = (own_index * blocks_here).reshape(1)

    piece = D // n_dev
    small = jnp.concatenate(
        [biases.reshape(L, -1), gains.reshape(L, -1), up_bias], axis=1
    )
    small = lax.all_gather(small, ("seq", "batch"), axis=0).astype(jnp.float32)
    vectors = jnp.moveaxis(small[:, :, : 8 * piece].reshape(n_dev, L, 8, piece), 0, 2).reshape(L, 8, D)
    hidden_shifts = jnp.moveaxis(small[:, :, 8 * piece :], 0, 1).reshape(L, -1)

    segs_all = lax.all_gather(segments[0], "seq", axis=0, tiled=True)
    padding = jnp.full((BLK,), -1, jnp.int32)
    segs_all = jnp.concatenate([padding, segs_all, padding]).reshape(-1, BLK)
    segs_near = lax.dynamic_slice_in_dim(segs_all, first[0], blocks_here + 2, axis=0)
    seg_window = jnp.concatenate([segs_near[j : j + blocks_here] for j in range(3)], axis=1)
    spot = (first[0] - 1 + jnp.arange(blocks_here)[:, None]) * BLK + jnp.arange(3 * BLK)[None, :]
    inside = (spot >= SHARED) & (spot < length)
    allowed = inside[:, None, :] & (seg_window[:, None, :] == segments.reshape(blocks_here, BLK)[:, :, None])
    shut = jnp.pad(jnp.where(allowed, 0.0, masked_score), ((0, 0), (0, 0), (0, BLK)))

    weights = [
        fetch_layer(layer, w_qkv, w_out, w_up, w_down, seq_count, depth) for layer in range(L)
    ]
    resid = layer_input[0].astype(jnp.float32)
    low = layer_input[0]
    saved = []
    for layer in range(L):
        mat_qkv, mat_out, mat_up, mat_down = weights[layer]
        bias = vectors[layer]
        proj = dot32(low, mat_qkv)
        queries = (proj[:, :D] + bias[0]).astype(jnp.bfloat16)
        kv = jnp.concatenate([proj[:, D : 2 * D], proj[:, 2 * D :] + bias[1]], axis=1).astype(jnp.bfloat16)
        kv_all, part = gather_rows(kv, queries, seq_count, depth, 2 + layer)
        mixed, part_mixed = attend(picks, first, queries, kv_all, shut, part)
        mixed = collect(part_mixed, mixed, seq_count, 4 + layer)
        resid_one = resid + dot32(mixed, mat_out) + bias[2]
        middle, normed_one, inv_one = norm_rows(resid_one, bias[6], bias[3])
        middle_low = middle.astype(jnp.bfloat16)
        hidden = dot32(middle_low, mat_up) + hidden_shifts[layer]
        active = jax.nn.gelu(hidden, approximate=False).astype(jnp.bfloat16)
        resid_two = middle + dot32(active, mat_down) + bias[4]
        result, normed_two, inv_two = norm_rows(resid_two, bias[7], bias[5])
        saved.append(
            (low, queries, kv_all, part, mixed, normed_one, inv_one, middle_low, hidden, active, normed_two, inv_two)
        )
        resid = result
        low = resid.astype(jnp.bfloat16)

    grad = d_out[0].astype(jnp.float32)
    owned = [None] * L
    is_shared = (own_index == 0) & (jnp.arange(rows) < SHARED)[:, None]
    for layer in reversed(range(L)):
        (low_in, queries, kv_all, part, mixed, normed_one, inv_one, middle_low, hidden, active, normed_two, inv_two) = saved[layer]
        mat_qkv, mat_out, mat_up, mat_down = weights[layer]
        bias = vectors[layer]
        gain_two_grad = jnp.sum(grad * normed_two, axis=0)
        shift_two_grad = jnp.sum(grad, axis=0)
        grad_two = norm_back(grad, normed_two, inv_two, bias[7])
        grad_two_low = grad_two.astype(jnp.bfloat16)
        down_grad = product_tn(active, grad_two_low)
        active_grad = product_nt(grad_two_low, mat_down)
        hidden_grad = jax.vjp(partial(jax.nn.gelu, approximate=False), hidden)[1](active_grad)[0]
        hidden_grad_low = hidden_grad.astype(jnp.bfloat16)
        up_grad = product_tn(middle_low, hidden_grad_low)
        middle_grad = grad_two + product_nt(hidden_grad_low, mat_up)
        gain_one_grad = jnp.sum(middle_grad * normed_one, axis=0)
        shift_one_grad = jnp.sum(middle_grad, axis=0)
        grad_one = norm_back(middle_grad, normed_one, inv_one, bias[6])
        grad_one_low = grad_one.astype(jnp.bfloat16)
        out_grad = product_tn(mixed, grad_one_low)
        cot = product_nt(grad_one_low, mat_out).astype(jnp.bfloat16)
        part_cot = spread(cot, seq_count, depth, 6 + layer)
        part_cot = jnp.where(own_index < HELPERS, part_cot, 0)
        cot = jnp.where(is_shared, 0, cot)
        dq, dk, dv, part_dq = attend_back(picks, first, queries, kv_all, shut, cot, part, part_cot)
        dq = collect(part_dq, dq, seq_count, 8 + layer)
        dkv = reduce_rows(dk, dv, seq_count, depth, 10 + layer)
        proj_grad = jnp.concatenate([dq, dkv.astype(jnp.bfloat16)], axis=1)
        qkv_grad = product_tn(low_in, proj_grad)
        small_rows = jnp.stack(
            [
                jnp.sum(dq.astype(jnp.float32), axis=0),
                jnp.sum(dkv[:, D:], axis=0),
                jnp.sum(grad_one, axis=0),
                shift_one_grad,
                jnp.sum(grad_two, axis=0),
                shift_two_grad,
                gain_one_grad,
                gain_two_grad,
            ]
        )
        small_rows = jnp.moveaxis(small_rows.reshape(8, n_dev, piece), 1, 0)
        hidden_rows = jnp.sum(hidden_grad, axis=0).reshape(n_dev, 8, -1)
        small_rows = jnp.concatenate([small_rows, hidden_rows], axis=2)
        small_rows = jnp.pad(small_rows, ((0, 0), (0, 0), (0, 128 - small_rows.shape[2])))
        owned[layer] = own_layer(
            [qkv_grad, out_grad, up_grad, down_grad, small_rows], seq_count, depth, 12 + layer
        )
        grad = grad_one + product_nt(proj_grad, mat_qkv)
    stacked = [jnp.stack([owned[layer][i] for layer in range(L)]) for i in range(5)]
    narrow = stacked[4]
    return (
        low[None],
        grad[None],
        stacked[0],
        stacked[1],
        stacked[2],
        stacked[3],
        narrow[:, 6:8, :piece],
        narrow[:, 0:6, :piece],
        narrow[:, :, piece : piece + up_bias.shape[1] // 8].reshape(L, -1),
    )


def solution(mesh):
    placed = (
        P("batch", "seq", None),
        P("batch", "seq"),
        P("batch", "seq", None, None),
        P(None, ("seq", "batch"), None),
        P(None, ("seq", "batch"), None),
        P(None, ("seq", "batch"), None),
        P(None, ("seq", "batch"), None),
        P(None, None, ("seq", "batch")),
        P(None, None, ("seq", "batch")),
        P(None, ("seq", "batch")),
        P("batch", "seq", None),
    )
    return jax.shard_map(
        on_device,
        mesh=mesh,
        in_specs=placed,
        out_specs=(
            P("batch", "seq", None),
            P("batch", "seq", None),
            P(None, ("seq", "batch"), None),
            P(None, ("seq", "batch"), None),
            P(None, ("seq", "batch"), None),
            P(None, ("seq", "batch"), None),
            P(None, None, ("seq", "batch")),
            P(None, None, ("seq", "batch")),
            P(None, ("seq", "batch")),
        ),
        check_vma=False,
    )
```

time: 3440 us -> 821 us (0.24)
  local copies, waits for them, and re-layouts: 1130 us -> 44.5 us
  waiting for transfers between devices: 1080 us -> 0 us
  Pallas kernels: 0 us -> 553 us
  blocking collectives: 489 us -> 77.7 us
  matrix products: 359 us -> 94.9 us
  other arithmetic: 191 us -> 40.1 us
  loops' own time: 102 us -> 0 us
  starting transfers between devices: 47.6 us -> 0 us
    reduce_scatter x6 -> x0, waiting for transfers between devices: 608 us -> none  [the longest x2 281 us: on_device(): lax.psum_scatter(down_grad, ('seq', 'batch'), scatter_dimension=0, tiled=...]
    pallas_call x0 -> x18, Pallas kernels: none -> 553 us  [the longest x2 146 us: reduce_weights(): pl.pallas_call(partial(reduce_weights_kernel, depth, orders), out_shape=[...]
    reshape x195 -> x8, local copies, waits for them, and re-layouts: 376 us -> 4.73 us  [the longest x2 2.35 us: on_device(): hidden_rows = jnp.sum(hidden_grad, axis=0).reshape(n_dev, 8, -1)]
    unnamed x26 -> x0, waiting for transfers between devices: 368 us -> none
    all_gather x8 -> x2, blocking collectives: 361 us -> 77.7 us  [the longest x1 70 us: on_device(): small = lax.all_gather(small, ('seq', 'batch'), axis=0).astype(jnp.float32)]
    dot_general x179 -> x24, matrix products: 292 us -> 94.9 us  [the longest x8 40.3 us: dot32(): return jnp.dot(a, b, preferred_element_type=jnp.float32)]
    another operation x187 -> x18, local copies, waits for them, and re-layouts: 193 us -> 18.1 us  [on_device(): jnp.stack([jnp.sum(dq.astype(jnp.float32), axis=0), jnp.sum(dkv[:, D:], a...]
    slice x172 -> x7, local copies, waits for them, and re-layouts: 144 us -> 2.04 us  [the longest x1 1.22 us: on_device(): result, normed_two, inv_two = norm_rows(resid_two, bias[7], bias[5])]
  transfers between devices with their start and end apart: 38 -> 0, of which waited for: 11 -> 0; matrix products, arithmetic and copies ran while one was open for 36% -> 0% of each run, Pallas kernels for 0% -> 0%
where the time goes in v1:
time: 821 us; the launch traced here: 812 us
  Pallas kernels  553 us (67%)
  matrix products  94.9 us (12%)
  blocking collectives  77.7 us (9%)
  local copies, waits for them, and re-layouts  44.5 us (5%)
  other arithmetic  40.1 us (5%)
    pallas_call x2, Pallas kernels, reduce_weights(): pl.pallas_call(partial(reduce_weights_kernel, depth, orders), out_shape=[...  146 us
    pallas_call x2, Pallas kernels, gather_weights(): pl.pallas_call(partial(gather_weights_kernel, depth, orders), out_shape=[...  122 us
    pallas_call x2, Pallas kernels, attend_back(): pl.pallas_call(attend_back_kernel, grid_spec=pltpu.PrefetchScalarGridSpec...  76.8 us
    all_gather x1, blocking collectives, on_device(): small = lax.all_gather(small, ('seq', 'batch'), axis=0).astype(jnp.float32)  70 us
    pallas_call x2, Pallas kernels, gather_rows(): pl.pallas_call(partial(gather_rows_kernel, depth), out_shape=[jax.ShapeDt...  66.4 us
    pallas_call x2, Pallas kernels, reduce_rows(): pl.pallas_call(partial(reduce_rows_kernel, depth), out_shape=jax.ShapeDty...  66 us
    pallas_call x2, Pallas kernels, attend(): pl.pallas_call(attend_kernel, grid_spec=pltpu.PrefetchScalarGridSpec(num_...  46.9 us
    dot_general x8, matrix products, dot32(): return jnp.dot(a, b, preferred_element_type=jnp.float32)  40.3 us

profile of v1, /device:TPU:0, one launch (start us, length us, event | category | flops | bytes accessed | tf_op | source)
XLA Modules:
  0.0 812.2 jit_solution(1930361575894325674)
XLA Ops:
  3.0 70.0 %all-gather.2 = bf16[32,2,288]{2,1,0:T(2,128)(2,1)S(1)} all-gather(bf16[1,2,288]{2,1,0:T(2,128)(2,1)S(1)} %maximum_bitcast_fusion), channel_id=2, replica_groups=mesh['seq'=8,'batch'=4] {'seq','batch'}, dimensions={0}, use_global_device_ids=true | all-gather | bytes 38016 | tf_op jit(solution)/shard_map/all_gather | solution.py:916
  81.0 60.7 %gather_weights.2 = (bf16[32,24,2304]{2,1,0:T(8,128)(2,1)}, bf16[32,24,768]{2,1,0:T(8,128)(2,1)}, bf16[32,24,3072]{2,1,0:T(8,128)(2,1)}, bf16[32,96,768]{2,1,0:T(8,128)(2,1)}) custom-call(bf16[24,2304]{1,0:T(8,128)(2,1)} %get-tuple-element.166.refs_0_, bf16[24,768]{1,0:T(8,128)(2,1)} %get-tuple-element.168.refs_1_, ...), custom_call_target="tpu_custom_call" | custom-call | tf_op jit(solution)/shard_map/gather_weights/pallas_call | solution.py:333
  146.7 33.0 %gather_rows.2 = (bf16[8,256,1536]{2,1,0:T(8,128)(2,1)}, bf16[16,768]{1,0:T(8,128)(2,1)}) custom-call(bf16[256,1536]{1,0:T(8,128)(2,1)} %pad_maximum_fusion.2.kv_ref, bf16[256,768]{1,0:T(8,128)(2,1)} %get-tuple-element.152.q_ref), custom_call_target="tpu_custom_call" | custom-call | tf_op jit(solution)/shard_map/gather_rows/pallas_call | solution.py:471
  179.7 7.7 all-gather.1
  190.7 23.4 %attend.2 = (bf16[256,768]{1,0:T(8,128)(2,1)}, bf16[16,768]{1,0:T(8,128)(2,1)}) custom-call(s32[144]{0:T(256)} %reshape.303.picks_ref, s32[1]{0:T(128)} %bitcast.1.first_ref, bf16[256,768]{1,0:T(8,128)(2,1)} %get-tuple-element.152.q_ref, bf16[2048,1536]{1,0:T(8,128)(2,1)} %bitcast.134, bf16[2048,1536]{1,0:T(8,128)(2,1)} %bitcast.135, ...), custom_call_target="tpu_custom_call" | custom-call | tf_op jit(solution)/shard_map/attend/pallas_call | solution.py:773
  214.1 5.3 collect.4
  222.6 11.3 %multiply_convert_fusion.1 = (bf16[256,3072]{1,0:T(8,128)(2,1)S(1)}, f32[256,3072]{1,0:T(8,128)}, f32[256,3072]{1,0:T(8,128)}) fusion(f32[3072]{0:T(1024)S(1)} %add.254, bf16[768,3072]{1,0:T(8,128)(2,1)} %bitcast.196, f32[256,768]{1,0:T(8,128)S(1)} %get-tuple-element.174, f32[768]{0:T(1024)S(1)} %add.251, f32[768]{0:T(1024)S(1)} %mul.262, ...), kind=kOutput, calls=%fused_computation.28 | convolution fusion | flops 1260847104 | bytes 13389824 | tf_op jit(solution)/shard_map/dot_general | solution.py:898
  234.1 4.3 fusion.81
  239.7 61.6 %gather_weights.3 = (bf16[32,24,2304]{2,1,0:T(8,128)(2,1)}, bf16[32,24,768]{2,1,0:T(8,128)(2,1)}, bf16[32,24,3072]{2,1,0:T(8,128)(2,1)}, bf16[32,96,768]{2,1,0:T(8,128)(2,1)}) custom-call(bf16[24,2304]{1,0:T(8,128)(2,1)} %get-tuple-element.167.refs_0_, bf16[24,768]{1,0:T(8,128)(2,1)} %get-tuple-element.169.refs_1_, ...), custom_call_target="tpu_custom_call" | custom-call | tf_op jit(solution)/shard_map/gather_weights/pallas_call | solution.py:333
  301.3 3.4 fusion.68
  306.7 33.4 %gather_rows.3 = (bf16[8,256,1536]{2,1,0:T(8,128)(2,1)}, bf16[16,768]{1,0:T(8,128)(2,1)}) custom-call(bf16[256,1536]{1,0:T(8,128)(2,1)} %pad_maximum_fusion.3.kv_ref, bf16[256,768]{1,0:T(8,128)(2,1)} %get-tuple-element.150.q_ref), custom_call_target="tpu_custom_call" | custom-call | tf_op jit(solution)/shard_map/gather_rows/pallas_call | solution.py:471
  340.2 23.4 %attend.3 = (bf16[256,768]{1,0:T(8,128)(2,1)}, bf16[16,768]{1,0:T(8,128)(2,1)}) custom-call(s32[144]{0:T(256)} %reshape.303.picks_ref, s32[1]{0:T(128)} %bitcast.1.first_ref, bf16[256,768]{1,0:T(8,128)(2,1)} %get-tuple-element.150.q_ref, bf16[2048,1536]{1,0:T(8,128)(2,1)} %bitcast.138, bf16[2048,1536]{1,0:T(8,128)(2,1)} %bitcast.139, ...), custom_call_target="tpu_custom_call" | custom-call | tf_op jit(solution)/shard_map/attend/pallas_call | solution.py:773
  363.6 5.3 collect.5
  375.8 11.7 %multiply_convert_fusion = (bf16[256,3072]{1,0:T(8,128)(2,1)}, f32[256,3072]{1,0:T(8,128)}, f32[256,3072]{1,0:T(8,128)}) fusion(f32[3072]{0:T(1024)S(1)} %add.279, bf16[768,3072]{1,0:T(8,128)(2,1)} %bitcast.202, f32[256,768]{1,0:T(8,128)S(1)} %get-tuple-element.179, f32[768]{0:T(1024)S(1)} %add.276, f32[768]{0:T(1024)S(1)} %mul.277, ...), kind=kOutput, calls=%fused_computation.15 | convolution fusion | flops 1260847104 | bytes 13389824 | tf_op jit(solution)/shard_map/dot_general | solution.py:898
  388.2 4.4 fusion.83
  401.6 7.2 fusion.84
  417.6 38.5 %attend_back.2 = (bf16[256,768]{1,0:T(8,128)(2,1)}, bf16[2048,768]{1,0:T(8,128)(2,1)}, bf16[2048,768]{1,0:T(8,128)(2,1)}, bf16[16,768]{1,0:T(8,128)(2,1)}) custom-call(s32[144]{0:T(256)} %reshape.303.picks_ref, s32[1]{0:T(128)} %bitcast.1.first_ref, bf16[256,768]{1,0:T(8,128)(2,1)} %get-tuple-element.150.q_ref, bf16[2048,1536]{1,0:T(8,128)(2,1)} %bitcast.140, ...), custom_call_target="tpu_custom_call" | custom-call | tf_op jit(solution)/shard_map/attend_back/pallas_call | solution.py:856
  456.1 5.2 collect.6
  462.5 33.0 %reduce_rows.2 = f32[256,1536]{1,0:T(8,128)} custom-call(bf16[8,256,768]{2,1,0:T(8,128)(2,1)} %bitcast.156, bf16[8,256,768]{2,1,0:T(8,128)(2,1)} %bitcast.157), custom_call_target="tpu_custom_call" | custom-call | tf_op jit(solution)/shard_map/reduce_rows/pallas_call | solution.py:620
  497.1 4.2 multiply_reduce_fusion.1
  502.3 5.2 fusion.85
  512.0 4.5 spread.3
  517.9 38.3 %attend_back.3 = (bf16[256,768]{1,0:T(8,128)(2,1)}, bf16[2048,768]{1,0:T(8,128)(2,1)}, bf16[2048,768]{1,0:T(8,128)(2,1)}, bf16[16,768]{1,0:T(8,128)(2,1)}) custom-call(s32[144]{0:T(256)} %reshape.303.picks_ref, s32[1]{0:T(128)} %bitcast.1.first_ref, bf16[256,768]{1,0:T(8,128)(2,1)} %get-tuple-element.152.q_ref, bf16[2048,1536]{1,0:T(8,128)(2,1)} %bitcast.136, ...), custom_call_target="tpu_custom_call" | custom-call | tf_op jit(solution)/shard_map/attend_back/pallas_call | solution.py:856
  556.2 5.3 collect.7
  565.5 33.0 %reduce_rows.3 = f32[256,1536]{1,0:T(8,128)} custom-call(bf16[8,256,768]{2,1,0:T(8,128)(2,1)} %bitcast.154, bf16[8,256,768]{2,1,0:T(8,128)(2,1)} %bitcast.155), custom_call_target="tpu_custom_call" | custom-call | tf_op jit(solution)/shard_map/reduce_rows/pallas_call | solution.py:620
  614.7 5.1 convolution_convert_fusion.3
  619.8 3.7 convolution_convert_fusion.4
  628.4 72.1 %reduce_weights.2 = (f32[24,2304]{1,0:T(8,128)}, f32[24,768]{1,0:T(8,128)}, f32[24,3072]{1,0:T(8,128)}, f32[96,768]{1,0:T(8,128)}, f32[8,128]{1,0:T(8,128)}) custom-call(bf16[32,24,2304]{2,1,0:T(8,128)(2,1)} %bitcast.149, bf16[32,24,768]{2,1,0:T(8,128)(2,1)} %bitcast.147, bf16[32,24,3072]{2,1,0:T(8,128)(2,1)} %bitcast.145, bf16[32,96,768]{2,1,0:T(8,128)(2,1)} %bitcast.143, ...), custom_call_target="tpu_custom_call" | custom-call | tf_op jit(solution)/shard_map/reduce_weights/pallas_call | solution.py:658
  709.2 5.1 convolution_convert_fusion
  714.5 3.7 convolution_convert_fusion.1
  722.9 73.8 %reduce_weights.3 = (f32[24,2304]{1,0:T(8,128)}, f32[24,768]{1,0:T(8,128)}, f32[24,3072]{1,0:T(8,128)}, f32[96,768]{1,0:T(8,128)}, f32[8,128]{1,0:T(8,128)}) custom-call(bf16[32,24,2304]{2,1,0:T(8,128)(2,1)} %bitcast.148, bf16[32,24,768]{2,1,0:T(8,128)(2,1)} %bitcast.146, bf16[32,24,3072]{2,1,0:T(8,128)(2,1)} %bitcast.144, bf16[32,96,768]{2,1,0:T(8,128)(2,1)} %bitcast.142, ...), custom_call_target="tpu_custom_call" | custom-call | tf_op jit(solution)/shard_map/reduce_weights/pallas_call | solution.py:658
  807.8 4.0 fusion.14
  (313 shorter events, 109.1 us)
Async XLA Ops:
  0.6 141.1 %copy-start.43 = (bf16[1,256,768]{2,1,0:T(8,128)(2,1)S(1)}, bf16[1,256,768]{2,1,0:T(8,128)(2,1)}, u32[]{:S(2)}) copy-start(bf16[1,256,768]{2,1,0:T(8,128)(2,1)} %param.11) | copy-start | bytes 1179652
  144.8 34.9 %copy-start.79 = (s32[1,256]{1,0:T(1,128)S(1)}, s32[1,256]{1,0:T(1,128)}, u32[]{:S(2)}) copy-start(s32[1,256]{1,0:T(1,128)} %param.12) | copy-start | bytes 3076
  144.8 45.0 %copy-start.78 = (s32[1,4,12,3]{2,1,3,0:T(4,128)S(1)}, s32[1,4,12,3]{2,1,3,0:T(4,128)}, u32[]{:S(2)}) copy-start(s32[1,4,12,3]{2,1,3,0:T(4,128)} %param.13) | copy-start | bytes 1732
  190.7 30.0 %copy-start.17 = (bf16[32,24,768]{2,1,0:T(8,128)(2,1)S(1)}, bf16[32,24,768]{2,1,0:T(8,128)(2,1)}, u32[]{:S(2)}) copy-start(bf16[32,24,768]{2,1,0:T(8,128)(2,1)} %get-tuple-element.48) | copy-start | bytes 3538948
  221.3 12.8 %copy-start.55 = (f32[256]{0:T(256)}, f32[256]{0:T(256)S(1)}, u32[]{:S(2)}) copy-start(f32[256]{0:T(256)S(1)} %broadcast_multiply_fusion.11) | copy-start | bytes 3076
  238.4 133.1 %copy-start.61 = (f32[256]{0:T(256)}, f32[256]{0:T(256)S(1)}, u32[]{:S(2)}) copy-start(f32[256]{0:T(256)S(1)} %broadcast_multiply_fusion.10) | copy-start | bytes 3076
  239.5 65.3 %copy-start.75 = (f32[256]{0:T(256)}, f32[256]{0:T(256)S(1)}, u32[]{:S(2)}) copy-start(f32[256]{0:T(256)S(1)} %add_rsqrt_fusion.2) | copy-start | bytes 3076
  239.6 132.0 %copy-start.51 = (f32[768]{0:T(1024)}, f32[768]{0:T(1024)S(1)}, u32[]{:S(2)}) copy-start(f32[768]{0:T(1024)S(1)} %mul.271) | copy-start | bytes 9220
  239.7 65.1 %copy-start.65 = (f32[768]{0:T(1024)}, f32[768]{0:T(1024)S(1)}, u32[]{:S(2)}) copy-start(f32[768]{0:T(1024)S(1)} %add.262) | copy-start | bytes 9220
  340.1 30.7 %copy-start.50 = (f32[32,24]{1,0:T(8,128)S(1)}, f32[32,24]{1,0:T(8,128)}, u32[]{:S(2)}) copy-start(f32[32,24]{1,0:T(8,128)} %get-tuple-element.124) | copy-start | bytes 9220
  340.1 31.4 %copy-start.3 = (f32[256,768]{1,0:T(8,128)S(1)}, f32[256,768]{1,0:T(8,128)}, u32[]{:S(2)}) copy-start(f32[256,768]{1,0:T(8,128)} %copy-done.2) | copy-start | bytes 2359300
  340.1 31.4 %copy-start.19 = (bf16[32,24,768]{2,1,0:T(8,128)(2,1)S(1)}, bf16[32,24,768]{2,1,0:T(8,128)(2,1)}, u32[]{:S(2)}) copy-start(bf16[32,24,768]{2,1,0:T(8,128)(2,1)} %get-tuple-element.56) | copy-start | bytes 3538948
  373.2 14.3 %copy-start.58 = (f32[256]{0:T(256)}, f32[256]{0:T(256)S(1)}, u32[]{:S(2)}) copy-start(f32[256]{0:T(256)S(1)} %broadcast_multiply_fusion.9) | copy-start | bytes 3076
  373.4 14.1 %copy-start.72 = (f32[256]{0:T(256)}, f32[256]{0:T(256)S(1)}, u32[]{:S(2)}) copy-start(f32[256]{0:T(256)S(1)} %add_rsqrt_fusion.1) | copy-start | bytes 3076
  411.9 85.1 %copy-start.5 = (f32[256,768]{1,0:T(8,128)}, f32[256,768]{1,0:T(8,128)S(1)}, u32[]{:S(2)}) copy-start(f32[256,768]{1,0:T(8,128)S(1)} %get-tuple-element.144) | copy-start | bytes 2359300
  462.4 34.6 %copy-start.27 = (bf16[128,768]{1,0:T(8,128)(2,1)}, bf16[128,768]{1,0:T(8,128)(2,1)S(1)}, u32[]{:S(2)}) copy-start(bf16[128,768]{1,0:T(8,128)(2,1)S(1)} %get-tuple-element.156) | copy-start | bytes 589828
  462.4 34.6 %copy-start.30 = (bf16[128,768]{1,0:T(8,128)(2,1)}, bf16[128,768]{1,0:T(8,128)(2,1)S(1)}, u32[]{:S(2)}) copy-start(bf16[128,768]{1,0:T(8,128)(2,1)S(1)} %get-tuple-element.157) | copy-start | bytes 589828
  462.5 34.6 %copy-start.52 = (f32[768]{0:T(1024)S(1)}, f32[768]{0:T(1024)}, u32[]{:S(2)}) copy-start(f32[768]{0:T(1024)} %copy-done.51) | copy-start | bytes 9220
  462.5 34.6 %copy-start.62 = (f32[256]{0:T(256)S(1)}, f32[256]{0:T(256)}, u32[]{:S(2)}) copy-start(f32[256]{0:T(256)} %copy-done.61) | copy-start | bytes 3076
  462.5 34.6 %copy-start.76 = (f32[256]{0:T(256)S(1)}, f32[256]{0:T(256)}, u32[]{:S(2)}) copy-start(f32[256]{0:T(256)} %copy-done.75) | copy-start | bytes 3076
  510.6 112.9 %copy-start.7 = (f32[256,768]{1,0:T(8,128)}, f32[256,768]{1,0:T(8,128)S(1)}, u32[]{:S(2)}) copy-start(f32[256,768]{1,0:T(8,128)S(1)} %get-tuple-element.140) | copy-start | bytes 2359300
  628.4 72.2 %copy-start.28 = (bf16[128,768]{1,0:T(8,128)(2,1)S(1)}, bf16[128,768]{1,0:T(8,128)(2,1)}, u32[]{:S(2)}) copy-start(bf16[128,768]{1,0:T(8,128)(2,1)} %copy-done.27) | copy-start | bytes 589828
  628.4 72.2 %copy-start.31 = (bf16[128,768]{1,0:T(8,128)(2,1)S(1)}, bf16[128,768]{1,0:T(8,128)(2,1)}, u32[]{:S(2)}) copy-start(bf16[128,768]{1,0:T(8,128)(2,1)} %copy-done.30) | copy-start | bytes 589828
  628.4 74.2 %copy-start = (f32[256,1536]{1,0:T(8,128)S(1)}, f32[256,1536]{1,0:T(8,128)}, u32[]{:S(2)}) copy-start(f32[256,1536]{1,0:T(8,128)} %reduce_rows.2) | copy-start | bytes 4718596
  628.4 78.0 %copy-start.68 = (f32[768]{0:T(1024)S(1)}, f32[768]{0:T(1024)}, u32[]{:S(2)}) copy-start(f32[768]{0:T(1024)} %get-tuple-element.141) | copy-start | bytes 9220
  628.4 78.1 %copy-start.67 = (f32[768]{0:T(1024)S(1)}, f32[768]{0:T(1024)}, u32[]{:S(2)}) copy-start(f32[768]{0:T(1024)} %get-tuple-element.110) | copy-start | bytes 9220
  628.4 80.8 %copy-start.12 = (f32[256,768]{1,0:T(8,128)S(1)}, f32[256,768]{1,0:T(8,128)}, u32[]{:S(2)}) copy-start(f32[256,768]{1,0:T(8,128)} %copy-done.11) | copy-start | bytes 2359300
  722.9 73.9 %copy-start.54 = (f32[8,128]{1,0:T(8,128)S(1)}, f32[8,128]{1,0:T(8,128)}, u32[]{:S(2)}) copy-start(f32[8,128]{1,0:T(8,128)} %get-tuple-element.75) | copy-start | bytes 12292
  722.9 78.0 %copy-start.46 = (f32[96,768]{1,0:T(8,128)S(1)}, f32[96,768]{1,0:T(8,128)}, u32[]{:S(2)}) copy-start(f32[96,768]{1,0:T(8,128)} %get-tuple-element.73) | copy-start | bytes 884740
  722.9 79.8 %copy-start.45 = (f32[24,3072]{1,0:T(8,128)S(1)}, f32[24,3072]{1,0:T(8,128)}, u32[]{:S(2)}) copy-start(f32[24,3072]{1,0:T(8,128)} %get-tuple-element.71) | copy-start | bytes 884740
  722.9 81.6 %copy-start.48 = (f32[24,768]{1,0:T(8,128)S(1)}, f32[24,768]{1,0:T(8,128)}, u32[]{:S(2)}) copy-start(f32[24,768]{1,0:T(8,128)} %get-tuple-element.69) | copy-start | bytes 221188
  722.9 83.1 %copy-start.47 = (f32[24,2304]{1,0:T(8,128)S(1)}, f32[24,2304]{1,0:T(8,128)}, u32[]{:S(2)}) copy-start(f32[24,2304]{1,0:T(8,128)} %get-tuple-element.67) | copy-start | bytes 663556
  (56 other events, 283.6 us)

commit v2 on v1

--- a/solution.py
+++ b/solution.py
@@ -21,15 +21,20 @@
     return ((p["y"] * 2 + p["x"]) * 2 + p["c"], p["z"])
 
 
-def moved(p, axis, d):
-    p = dict(p)
-    if d:
-        p[axis] = p[axis] + d if axis == "z" else 1 - p[axis]
-    return p
-
-
-def holds(p, depth):
-    return (p["z"] >= 0) & (p["z"] < depth)
+def flipped(p, axis):
+    return {**p, axis: 1 - p[axis]}
+
+
+def at_depth(p, z):
+    return {**p, "z": z}
+
+
+def number_in(depth):
+    return lambda p: device_of(p)[0] * depth + p["z"]
+
+
+def number_in_sequence(p):
+    return device_of(p)[0]
 
 
 def when(cond, action):
@@ -39,55 +44,48 @@
         pl.when(cond)(action)
 
 
-def both(one, other):
-    return other if one is None else one if other is None else one & other
+def ranked(z, rank, depth):
+    near = [sorted(range(depth), key=lambda q: (abs(q - k), q))[rank] for k in range(depth)]
+    return sum(jnp.where(z == k, near[k], 0) for k in range(depth))
 
 
 def offsets(order, depth):
-    return list(
-        itertools.product(*[range(1 - depth, depth) if a == "z" else (0, 1) for a in order])
-    )
+    return list(itertools.product(*[range(depth if a == "z" else 2) for a in order]))
+
+
+def target_of(order, offset, depth, me):
+    p = me
+    for axis, d in zip(order, offset):
+        if d:
+            p = at_depth(p, ranked(me["z"], d, depth)) if axis == "z" else flipped(p, axis)
+    return p
 
 
 def last_move(offset):
     return max([-1] + [i for i, d in enumerate(offset) if d])
-
-
-def onward(order, offset):
-    last = last_move(offset)
-    moves = []
-    if last >= 0 and order[last] == "z":
-        moves.append(("on", "z", -1 if offset[last] > 0 else 1))
-    for axis in order[last + 1 :]:
-        moves += [("start", axis, d) for d in ((1, -1) if axis == "z" else (1,))]
-    moves.append(("core", "c", 1))
-    return moves
 
 
 def greet(axes, depth, from_first=0):
     me = place()
     barrier = pltpu.get_barrier_semaphore()
+
+    def signal(device):
+        pl.semaphore_signal(barrier, inc=1, device_id=device, device_id_type=MESH)
+
     count = 0
     for axis in axes + ("c",):
-        for d in (1, -1) if axis == "z" else (1,):
-            peer = moved(me, axis, d)
-            cond = holds(peer, depth) if axis == "z" else None
-            when(
-                cond,
-                lambda peer=peer: pl.semaphore_signal(
-                    barrier, inc=1, device_id=device_of(peer), device_id_type=MESH
-                ),
-            )
-            count = count + (1 if cond is None else cond.astype(jnp.int32))
+        if axis == "z":
+            for step in (1, -1):
+                peer = at_depth(me, me["z"] + step)
+                cond = (peer["z"] >= 0) & (peer["z"] < depth)
+                when(cond, lambda peer=peer: signal(device_of(peer)))
+                count = count + cond.astype(jnp.int32)
+        else:
+            signal(device_of(flipped(me, axis)))
+            count = count + 1
     if from_first:
         seq = lax.axis_index("seq")
-
-        @pl.when(seq != 0)
-        def _():
-            pl.semaphore_signal(
-                barrier, inc=1, device_id=(0, lax.axis_index("batch")), device_id_type=MESH
-            )
-
+        when(seq != 0, lambda: signal((0, lax.axis_index("batch"))))
         count = count + jnp.where(seq == 0, from_first, 0)
     pl.semaphore_wait(barrier, count)
 
@@ -102,61 +100,60 @@
 
     @staticmethod
     def sends(order, depth):
-        return sum(len(onward(order, t)) for t in offsets(order, depth))
-
-    def origin(self, offset):
-        p = self.me
-        for axis, d in zip(self.order, offset):
-            p = moved(p, axis, d)
-        cond = None
-        if "z" in self.order and offset[self.order.index("z")]:
-            cond = holds(p, self.depth)
-        return p, cond
+        return sum(len(order) + 2 - last_move(t) for t in offsets(order, depth))
+
+    def onward(self, offset):
+        last = last_move(offset)
+        z = self.me["z"]
+        moves = []
+        if last >= 0 and self.order[last] == "z":
+            source = ranked(z, offset[last], self.depth)
+            peer = jnp.where(source < z, z + 1, z - 1)
+            moves.append((at_depth(self.me, peer), (peer >= 0) & (peer < self.depth)))
+        for axis in self.order[last + 1 :]:
+            if axis == "z":
+                moves.append((at_depth(self.me, z + 1), z + 1 < self.depth))
+                moves.append((at_depth(self.me, z - 1), z > 0))
+            else:
+                moves.append((flipped(self.me, axis), None))
+        moves.append((flipped(self.me, "c"), None))
+        return moves
 
     def arrival(self, p):
         ref = self.target(p)
         return pltpu.make_async_remote_copy(
-            src_ref=ref, dst_ref=ref, send_sem=self.send.at[self.send_at],
-            recv_sem=self.recv.at[self.number(p)], device_id=device_of(self.me), device_id_type=MESH,
+            src_ref=ref, dst_ref=ref, send_sem=self.send.at[0], recv_sem=self.recv.at[self.number(p)],
+            device_id=device_of(self.me), device_id_type=MESH,
         )
 
     def handle(self, offset):
-        p, cond = self.origin(offset)
+        p = target_of(self.order, offset, self.depth, self.me)
         own = not any(offset)
-        plans = []
-        for kind, axis, d in onward(self.order, offset):
-            peer = moved(self.me, axis, d)
-            also = holds(peer, self.depth) if axis == "z" else None
-            plans.append((peer, also, self.send_at))
+        if not own:
+            self.arrival(p).wait_recv()
+        for peer, cond in self.onward(offset):
+            copy = pltpu.make_async_remote_copy(
+                src_ref=self.source if own else self.target(p), dst_ref=self.target(p),
+                send_sem=self.send.at[self.send_at], recv_sem=self.recv.at[self.number(p)],
+                device_id=device_of(peer), device_id_type=MESH,
+            )
+            when(cond, copy.start)
+            self.sent.append((cond, self.send_at))
             self.send_at += 1
 
-        def act():
-            if not own:
-                self.arrival(p).wait_recv()
-            for peer, also, slot in plans:
-                copy = pltpu.make_async_remote_copy(
-                    src_ref=self.source if own else self.target(p), dst_ref=self.target(p),
-                    send_sem=self.send.at[slot], recv_sem=self.recv.at[self.number(p)],
-                    device_id=device_of(peer), device_id_type=MESH,
-                )
-                when(also, copy.start)
-
-        when(cond, act)
-        for peer, also, slot in plans:
-            self.sent.append((both(cond, also), slot))
+    def begin(self):
+        self.handle((0,) * len(self.order))
 
     def events(self):
-        marks = sorted(
-            (t for t in offsets(self.order, self.depth) if any(t)),
-            key=lambda t: (sum(abs(d) for d in t), t),
-        )
-        return [(sum(abs(d) for d in t), partial(self.handle, t)) for t in marks]
+        return [
+            (sum(t), partial(self.handle, t))
+            for t in sorted(offsets(self.order, self.depth), key=lambda t: (sum(t), t))
+            if any(t)
+        ]
 
     def siblings(self):
         for t in offsets(self.order, self.depth):
-            p, cond = self.origin(t)
-            p = moved(p, "c", 1)
-            when(cond, lambda p=p: self.arrival(p).wait_recv())
+            self.arrival(flipped(target_of(self.order, t, self.depth, self.me), "c")).wait_recv()
 
     def drain(self):
         for cond, slot in self.sent:
@@ -167,14 +164,14 @@
             when(cond, copy.wait_send)
 
 
-def run_gathers(jobs):
-    for job in jobs:
-        job.handle((0,) * len(job.order))
-    todo = []
-    for i, job in enumerate(jobs):
-        todo += [(when_, i, k, act) for k, (when_, act) in enumerate(job.events())]
-    for _, _, _, act in sorted(todo, key=lambda e: e[:3]):
-        act()
+def gather_events(jobs):
+    todo = [
+        (when_, i, k, act) for i, job in enumerate(jobs) for k, (when_, act) in enumerate(job.events())
+    ]
+    return [act for _, _, _, act in sorted(todo, key=lambda e: e[:3])]
+
+
+def end_gathers(jobs):
     for job in jobs:
         job.siblings()
     for job in jobs:
@@ -182,29 +179,47 @@
 
 
 class Reduce:
-    def __init__(self, partial_of, inbox, number, order, depth, send, recv):
-        self.partial_of, self.inbox, self.number = partial_of, inbox, number
+    def __init__(self, partial_of, inbox, order, depth, send, recv):
+        self.partial_of, self.inbox = partial_of, inbox
         self.order, self.depth, self.send, self.recv = order, depth, send, recv
         self.me = place()
-        self.edges = self.edge_table(order, depth)
+        self.base, _ = self.slots(order, depth)
+        self.marks = sorted(offsets(order, depth), key=lambda t: (-sum(t), t))
         self.sent = []
 
     @staticmethod
-    def edge_table(order, depth):
-        table = {}
+    def split(order, offset):
+        if "z" not in order:
+            return offset, 0
+        i = order.index("z")
+        return offset[:i] + (0,) + offset[i + 1 :], offset[i]
+
+    @staticmethod
+    def slots(order, depth):
+        base, count = {}, 0
+        deep = depth if "z" in order else 1
         for t in offsets(order, depth):
-            for move in onward(order, t):
-                table[(t, move)] = len(table)
-        return table
-
-    def owner(self, offset):
-        p = self.me
-        for axis, d in zip(self.order, offset):
-            p = moved(p, axis, d)
-        cond = None
-        if "z" in self.order and offset[self.order.index("z")]:
-            cond = holds(p, self.depth)
-        return p, cond
+            key, rank = Reduce.split(order, t)
+            if rank:
+                continue
+            last = last_move(key)
+            for i, axis in enumerate(order):
+                if i <= last:
+                    continue
+                base[(key, axis)] = count
+                if axis == "z":
+                    count += deep + 1
+                elif "z" in order and i > order.index("z"):
+                    count += deep
+                else:
+                    count += 1
+            base[(key, "c")] = count
+            count += deep
+        return base, count
+
+    def where_(self, key, axis, z):
+        deep = "z" in self.order and (axis == "c" or self.order.index(axis) > self.order.index("z"))
+        return self.base[(key, axis)] + (z if deep else 0)
 
     def copy(self, source, edge, slot, peer):
         return pltpu.make_async_remote_copy(
@@ -212,65 +227,60 @@
             recv_sem=self.recv.at[edge], device_id=device_of(peer), device_id_type=MESH,
         )
 
-    def slots(self):
-        return {t: i for i, t in enumerate(offsets(self.order, self.depth))}
-
     def start(self, offset):
-        p, cond = self.owner(offset)
-        q = moved(p, "c", 1)
-        slot = self.slots()[offset]
-        edge = self.edges[(offset, ("core", "c", 1))]
-        when(cond, lambda: self.copy(self.partial_of(q), edge, slot, moved(self.me, "c", 1)).start())
-        self.sent.append((cond, slot))
-
-    def children(self, offset):
-        found = []
-        for kind, axis, d in onward(self.order, offset):
-            cond = None
+        p = target_of(self.order, offset, self.depth, self.me)
+        key, _ = self.split(self.order, offset)
+        slot = self.marks.index(offset)
+        edge = self.where_(key, "c", p["z"])
+        peer = flipped(self.me, "c")
+        self.copy(self.partial_of(flipped(p, "c")), edge, slot, peer).start()
+        self.sent.append(slot)
+
+    def kids(self, offset, p):
+        key, rank = self.split(self.order, offset)
+        last, z = last_move(offset), self.me["z"]
+        found = [(self.where_(key, "c", p["z"]), None)]
+        for axis in self.order[last + 1 :]:
             if axis == "z":
-                cond = holds(moved(self.me, "z", d), self.depth)
-            found.append((self.edges[(offset, (kind, axis, d))], cond, kind))
+                at = self.base[(key, "z")]
+                found += [(at + z, z > 0), (at + self.depth, z + 1 < self.depth)]
+            else:
+                found.append((self.where_(key, axis, p["z"]), None))
+        if last >= 0 and self.order[last] == "z":
+            far = jnp.where(p["z"] < z, z + 1, z - 1)
+            found.append((self.base[(key, "z")] + p["z"], (far >= 0) & (far < self.depth)))
         return found
 
-    def upward(self, offset):
-        k = last_move(offset)
-        axis, d = self.order[k], offset[k]
-        step = 1 if d > 0 else -1
-        parent = list(offset)
-        parent[k] = d - step if axis == "z" else 0
-        if axis == "z" and parent[k]:
-            kind, back = "on", -step
+    def upward(self, offset, p):
+        key, rank = self.split(self.order, offset)
+        k, z = last_move(offset), self.me["z"]
+        axis = self.order[k]
+        if axis == "z":
+            edge = self.base[(key, "z")] + jnp.where(p["z"] == z - 1, self.depth, p["z"])
+            return edge, at_depth(self.me, jnp.where(p["z"] < z, z - 1, z + 1))
+        parent = key[:k] + (0,) + key[k + 1 :]
+        return self.where_(parent, axis, p["z"]), flipped(self.me, axis)
+
+    def handle(self, offset, add, finish):
+        p = target_of(self.order, offset, self.depth, self.me)
+        kids = self.kids(offset, p)
+        slot = len(self.marks) + self.marks.index(offset)
+        for edge, cond in kids:
+            when(cond, self.copy(self.inbox.at[edge], edge, slot, self.me).wait_recv)
+        parts = [(self.inbox.at[edge], cond) for edge, cond in kids]
+        if any(offset):
+            into = parts[0][0]
+            add(self.partial_of(p), parts, into)
+            edge, peer = self.upward(offset, p)
+            self.copy(into, edge, slot, peer).start()
+            self.sent.append(slot)
         else:
-            kind, back = "start", -step if axis == "z" else 1
-        edge = self.edges[(tuple(parent), (kind, axis, back))]
-        return edge, moved(self.me, axis, step)
-
-    def handle(self, offset, add, finish):
-        p, cond = self.owner(offset)
-        kids = self.children(offset)
-        core = [e for e, c, kind in kids if kind == "core"][0]
-        slot = len(self.slots()) + self.slots()[offset]
-
-        def act():
-            for edge, also, _ in kids:
-                when(also, lambda edge=edge: self.copy(self.inbox.at[edge], edge, slot, self.me).wait_recv())
-            if any(offset):
-                add(self.partial_of(p), [(self.inbox.at[e], c) for e, c, _ in kids], self.inbox.at[core])
-                edge, peer = self.upward(offset)
-                self.copy(self.inbox.at[core], edge, slot, peer).start()
-            else:
-                finish(self.partial_of(p), [(self.inbox.at[e], c) for e, c, _ in kids])
-
-        when(cond, act)
-        if any(offset):
-            self.sent.append((cond, slot))
-
-    def marks(self):
-        return sorted(offsets(self.order, self.depth), key=lambda t: (-sum(abs(d) for d in t), t))
+            finish(self.partial_of(p), parts)
 
     def drain(self):
-        for cond, slot in self.sent:
-            when(cond, self.copy(self.inbox.at[0], 0, slot, self.me).wait_send)
+        for slot in self.sent:
+            self.copy(self.inbox.at[0], 0, slot, self.me).wait_send()
+
 
 D = 768
 H = 12
@@ -295,67 +305,77 @@
 IN_VMEM = pl.BlockSpec(memory_space=pltpu.VMEM)
 
 
-def number_in(depth):
-    return lambda p: device_of(p)[0] * depth + p["z"]
-
-
 def dma(*shape):
     return pltpu.SemaphoreType.DMA(shape)
 
 
-def gather_weights_kernel(depth, orders, *refs):
-    n = len(orders)
+def gather_pieces(pieces, sources, targets, depth, send, recv, at=0):
+    jobs = []
+    for i, (which, first, rows, order) in enumerate(pieces):
+        rows = pl.ds(first, rows)
+        number = number_in(depth) if "z" in order else number_in_sequence
+        jobs.append(
+            Gather(
+                sources[which].at[rows],
+                lambda p, which=which, rows=rows, number=number: targets[which].at[number(p), rows],
+                number, order, depth, send, recv.at[i], at,
+            )
+        )
+        at += Gather.sends(order, depth)
+    return jobs
+
+
+def own_copies(pieces, sources, targets, depth, local):
+    me = place()
+    numbers = {which: (number_in(depth) if "z" in order else number_in_sequence) for which, _, _, order in pieces}
+    return [
+        pltpu.make_async_copy(sources[which], targets[which].at[number(me)], local.at[which])
+        for which, number in numbers.items()
+    ]
+
+
+def gather_weights_kernel(depth, pieces, n, *refs):
     sources, targets = refs[:n], refs[n : 2 * n]
     send, recv, local = refs[2 * n :]
     greet(("y", "x", "z"), depth)
-    me = place()
-    number = number_in(depth)
-    jobs, own, at = [], [], 0
-    for i, order in enumerate(orders):
-        copy = pltpu.make_async_copy(sources[i], targets[i].at[number(me)], local.at[i])
+    own = own_copies(pieces, sources, targets, depth, local)
+    jobs = gather_pieces(pieces, sources, targets, depth, send, recv)
+    for job in jobs:
+        job.begin()
+    for copy in own:
         copy.start()
-        own.append(copy)
-        jobs.append(
-            Gather(
-                sources[i], lambda p, i=i: targets[i].at[number(p)], number, order, depth,
-                send, recv.at[i], at,
-            )
-        )
-        at += Gather.sends(order, depth)
-    run_gathers(jobs)
+    for act in gather_events(jobs):
+        act()
+    end_gathers(jobs)
     for copy in own:
         copy.wait()
 
 
-def gather_weights(arrays, orders, depth, n_dev, cid):
-    total = sum(Gather.sends(order, depth) for order in orders)
+def gather_weights(arrays, pieces, depth, n_dev, cid):
     n = len(arrays)
+    seq_only = {which for which, _, _, order in pieces if "z" not in order}
+    counts = [n_dev // depth if i in seq_only else n_dev for i in range(n)]
+    total = sum(Gather.sends(order, depth) for _, _, _, order in pieces)
     return pl.pallas_call(
-        partial(gather_weights_kernel, depth, orders),
-        out_shape=[jax.ShapeDtypeStruct((n_dev,) + a.shape, a.dtype) for a in arrays],
+        partial(gather_weights_kernel, depth, pieces, n),
+        out_shape=[jax.ShapeDtypeStruct((k,) + a.shape, a.dtype) for k, a in zip(counts, arrays)],
         in_specs=[ANYWHERE] * n,
         out_specs=[ANYWHERE] * n,
-        scratch_shapes=[dma(total), dma(n, n_dev), dma(n)],
+        scratch_shapes=[dma(total), dma(len(pieces), n_dev), dma(n)],
         compiler_params=pltpu.CompilerParams(collective_id=cid, has_side_effects=True),
         name="gather_weights",
     )(*arrays)
 
 
-def fetch_layer(layer, w_qkv, w_out, w_up, w_down, seq_count, depth):
-    if seq_count != 8:
-        gathered = [
-            lax.all_gather(w[layer], ("seq", "batch"), axis=0, tiled=True)
-            for w in (w_qkv, w_out, w_up, w_down)
-        ]
-        return tuple(gathered)
-    n_dev = seq_count * depth
-    rows = w_down.shape[1] * 2 // 3
-    got = gather_weights(
-        [w_qkv[layer], w_out[layer], w_up[layer], w_down[layer]],
-        [Z_Y_X, Z_X_Y, Z_X_Y, X_Y_Z],
-        depth, n_dev, layer,
-    )
-    return tuple(g.reshape(-1, g.shape[-1]) for g in got)
+def weight_pieces(rows_in, rows_down):
+    two_thirds = rows_down * 2 // 3
+    return [
+        (0, 0, rows_in, Z_Y_X),
+        (1, 0, rows_in, Z_X_Y),
+        (2, 0, rows_in, Z_X_Y),
+        (3, 0, two_thirds, X_Y_Z),
+        (3, two_thirds, rows_down - two_thirds, Z_Y_X),
+    ]
 
 
 def to_helpers(depth, source, target, send, recv):
@@ -457,7 +477,11 @@
             )
         )
         at += Gather.sends(order, depth)
-    run_gathers(jobs)
+    for job in jobs:
+        job.begin()
+    for act in gather_events(jobs):
+        act()
+    end_gathers(jobs)
     own.wait()
     end()
 
@@ -579,7 +603,7 @@
 
 
 def run_reduces(jobs):
-    marks = [(k, i, t) for i, (job, _) in enumerate(jobs) for k, t in enumerate(job.marks())]
+    marks = [(k, i, t) for i, (job, _) in enumerate(jobs) for k, t in enumerate(job.marks)]
     marks.sort()
     for _, i, t in marks:
         jobs[i][0].start(t)
@@ -602,7 +626,7 @@
             (
                 Reduce(
                     lambda p, source=source, window=window: source.at[number_in_sequence(p), window],
-                    inboxes[i], number_in_sequence, order, depth, send.at[i], recv.at[i],
+                    inboxes[i], order, depth, send.at[i], recv.at[i],
                 ),
                 out_ref.at[window, pl.ds(i % 2 * half, half)],
             )
@@ -615,7 +639,7 @@
         both_parts = jnp.concatenate([dk, dv], axis=1).astype(jnp.float32)
         return lax.psum_scatter(both_parts, "seq", scatter_dimension=0, tiled=True)
     rows = dk.shape[0] // seq_count
-    edges = len(Reduce.edge_table(Y_X, depth))
+    _, edges = Reduce.slots(Y_X, depth)
     slots = 2 * len(offsets(Y_X, depth))
     return pl.pallas_call(
         partial(reduce_rows_kernel, depth),
@@ -631,36 +655,40 @@
     )(dk.reshape(seq_count, rows, D), dv.reshape(seq_count, rows, D))
 
 
-def reduce_weights_kernel(depth, orders, *refs):
-    n = len(orders)
-    sources, targets, inboxes = refs[:n], refs[n : 2 * n], refs[2 * n : 3 * n]
-    send, recv = refs[3 * n : 4 * n], refs[4 * n :]
+def reduce_weights_kernel(depth, pieces, n, *refs):
+    m = len(pieces)
+    sources, targets, inboxes = refs[:n], refs[n : 2 * n], refs[2 * n : 2 * n + m]
+    send, recv = refs[2 * n + m : 2 * n + 2 * m], refs[2 * n + 2 * m :]
     greet(("y", "x", "z"), depth)
     number = number_in(depth)
-    run_reduces(
-        [
+    jobs = []
+    for i, (which, first, rows, order) in enumerate(pieces):
+        rows = pl.ds(first, rows)
+        jobs.append(
             (
                 Reduce(
-                    lambda p, i=i: sources[i].at[number(p)], inboxes[i], number, orders[i], depth,
-                    send[i], recv[i],
+                    lambda p, which=which, rows=rows: sources[which].at[number(p), rows],
+                    inboxes[i], order, depth, send[i], recv[i],
                 ),
-                targets[i],
+                targets[which].at[rows],
             )
-            for i in range(n)
-        ]
-    )
-
-
-def reduce_weights(parts, orders, depth, cid):
+        )
+    run_reduces(jobs)
+
+
+def reduce_weights(parts, pieces, depth, cid):
     n = len(parts)
-    edges = [len(Reduce.edge_table(order, depth)) for order in orders]
-    slots = [2 * len(offsets(order, depth)) for order in orders]
+    edges = [Reduce.slots(order, depth)[1] for _, _, _, order in pieces]
+    slots = [2 * len(offsets(order, depth)) for _, _, _, order in pieces]
     return pl.pallas_call(
-        partial(reduce_weights_kernel, depth, orders),
+        partial(reduce_weights_kernel, depth, pieces, n),
         out_shape=[jax.ShapeDtypeStruct(a.shape[1:], jnp.float32) for a in parts],
         in_specs=[IN_VMEM] * n,
         out_specs=[IN_VMEM] * n,
-        scratch_shapes=[pltpu.VMEM((e,) + a.shape[1:], a.dtype) for e, a in zip(edges, parts)]
+        scratch_shapes=[
+            pltpu.VMEM((e, rows, parts[which].shape[2]), parts[which].dtype)
+            for e, (which, _, rows, _) in zip(edges, pieces)
+        ]
         + [dma(s) for s in slots]
         + [dma(e) for e in edges],
         compiler_params=pltpu.CompilerParams(
@@ -679,7 +707,8 @@
             for a in matrices
         ] + [lax.psum_scatter(small, ("seq", "batch"), scatter_dimension=0, tiled=True)[0]]
     cut = [a.astype(jnp.bfloat16).reshape(n_dev, -1, a.shape[-1]) for a in parts[:4]] + [parts[4]]
-    return reduce_weights(cut, [Z_Y_X, Z_X_Y, Z_X_Y, X_Y_Z, Z_Y_X], depth, cid)
+    pieces = weight_pieces(cut[0].shape[1], cut[3].shape[1]) + [(4, 0, 8, Z_Y_X)]
+    return reduce_weights(cut, pieces, depth, cid)
 
 
 def product(a, b):
@@ -911,13 +940,34 @@
 
     piece = D // n_dev
     small = jnp.concatenate(
-        [biases.reshape(L, -1), gains.reshape(L, -1), up_bias], axis=1
+        [biases.reshape(-1, piece), gains.reshape(-1, piece), up_bias.reshape(-1, piece)], axis=0
+    ).T
+    pieces = weight_pieces(w_qkv.shape[1], w_down.shape[1])
+    arrays = [[w[layer] for w in (w_qkv, w_out, w_up, w_down)] for layer in range(L)]
+    if seq_count == 8:
+        small = jnp.pad(small, ((0, 0), (0, 128 - small.shape[1])))
+        segs = jnp.pad(segments.reshape(-1, 128), ((0, 8 - rows // 128), (0, 0)))
+        more = [(4, 0, piece, Z_Y_X), (5, 0, 8, Y_X)]
+        *first_layer, small, segs_all = gather_weights(
+            arrays[0] + [small, segs], more + pieces, depth, n_dev, 0
+        )
+        weights = [first_layer, gather_weights(arrays[1], pieces, depth, n_dev, 1)]
+        weights = [[w.reshape(-1, w.shape[-1]) for w in held] for held in weights]
+        segs_all = segs_all[:, : rows // 128].reshape(-1)
+        small = small.reshape(D, 128)
+    else:
+        small = lax.all_gather(small, ("seq", "batch"), axis=0, tiled=True)
+        segs_all = lax.all_gather(segments[0], "seq", axis=0, tiled=True)
+        weights = [
+            [lax.all_gather(w, ("seq", "batch"), axis=0, tiled=True) for w in held] for held in arrays
+        ]
+    small = small.astype(jnp.float32).T
+    vectors = jnp.concatenate(
+        [small[: 6 * L].reshape(L, 6, D), small[6 * L : 8 * L].reshape(L, 2, D)], axis=1
     )
-    small = lax.all_gather(small, ("seq", "batch"), axis=0).astype(jnp.float32)
-    vectors = jnp.moveaxis(small[:, :, : 8 * piece].reshape(n_dev, L, 8, piece), 0, 2).reshape(L, 8, D)
-    hidden_shifts = jnp.moveaxis(small[:, :, 8 * piece :], 0, 1).reshape(L, -1)
-
-    segs_all = lax.all_gather(segments[0], "seq", axis=0, tiled=True)
+    hidden_shifts = small[8 * L : 12 * L].reshape(L, 4, n_dev, piece)
+    hidden_shifts = jnp.swapaxes(hidden_shifts, 1, 2).reshape(L, -1)
+
     padding = jnp.full((BLK,), -1, jnp.int32)
     segs_all = jnp.concatenate([padding, segs_all, padding]).reshape(-1, BLK)
     segs_near = lax.dynamic_slice_in_dim(segs_all, first[0], blocks_here + 2, axis=0)
@@ -927,9 +977,6 @@
     allowed = inside[:, None, :] & (seg_window[:, None, :] == segments.reshape(blocks_here, BLK)[:, :, None])
     shut = jnp.pad(jnp.where(allowed, 0.0, masked_score), ((0, 0), (0, 0), (0, BLK)))
 
-    weights = [
-        fetch_layer(layer, w_qkv, w_out, w_up, w_down, seq_count, depth) for layer in range(L)
-    ]
     resid = layer_input[0].astype(jnp.float32)
     low = layer_input[0]
     saved = []

time: 821 us -> 723 us (0.88)
  blocking collectives: 77.7 us -> 0 us
    all_gather x2 -> x0, blocking collectives: 77.7 us -> none  [the longest x1 70 us: on_device(): small = lax.all_gather(small, ('seq', 'batch'), axis=0).astype(jnp.float32)]
where the time goes in v2:
time: 723 us; the launch traced here: 715 us
  Pallas kernels  547 us (76%)
  matrix products  89.6 us (12%)
  local copies, waits for them, and re-layouts  38.5 us (5%)
  other arithmetic  36.9 us (5%)
    pallas_call x2, Pallas kernels, gather_weights(): pl.pallas_call(partial(gather_weights_kernel, depth, pieces, n), out_shap...  132 us
    pallas_call x2, Pallas kernels, reduce_weights(): pl.pallas_call(partial(reduce_weights_kernel, depth, pieces, n), out_shap...  130 us
    pallas_call x2, Pallas kernels, attend_back(): pl.pallas_call(attend_back_kernel, grid_spec=pltpu.PrefetchScalarGridSpec...  76.7 us
    pallas_call x2, Pallas kernels, gather_rows(): pl.pallas_call(partial(gather_rows_kernel, depth), out_shape=[jax.ShapeDt...  66.6 us
    pallas_call x2, Pallas kernels, reduce_rows(): pl.pallas_call(partial(reduce_rows_kernel, depth), out_shape=jax.ShapeDty...  66 us
    pallas_call x2, Pallas kernels, attend(): pl.pallas_call(attend_kernel, grid_spec=pltpu.PrefetchScalarGridSpec(num_...  46.7 us
    dot_general x8, matrix products, dot32(): return jnp.dot(a, b, preferred_element_type=jnp.float32)  38.7 us
    dot_general x8, matrix products, product_tn(): lax.dot_general(a, b, (((0,), (0,)), ((), ())), preferred_element_type=jn...  27.1 us

profile of v2, /device:TPU:0, one launch (start us, length us, event | category | flops | bytes accessed | tf_op | source)
XLA Modules:
  0.0 714.6 jit_solution(17556919405566249532)
XLA Ops:
  11.5 70.1 %gather_weights.2 = (bf16[32,24,2304]{2,1,0:T(8,128)(2,1)}, bf16[32,24,768]{2,1,0:T(8,128)(2,1)}, bf16[32,24,3072]{2,1,0:T(8,128)(2,1)}, bf16[32,96,768]{2,1,0:T...) custom-call(bf16[24,2304]{1,0:T(8,128)(2,1)} %get-tuple-element.159.refs_0_, ...), custom_call_target="tpu_custom_call" | custom-call | tf_op jit(solution)/shard_map/gather_weights/pallas_call | solution.py:359
  83.5 3.1 convolution_bitcast_fusion
  88.5 33.3 %gather_rows.2 = (bf16[8,256,1536]{2,1,0:T(8,128)(2,1)}, bf16[16,768]{1,0:T(8,128)(2,1)}) custom-call(bf16[256,1536]{1,0:T(8,128)(2,1)} %pad_maximum_fusion.2.kv_ref, bf16[256,768]{1,0:T(8,128)(2,1)} %get-tuple-element.145.q_ref), custom_call_target="tpu_custom_call" | custom-call | tf_op jit(solution)/shard_map/gather_rows/pallas_call | solution.py:495
  125.8 23.4 %attend.2 = (bf16[256,768]{1,0:T(8,128)(2,1)}, bf16[16,768]{1,0:T(8,128)(2,1)}) custom-call(s32[144]{0:T(256)} %reshape.316.picks_ref, s32[1]{0:T(128)} %bitcast.1.first_ref, bf16[256,768]{1,0:T(8,128)(2,1)} %get-tuple-element.145.q_ref, bf16[2048,1536]{1,0:T(8,128)(2,1)} %bitcast.136, bf16[2048,1536]{1,0:T(8,128)(2,1)} %bitcast.137, ...), custom_call_target="tpu_custom_call" | custom-call | tf_op jit(solution)/shard_map/attend/pallas_call | solution.py:802
  149.2 5.3 collect.4
  157.0 11.4 %multiply_convert_fusion.1 = (bf16[256,3072]{1,0:T(8,128)(2,1)S(1)}, f32[256,3072]{1,0:T(8,128)}, f32[256,3072]{1,0:T(8,128)}) fusion(f32[3072]{0:T(1024)S(1)} %add.258, bf16[768,3072]{1,0:T(8,128)(2,1)} %bitcast.203, f32[256,768]{1,0:T(8,128)S(1)} %get-tuple-element.169, f32[768]{0:T(1024)S(1)} %get-tuple-element.122, f32[768]{0:T(1024)S(1)} %get-tuple-element.189, ...), kind=kOutput, calls=%fused_computation.28 | convolution fusion | flops 1260847104 | bytes 13389824 | tf_op jit(solution)/shard_map/dot_general | solution.py:927
  168.4 4.4 fusion.82
  173.1 62.3 %gather_weights.3 = (bf16[32,24,2304]{2,1,0:T(8,128)(2,1)}, bf16[32,24,768]{2,1,0:T(8,128)(2,1)}, bf16[32,24,3072]{2,1,0:T(8,128)(2,1)}, bf16[32,96,768]{2,1,0:T(8,128)(2,1)}) custom-call(bf16[24,2304]{1,0:T(8,128)(2,1)} %get-tuple-element.160.refs_0_, bf16[24,768]{1,0:T(8,128)(2,1)} %get-tuple-element.164.refs_1_, ...), custom_call_target="tpu_custom_call" | custom-call | tf_op jit(solution)/shard_map/gather_weights/pallas_call | solution.py:359
  235.4 3.2 fusion.68
  240.4 33.3 %gather_rows.3 = (bf16[8,256,1536]{2,1,0:T(8,128)(2,1)}, bf16[16,768]{1,0:T(8,128)(2,1)}) custom-call(bf16[256,1536]{1,0:T(8,128)(2,1)} %pad_maximum_fusion.3.kv_ref, bf16[256,768]{1,0:T(8,128)(2,1)} %get-tuple-element.143.q_ref), custom_call_target="tpu_custom_call" | custom-call | tf_op jit(solution)/shard_map/gather_rows/pallas_call | solution.py:495
  273.6 23.3 %attend.3 = (bf16[256,768]{1,0:T(8,128)(2,1)}, bf16[16,768]{1,0:T(8,128)(2,1)}) custom-call(s32[144]{0:T(256)} %reshape.316.picks_ref, s32[1]{0:T(128)} %bitcast.1.first_ref, bf16[256,768]{1,0:T(8,128)(2,1)} %get-tuple-element.143.q_ref, bf16[2048,1536]{1,0:T(8,128)(2,1)} %bitcast.140, bf16[2048,1536]{1,0:T(8,128)(2,1)} %bitcast.141, ...), custom_call_target="tpu_custom_call" | custom-call | tf_op jit(solution)/shard_map/attend/pallas_call | solution.py:802
  296.9 5.5 collect.5
  306.1 9.7 %multiply_convert_fusion = (bf16[256,3072]{1,0:T(8,128)(2,1)S(1)}, f32[256,3072]{1,0:T(8,128)S(1)}, f32[256,3072]{1,0:T(8,128)S(1)}) fusion(f32[3072]{0:T(1024)S(1)} %add.283, bf16[768,3072]{1,0:T(8,128)(2,1)} %bitcast.209, f32[256,768]{1,0:T(8,128)S(1)} %get-tuple-element.174, f32[768]{0:T(1024)S(1)} %get-tuple-element.116, ...), kind=kOutput, calls=%fused_computation.15 | convolution fusion | flops 1260847104 | bytes 13389824 | tf_op jit(solution)/shard_map/dot_general | solution.py:927
  315.9 4.5 fusion.84
  334.8 38.4 %attend_back.2 = (bf16[256,768]{1,0:T(8,128)(2,1)}, bf16[2048,768]{1,0:T(8,128)(2,1)}, bf16[2048,768]{1,0:T(8,128)(2,1)}, bf16[16,768]{1,0:T(8,128)(2,1)}) custom-call(s32[144]{0:T(256)} %reshape.316.picks_ref, s32[1]{0:T(128)} %bitcast.1.first_ref, bf16[256,768]{1,0:T(8,128)(2,1)} %get-tuple-element.143.q_ref, bf16[2048,1536]{1,0:T(8,128)(2,1)} %bitcast.142, ...), custom_call_target="tpu_custom_call" | custom-call | tf_op jit(solution)/shard_map/attend_back/pallas_call | solution.py:885
  373.3 5.3 collect.6
  379.8 33.0 %reduce_rows.2 = f32[256,1536]{1,0:T(8,128)} custom-call(bf16[8,256,768]{2,1,0:T(8,128)(2,1)} %bitcast.158, bf16[8,256,768]{2,1,0:T(8,128)(2,1)} %bitcast.159), custom_call_target="tpu_custom_call" | custom-call | tf_op jit(solution)/shard_map/reduce_rows/pallas_call | solution.py:644
  414.4 4.2 multiply_reduce_fusion.1
  419.5 5.4 fusion.86
  429.5 4.5 spread.3
  435.4 38.3 %attend_back.3 = (bf16[256,768]{1,0:T(8,128)(2,1)}, bf16[2048,768]{1,0:T(8,128)(2,1)}, bf16[2048,768]{1,0:T(8,128)(2,1)}, bf16[16,768]{1,0:T(8,128)(2,1)}) custom-call(s32[144]{0:T(256)} %reshape.316.picks_ref, s32[1]{0:T(128)} %bitcast.1.first_ref, bf16[256,768]{1,0:T(8,128)(2,1)} %get-tuple-element.145.q_ref, bf16[2048,1536]{1,0:T(8,128)(2,1)} %bitcast.138, ...), custom_call_target="tpu_custom_call" | custom-call | tf_op jit(solution)/shard_map/attend_back/pallas_call | solution.py:885
  473.8 5.2 collect.7
  483.0 33.0 %reduce_rows.3 = f32[256,1536]{1,0:T(8,128)} custom-call(bf16[8,256,768]{2,1,0:T(8,128)(2,1)} %bitcast.156, bf16[8,256,768]{2,1,0:T(8,128)(2,1)} %bitcast.157), custom_call_target="tpu_custom_call" | custom-call | tf_op jit(solution)/shard_map/reduce_rows/pallas_call | solution.py:644
  532.2 5.3 convolution_convert_fusion.3
  537.5 3.7 convolution_convert_fusion.4
  543.2 2.9 convolution_convert_fusion.5
  546.1 64.1 %reduce_weights.2 = (f32[24,2304]{1,0:T(8,128)}, f32[24,768]{1,0:T(8,128)}, f32[24,3072]{1,0:T(8,128)}, f32[96,768]{1,0:T(8,128)}, f32[8,128]{1,0:T(8,128)}) custom-call(bf16[32,24,2304]{2,1,0:T(8,128)(2,1)} %bitcast.151, bf16[32,24,768]{2,1,0:T(8,128)(2,1)} %bitcast.149, bf16[32,24,3072]{2,1,0:T(8,128)(2,1)} %bitcast.147, bf16[32,96,768]{2,1,0:T(8,128)(2,1)} %bitcast.145, ...), custom_call_target="tpu_custom_call" | custom-call | tf_op jit(solution)/shard_map/reduce_weights/pallas_call | solution.py:683
  619.0 5.3 convolution_convert_fusion
  624.4 3.7 convolution_convert_fusion.1
  629.7 3.1 convolution_convert_fusion.2
  632.8 66.2 %reduce_weights.3 = (f32[24,2304]{1,0:T(8,128)}, f32[24,768]{1,0:T(8,128)}, f32[24,3072]{1,0:T(8,128)}, f32[96,768]{1,0:T(8,128)}, f32[8,128]{1,0:T(8,128)}) custom-call(bf16[32,24,2304]{2,1,0:T(8,128)(2,1)} %bitcast.150, bf16[32,24,768]{2,1,0:T(8,128)(2,1)} %bitcast.148, bf16[32,24,3072]{2,1,0:T(8,128)(2,1)} %bitcast.146, bf16[32,96,768]{2,1,0:T(8,128)(2,1)} %bitcast.144, ...), custom_call_target="tpu_custom_call" | custom-call | tf_op jit(solution)/shard_map/reduce_weights/pallas_call | solution.py:683
  710.1 4.0 fusion.14
  (310 shorter events, 93.7 us)
Async XLA Ops:
  0.6 82.9 %copy-start.42 = (bf16[1,256,768]{2,1,0:T(8,128)(2,1)S(1)}, bf16[1,256,768]{2,1,0:T(8,128)(2,1)}, u32[]{:S(2)}) copy-start(bf16[1,256,768]{2,1,0:T(8,128)(2,1)} %param.11) | copy-start | bytes 1179652
  83.5 220.2 %copy-start.48 = (f32[768]{0:T(1024)}, f32[768]{0:T(1024)S(1)}, u32[]{:S(2)}) copy-start(f32[768]{0:T(1024)S(1)} %get-tuple-element.190) | copy-start | bytes 9220
  83.5 220.2 %copy-start.62 = (f32[768]{0:T(1024)}, f32[768]{0:T(1024)S(1)}, u32[]{:S(2)}) copy-start(f32[768]{0:T(1024)S(1)} %get-tuple-element.120) | copy-start | bytes 9220
  86.6 36.8 %copy-start.78 = (s32[1,256]{1,0:T(1,128)S(1)}, s32[1,256]{1,0:T(1,128)}, u32[]{:S(2)}) copy-start(s32[1,256]{1,0:T(1,128)} %param.12) | copy-start | bytes 3076
  86.6 38.4 %copy-start.76 = (s32[1,4,12,3]{2,1,3,0:T(4,128)S(1)}, s32[1,4,12,3]{2,1,3,0:T(4,128)}, u32[]{:S(2)}) copy-start(s32[1,4,12,3]{2,1,3,0:T(4,128)} %param.13) | copy-start | bytes 1732
  125.8 30.0 %copy-start.15 = (bf16[32,24,768]{2,1,0:T(8,128)(2,1)S(1)}, bf16[32,24,768]{2,1,0:T(8,128)(2,1)}, u32[]{:S(2)}) copy-start(bf16[32,24,768]{2,1,0:T(8,128)(2,1)} %get-tuple-element.52) | copy-start | bytes 3538948
  156.5 11.9 %copy-start.53 = (f32[256]{0:T(256)}, f32[256]{0:T(256)S(1)}, u32[]{:S(2)}) copy-start(f32[256]{0:T(256)S(1)} %broadcast_multiply_fusion.11) | copy-start | bytes 3076
  156.7 11.7 %copy-start.67 = (f32[256]{0:T(256)}, f32[256]{0:T(256)S(1)}, u32[]{:S(2)}) copy-start(f32[256]{0:T(256)S(1)} %add_rsqrt_fusion.3) | copy-start | bytes 3076
  168.4 71.0 %copy-start.6 = (bf16[256,3072]{1,0:T(8,128)(2,1)}, bf16[256,3072]{1,0:T(8,128)(2,1)S(1)}, u32[]{:S(2)}) copy-start(bf16[256,3072]{1,0:T(8,128)(2,1)S(1)} %get-tuple-element.140) | copy-start | bytes 4718596
  172.8 130.9 %copy-start.59 = (f32[256]{0:T(256)}, f32[256]{0:T(256)S(1)}, u32[]{:S(2)}) copy-start(f32[256]{0:T(256)S(1)} %broadcast_multiply_fusion.10) | copy-start | bytes 3076
  173.1 130.6 %copy-start.73 = (f32[256]{0:T(256)}, f32[256]{0:T(256)S(1)}, u32[]{:S(2)}) copy-start(f32[256]{0:T(256)S(1)} %add_rsqrt_fusion.2) | copy-start | bytes 3076
  303.6 12.2 %copy-start.22 = (bf16[128,768]{1,0:T(8,128)(2,1)}, bf16[128,768]{1,0:T(8,128)(2,1)S(1)}, u32[]{:S(2)}) copy-start(bf16[128,768]{1,0:T(8,128)(2,1)S(1)} %get-tuple-element.151) | copy-start | bytes 589828
  303.6 12.2 %copy-start.24 = (bf16[128,768]{1,0:T(8,128)(2,1)}, bf16[128,768]{1,0:T(8,128)(2,1)S(1)}, u32[]{:S(2)}) copy-start(bf16[128,768]{1,0:T(8,128)(2,1)S(1)} %get-tuple-element.152) | copy-start | bytes 589828
  329.4 84.9 %copy-start.2 = (f32[256,768]{1,0:T(8,128)}, f32[256,768]{1,0:T(8,128)S(1)}, u32[]{:S(2)}) copy-start(f32[256,768]{1,0:T(8,128)S(1)} %get-tuple-element.137) | copy-start | bytes 2359300
  379.7 34.6 %copy-start.26 = (bf16[128,768]{1,0:T(8,128)(2,1)}, bf16[128,768]{1,0:T(8,128)(2,1)S(1)}, u32[]{:S(2)}) copy-start(bf16[128,768]{1,0:T(8,128)(2,1)S(1)} %get-tuple-element.149) | copy-start | bytes 589828
  379.7 34.6 %copy-start.29 = (bf16[128,768]{1,0:T(8,128)(2,1)}, bf16[128,768]{1,0:T(8,128)(2,1)S(1)}, u32[]{:S(2)}) copy-start(bf16[128,768]{1,0:T(8,128)(2,1)S(1)} %get-tuple-element.150) | copy-start | bytes 589828
  379.7 34.6 %copy-start.49 = (f32[768]{0:T(1024)S(1)}, f32[768]{0:T(1024)}, u32[]{:S(2)}) copy-start(f32[768]{0:T(1024)} %copy-done.48) | copy-start | bytes 9220
  379.7 34.6 %copy-start.60 = (f32[256]{0:T(256)S(1)}, f32[256]{0:T(256)}, u32[]{:S(2)}) copy-start(f32[256]{0:T(256)} %copy-done.59) | copy-start | bytes 3076
  379.7 34.6 %copy-start.74 = (f32[256]{0:T(256)S(1)}, f32[256]{0:T(256)}, u32[]{:S(2)}) copy-start(f32[256]{0:T(256)} %copy-done.73) | copy-start | bytes 3076
  428.1 113.1 %copy-start.4 = (f32[256,768]{1,0:T(8,128)}, f32[256,768]{1,0:T(8,128)S(1)}, u32[]{:S(2)}) copy-start(f32[256,768]{1,0:T(8,128)S(1)} %get-tuple-element.133) | copy-start | bytes 2359300
  546.1 64.2 %copy-start.27 = (bf16[128,768]{1,0:T(8,128)(2,1)S(1)}, bf16[128,768]{1,0:T(8,128)(2,1)}, u32[]{:S(2)}) copy-start(bf16[128,768]{1,0:T(8,128)(2,1)} %copy-done.26) | copy-start | bytes 589828
  546.1 64.2 %copy-start.30 = (bf16[128,768]{1,0:T(8,128)(2,1)S(1)}, bf16[128,768]{1,0:T(8,128)(2,1)}, u32[]{:S(2)}) copy-start(bf16[128,768]{1,0:T(8,128)(2,1)} %copy-done.29) | copy-start | bytes 589828
  546.1 66.2 %copy-start = (f32[256,1536]{1,0:T(8,128)S(1)}, f32[256,1536]{1,0:T(8,128)}, u32[]{:S(2)}) copy-start(f32[256,1536]{1,0:T(8,128)} %reduce_rows.2) | copy-start | bytes 4718596
  546.1 69.9 %copy-start.65 = (f32[768]{0:T(1024)S(1)}, f32[768]{0:T(1024)}, u32[]{:S(2)}) copy-start(f32[768]{0:T(1024)} %get-tuple-element.134) | copy-start | bytes 9220
  546.1 70.0 %copy-start.64 = (f32[768]{0:T(1024)S(1)}, f32[768]{0:T(1024)}, u32[]{:S(2)}) copy-start(f32[768]{0:T(1024)} %get-tuple-element.105) | copy-start | bytes 9220
  632.8 66.2 %copy-start.52 = (f32[8,128]{1,0:T(8,128)S(1)}, f32[8,128]{1,0:T(8,128)}, u32[]{:S(2)}) copy-start(f32[8,128]{1,0:T(8,128)} %get-tuple-element.79) | copy-start | bytes 12292
  632.8 70.3 %copy-start.45 = (f32[96,768]{1,0:T(8,128)S(1)}, f32[96,768]{1,0:T(8,128)}, u32[]{:S(2)}) copy-start(f32[96,768]{1,0:T(8,128)} %get-tuple-element.77) | copy-start | bytes 884740
  632.8 72.2 %copy-start.44 = (f32[24,3072]{1,0:T(8,128)S(1)}, f32[24,3072]{1,0:T(8,128)}, u32[]{:S(2)}) copy-start(f32[24,3072]{1,0:T(8,128)} %get-tuple-element.75) | copy-start | bytes 884740
  632.8 74.0 %copy-start.47 = (f32[24,768]{1,0:T(8,128)S(1)}, f32[24,768]{1,0:T(8,128)}, u32[]{:S(2)}) copy-start(f32[24,768]{1,0:T(8,128)} %get-tuple-element.73) | copy-start | bytes 221188
  632.8 75.5 %copy-start.46 = (f32[24,2304]{1,0:T(8,128)S(1)}, f32[24,2304]{1,0:T(8,128)}, u32[]{:S(2)}) copy-start(f32[24,2304]{1,0:T(8,128)} %get-tuple-element.71) | copy-start | bytes 663556
  699.0 11.1 %copy-start.5 = (f32[256,768]{1,0:T(8,128)S(1)}, f32[256,768]{1,0:T(8,128)}, u32[]{:S(2)}) copy-start(f32[256,768]{1,0:T(8,128)} %copy-done.4) | copy-start | bytes 2359300
  699.0 11.1 %copy-start.34 = (bf16[128,768]{1,0:T(8,128)(2,1)S(1)}, bf16[128,768]{1,0:T(8,128)(2,1)}, u32[]{:S(2)}) copy-start(bf16[128,768]{1,0:T(8,128)(2,1)} %copy-done.32) | copy-start | bytes 589828
  (57 other events, 269.0 us)

commit v3 on v2

v3 whole, which is shorter than its diff:
```python
import itertools
from functools import partial
from types import SimpleNamespace

import jax
import jax.numpy as jnp
from jax import lax
from jax.experimental import pallas as pl
from jax.experimental.pallas import tpu as pltpu
from jax.sharding import PartitionSpec as P

MESH = pl.DeviceIdType.MESH
SEQ, BATCH = "seq", "batch"


HEAD_PLACES = SimpleNamespace(
    arrivals=(
        (13, 14, 32, 23, 53, 40, 88, 31, 59, 61, 74, 67, 81, 87, 107),
        (11, 12, 29),
        (21, 15, 41, 25, 42, 50, 90, 34, 58, 64, 79, 68, 101, 92, 105),
        (18, 33, 46, 17, 43, 66, 96, 45, 97, 65, 104, 71, 106, 89, 108),
        (30, 20, 49, 10, 62, 63, 115, 48, 77, 69, 111, 82, 120, 110, 125),
        (27, 24, 57, 22, 60, 52, 94, 39, 78, 80, 100, 76, 91, 103, 114),
        (38, 26, 51, 35, 70, 73, 95, 37, 84, 85, 117, 93, 123, 109, 128),
        (16, 28, 83, 19, 47, 99, 118, 4, 36, 75, 126, 72, 122, 134, 131),
        (55, 54, 127, 56, 86, 132, 142, 44, 98, 137, 140, 102, 135, 143, 145),
        (129, 124, 146),
        (133, 130, 141),
        (138, 136, 147),
        (144, 139, 148),
    ),
    project=112,
)
TAIL_PLACES = SimpleNamespace(
    arrivals=(
        (9, 8, 48, 19, 39, 31, 73, 26, 62, 57, 75, 65, 86, 83, 93),
        (36, 5, 32, 6, 17, 38, 68, 13, 67, 50, 72, 56, 69, 70, 87),
        (28, 10, 61, 11, 47, 46, 80, 20, 60, 64, 82, 74, 91, 89, 110),
        (34, 23, 44, 24, 49, 51, 78, 43, 81, 88, 107, 77, 92, 99, 104),
        (33, 29, 66, 30, 59, 71, 95, 45, 76, 79, 102, 84, 119, 98, 114),
        (53, 55, 90, 35, 52, 96, 103, 40, 58, 106, 115, 63, 112, 123, 122),
        (37, 105, 120, 42, 85, 117, 129, 54, 94, 121, 131, 97, 130, 133, 135),
        (116, 113, 132),
        (118, 126, 134),
        (125, 124, 136),
        (127, 128, 137),
    ),
    steps=(3, 4, 12, 15, 16, 21, 22, 27, 41),
    project=100,
)
ROWS_PLACES = SimpleNamespace(
    rows=(
        (0, 3, 4, 17, 53),
        (1, 7, 9, 25, 45),
        (11, 23, 21, 43, 52),
        (6, 13, 30, 38, 54),
    ),
    weights=(
        (5, 10, 16, 14, 15, 8, 19, 18, 12, 24, 20, 34, 31, 22, 32, 46, 55),
        (27, 28, 29, 37, 33, 39, 36, 41, 35, 47, 42, 44, 40, 49, 50, 48, 56),
    ),
    grads=(2, 26),
    collect=51,
)
BELOW_PLACES = SimpleNamespace(
    weights=(
        (9, 12, 11, 14, 47, 36, 45, 27, 66, 48, 20, 52, 70, 54, 61, 73, 77),
        (10, 37, 49, 24, 58, 26, 33, 69, 68, 30, 32, 64, 72, 40, 63, 75, 78),
        (6, 22, 18, 23, 31, 21, 39, 29, 42, 38, 43, 46, 60, 53, 62, 74, 76),
        (1, 4, 3, 2, 15, 13, 7, 19, 41, 17, 44, 28, 59, 16, 55, 67, 71),
    ),
    grads=(8, 5, 0),
    steps=(25, 34, 35, 50, 51, 56, 57, 65),
)
LAST_PLACES = SimpleNamespace(
    weights=(
        (22, 31, 32, 33, 61, 36, 57, 65, 74, 41, 63, 67, 79, 58, 72, 84, 88),
        (21, 43, 45, 47, 62, 46, 48, 75, 77, 51, 64, 78, 80, 56, 83, 81, 87),
        (11, 29, 34, 40, 49, 50, 44, 37, 52, 53, 55, 60, 68, 66, 70, 82, 86),
        (9, 13, 15, 18, 30, 35, 23, 42, 54, 25, 27, 59, 71, 39, 69, 76, 85),
        (1, 2, 5, 12, 14, 3, 4, 17, 24, 6, 7, 16, 28, 8, 19, 26, 38),
    ),
    grads=(20, 10, 0),
    steps=(73,),
)


def place():
    s = lax.axis_index(SEQ)
    return {"y": s // 4, "x": (s // 2) % 2, "c": s % 2, "z": lax.axis_index(BATCH)}


def device_of(p):
    return ((p["y"] * 2 + p["x"]) * 2 + p["c"], p["z"])


def flipped(p, axis):
    return {**p, axis: 1 - p[axis]}


def at_depth(p, z):
    return {**p, "z": z}


def number_in(depth):
    return lambda p: device_of(p)[0] * depth + p["z"]


def number_in_sequence(p):
    return device_of(p)[0]


def when(cond, action):
    if cond is None:
        action()
    else:
        pl.when(cond)(action)


def ranked(z, rank, depth):
    near = [sorted(range(depth), key=lambda q: (abs(q - k), q))[rank] for k in range(depth)]
    return sum(jnp.where(z == k, near[k], 0) for k in range(depth))


def offsets(order, depth):
    return list(itertools.product(*[range(depth if a == "z" else 2) for a in order]))


def target_of(order, offset, depth, me):
    p = me
    for axis, d in zip(order, offset):
        if d:
            p = at_depth(p, ranked(me["z"], d, depth)) if axis == "z" else flipped(p, axis)
    return p


def last_move(offset):
    return max([-1] + [i for i, d in enumerate(offset) if d])


def greet(axes, depth, spread=False, collect=False):
    me = place()
    barrier = pltpu.get_barrier_semaphore()

    def signal(device):
        pl.semaphore_signal(barrier, inc=1, device_id=device, device_id_type=MESH)

    count = 0
    for axis in axes + ("c",):
        if axis == "z":
            for step in (1, -1):
                peer = at_depth(me, me["z"] + step)
                cond = (peer["z"] >= 0) & (peer["z"] < depth)
                when(cond, lambda peer=peer: signal(device_of(peer)))
                count = count + cond.astype(jnp.int32)
        else:
            signal(device_of(flipped(me, axis)))
            count = count + 1
    if spread or collect:
        seq, z = lax.axis_index(SEQ), lax.axis_index(BATCH)
        if spread:
            when(seq != 0, lambda: signal((0, z)))
            count = count + jnp.where(seq == 0, HELPERS - 1, 0)
        if collect:

            @pl.when(seq == 0)
            def _():
                for j in range(1, HELPERS):
                    signal((j, z))

            count = count + jnp.where(seq == 0, 0, 1)
    pl.semaphore_wait(barrier, count)


class Gather:
    def __init__(self, source, target, number, order, depth, send, recv, send_at):
        self.source, self.target, self.number = source, target, number
        self.order, self.depth, self.send, self.recv = order, depth, send, recv
        self.send_at = send_at
        self.me = place()
        self.sent = []

    @staticmethod
    def sends(order, depth):
        return sum(len(order) + 2 - last_move(t) for t in offsets(order, depth))

    def onward(self, offset):
        last = last_move(offset)
        z = self.me["z"]
        moves = []
        if last >= 0 and self.order[last] == "z":
            source = ranked(z, offset[last], self.depth)
            peer = jnp.where(source < z, z + 1, z - 1)
            moves.append((at_depth(self.me, peer), (peer >= 0) & (peer < self.depth)))
        for axis in self.order[last + 1 :]:
            if axis == "z":
                moves.append((at_depth(self.me, z + 1), z + 1 < self.depth))
                moves.append((at_depth(self.me, z - 1), z > 0))
            else:
                moves.append((flipped(self.me, axis), None))
        moves.append((flipped(self.me, "c"), None))
        return moves

    def arrival(self, p):
        ref = self.target(p)
        return pltpu.make_async_remote_copy(
            src_ref=ref, dst_ref=ref, send_sem=self.send.at[0], recv_sem=self.recv.at[self.number(p)],
            device_id=device_of(self.me), device_id_type=MESH,
        )

    def handle(self, offset):
        p = target_of(self.order, offset, self.depth, self.me)
        own = not any(offset)
        if not own:
            self.arrival(p).wait_recv()
        for peer, cond in self.onward(offset):
            copy = pltpu.make_async_remote_copy(
                src_ref=self.source if own else self.target(p), dst_ref=self.target(p),
                send_sem=self.send.at[self.send_at], recv_sem=self.recv.at[self.number(p)],
                device_id=device_of(peer), device_id_type=MESH,
            )
            when(cond, copy.start)
            self.sent.append((cond, self.send_at))
            self.send_at += 1

    def begin(self):
        self.handle((0,) * len(self.order))

    def events(self, places):
        marks = [t for t in offsets(self.order, self.depth) if any(t)]
        return [(at, partial(self.handle, t)) for at, t in zip(places, marks, strict=True)]

    def siblings(self):
        for t in offsets(self.order, self.depth):
            self.arrival(flipped(target_of(self.order, t, self.depth, self.me), "c")).wait_recv()

    def drain(self):
        for cond, slot in self.sent:
            copy = pltpu.make_async_remote_copy(
                src_ref=self.source, dst_ref=self.target(self.me), send_sem=self.send.at[slot],
                recv_sem=self.recv.at[self.number(self.me)], device_id=device_of(self.me), device_id_type=MESH,
            )
            when(cond, copy.wait_send)


def end_gathers(jobs):
    for job in jobs:
        job.siblings()
    for job in jobs:
        job.drain()


class Reduce:
    def __init__(self, partial_of, inbox, order, depth, send, recv):
        self.partial_of, self.inbox = partial_of, inbox
        self.order, self.depth, self.send, self.recv = order, depth, send, recv
        self.me = place()
        self.base, _ = self.slots(order, depth)
        self.marks = sorted(offsets(order, depth), key=lambda t: (-sum(t), t))
        self.sent = []

    @staticmethod
    def split(order, offset):
        if "z" not in order:
            return offset, 0
        i = order.index("z")
        return offset[:i] + (0,) + offset[i + 1 :], offset[i]

    @staticmethod
    def slots(order, depth):
        base, count = {}, 0
        deep = depth if "z" in order else 1
        for t in offsets(order, depth):
            key, rank = Reduce.split(order, t)
            if rank:
                continue
            last = last_move(key)
            for i, axis in enumerate(order):
                if i <= last:
                    continue
                base[(key, axis)] = count
                if axis == "z":
                    count += deep + 1
                elif "z" in order and i > order.index("z"):
                    count += deep
                else:
                    count += 1
            base[(key, "c")] = count
            count += deep
        return base, count

    def where_(self, key, axis, z):
        deep = "z" in self.order and (axis == "c" or self.order.index(axis) > self.order.index("z"))
        return self.base[(key, axis)] + (z if deep else 0)

    def copy(self, source, edge, slot, peer):
        return pltpu.make_async_remote_copy(
            src_ref=source, dst_ref=self.inbox.at[edge], send_sem=self.send.at[slot],
            recv_sem=self.recv.at[edge], device_id=device_of(peer), device_id_type=MESH,
        )

    def start(self, offset):
        p = target_of(self.order, offset, self.depth, self.me)
        key, _ = self.split(self.order, offset)
        slot = self.marks.index(offset)
        edge = self.where_(key, "c", p["z"])
        peer = flipped(self.me, "c")
        self.copy(self.partial_of(flipped(p, "c")), edge, slot, peer).start()
        self.sent.append(slot)

    def kids(self, offset, p):
        key, rank = self.split(self.order, offset)
        last, z = last_move(offset), self.me["z"]
        found = [(self.where_(key, "c", p["z"]), None)]
        for axis in self.order[last + 1 :]:
            if axis == "z":
                at = self.base[(key, "z")]
                found += [(at + z, z > 0), (at + self.depth, z + 1 < self.depth)]
            else:
                found.append((self.where_(key, axis, p["z"]), None))
        if last >= 0 and self.order[last] == "z":
            far = jnp.where(p["z"] < z, z + 1, z - 1)
            found.append((self.base[(key, "z")] + p["z"], (far >= 0) & (far < self.depth)))
        return found

    def upward(self, offset, p):
        key, rank = self.split(self.order, offset)
        k, z = last_move(offset), self.me["z"]
        axis = self.order[k]
        if axis == "z":
            edge = self.base[(key, "z")] + jnp.where(p["z"] == z - 1, self.depth, p["z"])
            return edge, at_depth(self.me, jnp.where(p["z"] < z, z - 1, z + 1))
        parent = key[:k] + (0,) + key[k + 1 :]
        return self.where_(parent, axis, p["z"]), flipped(self.me, axis)

    def handle(self, offset, add, finish):
        p = target_of(self.order, offset, self.depth, self.me)
        kids = self.kids(offset, p)
        slot = len(self.marks) + self.marks.index(offset)
        for edge, cond in kids:
            when(cond, self.copy(self.inbox.at[edge], edge, slot, self.me).wait_recv)
        parts = [(self.inbox.at[edge], cond) for edge, cond in kids]
        if any(offset):
            into = parts[0][0]
            add(self.partial_of(p), parts, into)
            edge, peer = self.upward(offset, p)
            self.copy(into, edge, slot, peer).start()
            self.sent.append(slot)
        else:
            finish(self.partial_of(p), parts)

    def drain(self):
        for slot in self.sent:
            self.copy(self.inbox.at[0], 0, slot, self.me).wait_send()


D = 768
H = 12
DH = 64
BLK = 64
R = 3
GLOB = 2
L = 2
PAIRS = H // 2
WIDE = 2 * DH
SHARED = GLOB * BLK
SHARE = 16
HELPERS = SHARED // SHARE
VMEM_LIMIT = 60 * 1024 * 1024

layer_eps = 1e-06
masked_score = -1e30

Z_Y_X, Z_X_Y, X_Y_Z, Y_X_Z = ("z", "y", "x"), ("z", "x", "y"), ("x", "y", "z"), ("y", "x", "z")
Y_X, X_Y = ("y", "x"), ("x", "y")
ANYWHERE = pl.BlockSpec(memory_space=pl.ANY)
IN_VMEM = pl.BlockSpec(memory_space=pltpu.VMEM)


def dma(*shape):
    return pltpu.SemaphoreType.DMA(shape)


def product(a, b):
    return lax.dot_general(a, b, (((1,), (0,)), ((), ())), preferred_element_type=jnp.float32)


def product_nt(a, b):
    return lax.dot_general(a, b, (((1,), (1,)), ((), ())), preferred_element_type=jnp.float32)


def product_tn(a, b):
    return lax.dot_general(a, b, (((0,), (0,)), ((), ())), preferred_element_type=jnp.float32)


def split_heads(pair_rows):
    low_lanes = lax.broadcasted_iota(jnp.int32, (1, WIDE), 1) < DH
    zero = jnp.zeros_like(pair_rows)
    return jnp.concatenate([jnp.where(low_lanes, pair_rows, zero), jnp.where(low_lanes, zero, pair_rows)], axis=0)


def join_heads(stacked):
    low_lanes = lax.broadcasted_iota(jnp.int32, (1, WIDE), 1) < DH
    rows = stacked.shape[0] // 2
    return jnp.where(low_lanes, stacked[:rows], stacked[rows:])


def row_of(block):
    return pl.multiple_of(block * BLK, BLK)


def block_of(ref, block):
    held = ref.shape[2] // BLK
    return ref[block // held, 0, pl.ds(row_of(block % held), BLK)]


def whole(ref):
    return ref[...].reshape(-1, WIDE)


def window_blocks(first, block, blocks_all):
    return [(first + block + j - 1 + blocks_all) % blocks_all for j in range(3)]


def drawn_blocks(picks_ref, pair, block, r):
    return [picks_ref[(block * H + 2 * pair + side) * R + r] for side in range(2)]


def bring(picks_ref, first, pair, pairs, blocks_here):
    low_lanes = lax.broadcasted_iota(jnp.int32, (1, WIDE), 1) < DH
    for block in range(blocks_here):
        for source, target in pairs:
            blocks_all = source.shape[0] * source.shape[2] // BLK
            for j, one in enumerate(window_blocks(first, block, blocks_all)):
                target[block, j * BLK : (j + 1) * BLK] = block_of(source, one)
            for r in range(R):
                one, two = drawn_blocks(picks_ref, pair, block, r)
                target[block, (3 + r) * BLK : (4 + r) * BLK] = jnp.where(
                    low_lanes, block_of(source, one), block_of(source, two)
                )


def with_shared(ref, near):
    return jnp.concatenate([ref[0, 0, 0:SHARED], near], axis=0)


def key_scores(keys, q_heads, shut):
    scores = product_nt(keys, q_heads)
    end = SHARED + 3 * BLK
    return jnp.concatenate([scores[:SHARED], scores[SHARED:end] + shut, scores[end:]], axis=0)


def soft(scores):
    top = jnp.max(scores, axis=0, keepdims=True)
    weight = jnp.exp(scores - top)
    total = jnp.sum(weight, axis=0, keepdims=True)
    return weight * (1.0 / total), top + jnp.log(total)


def attend_kernel(
    picks_ref, first_ref, q_ref, k_ref, v_ref, shut_ref, part_ref, o_ref, po_ref, log_ref, plog_ref, near_k, near_v
):
    pair = pl.program_id(0)
    blocks_here = q_ref.shape[0] // BLK
    bring(picks_ref, first_ref[0], pair, [(k_ref, near_k), (v_ref, near_v)], blocks_here)
    scale = jnp.bfloat16(DH ** (-0.5))
    weight, logs = soft(product_nt(whole(k_ref), split_heads(part_ref[...] * scale)))
    mixed = product_tn(weight.astype(jnp.bfloat16), whole(v_ref))
    po_ref[...] = join_heads(mixed).astype(po_ref.dtype)
    plog_ref[0] = logs
    for block in range(blocks_here):
        here = slice(block * BLK, (block + 1) * BLK)
        q_heads = split_heads(q_ref[here] * scale)
        weight, logs = soft(key_scores(with_shared(k_ref, near_k[block]), q_heads, shut_ref[block]))
        mixed = product_tn(weight.astype(jnp.bfloat16), with_shared(v_ref, near_v[block]))
        o_ref[here] = join_heads(mixed).astype(o_ref.dtype)
        log_ref[0, block : block + 1] = logs


def near_rows(rows, dtype):
    return pltpu.VMEM((rows // BLK, 6 * BLK, WIDE), dtype)


def columns(rows, shift=0):
    return pl.BlockSpec((rows, WIDE), lambda p, *_: (0, p + shift))


def of_all(kv, shift=0):
    return pl.BlockSpec((kv.shape[0], 1, kv.shape[2], WIDE), lambda p, *_: (0, p + shift, 0, 0))


def by_pair(rows, lanes):
    return pl.BlockSpec((1, rows, lanes), lambda p, *_: (p, 0, 0))


def attend(picks, first, queries, kv, shut, part):
    rows = queries.shape[0]
    blocks = rows // BLK
    return pl.pallas_call(
        attend_kernel,
        grid_spec=pltpu.PrefetchScalarGridSpec(
            num_scalar_prefetch=2,
            grid=(PAIRS,),
            in_specs=[
                columns(rows), of_all(kv), of_all(kv, PAIRS),
                pl.BlockSpec(shut.shape, lambda p, *_: (0, 0, 0)), columns(SHARE),
            ],
            out_specs=[columns(rows), columns(SHARE), by_pair(blocks, WIDE), by_pair(1, 2 * SHARE)],
            scratch_shapes=[near_rows(rows, jnp.bfloat16)] * 2,
        ),
        out_shape=[
            jax.ShapeDtypeStruct((rows, D), jnp.bfloat16),
            jax.ShapeDtypeStruct((SHARE, D), jnp.bfloat16),
            jax.ShapeDtypeStruct((PAIRS, blocks, WIDE), jnp.float32),
            jax.ShapeDtypeStruct((PAIRS, 1, 2 * SHARE), jnp.float32),
        ],
        compiler_params=pltpu.CompilerParams(vmem_limit_bytes=VMEM_LIMIT),
        name="attend",
    )(picks, first, queries, kv, kv, shut, part)


def score_grads(weight, values, cot_heads):
    grads = product_nt(values, cot_heads)
    mean = jnp.sum(weight * grads, axis=0, keepdims=True)
    return (weight * (grads - mean)).astype(jnp.bfloat16)


def attend_back_kernel(
    picks_ref, first_ref, q_ref, k_ref, v_ref, shut_ref, do_ref, part_ref, pdo_ref, log_ref, plog_ref,
    dq_ref, dk_ref, dv_ref, pdq_ref, sum_k, sum_v, near_k, near_v, grad_k, grad_v,
):
    pair = pl.program_id(0)
    first = first_ref[0]
    blocks_here, blocks_all = q_ref.shape[0] // BLK, sum_k.shape[0] // BLK
    bring(picks_ref, first, pair, [(k_ref, near_k), (v_ref, near_v)], blocks_here)
    low_lanes = lax.broadcasted_iota(jnp.int32, (1, WIDE), 1) < DH
    step = DH ** (-0.5)
    scale = jnp.bfloat16(step)
    part, cot = split_heads(part_ref[...] * scale), split_heads(pdo_ref[...])
    weight = jnp.exp(product_nt(whole(k_ref), part) - plog_ref[0])
    grads = score_grads(weight, whole(v_ref), cot)
    pdq_ref[...] = (join_heads(product_tn(grads, whole(k_ref))) * step).astype(pdq_ref.dtype)
    sum_k[...] = product(grads, part)
    sum_v[...] = product(weight.astype(jnp.bfloat16), cot)
    shared_k = jnp.zeros((SHARED, WIDE), jnp.float32)
    shared_v = jnp.zeros((SHARED, WIDE), jnp.float32)
    for block in range(blocks_here):
        here = slice(block * BLK, (block + 1) * BLK)
        do = jnp.where(first + block < GLOB, jnp.bfloat16(0), do_ref[here])
        q_heads, do_heads = split_heads(q_ref[here] * scale), split_heads(do)
        keys, values = with_shared(k_ref, near_k[block]), with_shared(v_ref, near_v[block])
        weight = jnp.exp(key_scores(keys, q_heads, shut_ref[block]) - log_ref[0, block : block + 1])
        grads = score_grads(weight, values, do_heads)
        dq_ref[here] = (join_heads(product_tn(grads, keys)) * step).astype(dq_ref.dtype)
        key_grad = product(grads, q_heads)
        value_grad = product(weight.astype(jnp.bfloat16), do_heads)
        shared_k = shared_k + key_grad[:SHARED]
        shared_v = shared_v + value_grad[:SHARED]
        grad_k[block] = key_grad[SHARED:]
        grad_v[block] = value_grad[SHARED:]
    sum_k[0:SHARED] += shared_k
    sum_v[0:SHARED] += shared_v
    for block in range(blocks_here):
        for grad, total in ((grad_k, sum_k), (grad_v, sum_v)):
            for j, one in enumerate(window_blocks(first, block, blocks_all)):
                total[pl.ds(row_of(one), BLK)] += grad[block, j * BLK : (j + 1) * BLK]
            for r in range(R):
                tile = grad[block, (3 + r) * BLK : (4 + r) * BLK]
                one, two = drawn_blocks(picks_ref, pair, block, r)
                total[pl.ds(row_of(one), BLK)] += jnp.where(low_lanes, tile, 0.0)
                total[pl.ds(row_of(two), BLK)] += jnp.where(low_lanes, 0.0, tile)
    dk_ref[...] = sum_k[...].astype(dk_ref.dtype).reshape(dk_ref.shape)
    dv_ref[...] = sum_v[...].astype(dv_ref.dtype).reshape(dv_ref.shape)


def attend_back(picks, first, queries, kv, shut, cot, part, part_cot, logs, part_logs):
    rows, grads = queries.shape[0], (kv.shape[0], PAIRS) + kv.shape[2:]
    length = kv.shape[0] * kv.shape[2]
    return pl.pallas_call(
        attend_back_kernel,
        grid_spec=pltpu.PrefetchScalarGridSpec(
            num_scalar_prefetch=2,
            grid=(PAIRS,),
            in_specs=[
                columns(rows), of_all(kv), of_all(kv, PAIRS),
                pl.BlockSpec(shut.shape, lambda p, *_: (0, 0, 0)), columns(rows), columns(SHARE), columns(SHARE),
                by_pair(rows // BLK, WIDE), by_pair(1, 2 * SHARE),
            ],
            out_specs=[columns(rows), of_all(kv), of_all(kv), columns(SHARE)],
            scratch_shapes=[pltpu.VMEM((length, WIDE), jnp.float32)] * 2
            + [near_rows(rows, jnp.bfloat16)] * 2
            + [near_rows(rows, jnp.float32)] * 2,
        ),
        out_shape=[
            jax.ShapeDtypeStruct((rows, D), jnp.bfloat16),
            jax.ShapeDtypeStruct(grads, jnp.bfloat16),
            jax.ShapeDtypeStruct(grads, jnp.bfloat16),
            jax.ShapeDtypeStruct((SHARE, D), jnp.bfloat16),
        ],
        compiler_params=pltpu.CompilerParams(vmem_limit_bytes=VMEM_LIMIT),
        name="attend_back",
    )(picks, first, queries, kv, kv, shut, cot, part, part_cot, logs, part_logs)


def call(body, name, cid, ins, outs, scratch):
    names = list(ins) + list(outs) + list(scratch)
    got = pl.pallas_call(
        lambda *refs: body(SimpleNamespace(**dict(zip(names, refs)))),
        out_shape=[jax.ShapeDtypeStruct(shape, dtype) for shape, dtype, _ in outs.values()],
        in_specs=[where for _, where in ins.values()],
        out_specs=[where for _, _, where in outs.values()],
        scratch_shapes=list(scratch.values()),
        compiler_params=pltpu.CompilerParams(
            collective_id=cid, has_side_effects=cid is not None, vmem_limit_bytes=VMEM_LIMIT
        ),
        name=name,
    )(*[array for array, _ in ins.values()])
    return SimpleNamespace(**dict(zip(outs, got)))


def over(count, act):
    def step(i, carry):
        act(i)
        return carry

    lax.fori_loop(0, count, step, 0)


def span(i, size, first=0):
    return pl.ds(pl.multiple_of(first + i * size, size), size)


def run_in_order(timed):
    for _, act in sorted(timed, key=lambda pair: pair[0]):
        act()


def layer_pieces(rows_in, rows_down, first):
    half, wide = rows_down // 2, 3 * D // 2
    return [
        (first, 0, rows_in, 0, wide, Z_Y_X),
        (first, 0, rows_in, wide, wide, Z_X_Y),
        (first + 1, 0, rows_in, 0, D, Z_X_Y),
        (first + 2, 0, rows_in, 0, 2 * D, Z_Y_X),
        (first + 2, 0, rows_in, 2 * D, 2 * D, Z_X_Y),
        (first + 3, 0, half, 0, D, X_Y_Z),
        (first + 3, half, half, 0, D, Y_X_Z),
    ]


class Gathering:
    def __init__(self, arrays, pieces, seq_count, depth, near):
        self.near = near
        self.arrays, self.pieces, self.depth, self.n_dev = arrays, pieces, depth, seq_count * depth
        flat_only = {which for which, *_, order in pieces if "z" not in order}
        self.counts = [seq_count if i in flat_only else self.n_dev for i in range(len(arrays))]

    def ins(self):
        return {"slab%d" % i: (a, ANYWHERE) for i, a in enumerate(self.arrays)}

    def outs(self):
        return {
            "every%d" % i: ((n,) + a.shape, a.dtype, IN_VMEM if i in self.near else ANYWHERE)
            for i, (n, a) in enumerate(zip(self.counts, self.arrays))
        }

    def scratch(self):
        total = sum(Gather.sends(order, self.depth) for *_, order in self.pieces)
        return {
            "g_send": dma(total),
            "g_recv": dma(len(self.pieces), self.n_dev),
            "g_local": dma(len(self.arrays)),
        }

    def number(self, i):
        return number_in(self.depth) if self.counts[i] == self.n_dev else number_in_sequence

    def begin(self, refs):
        slabs = [getattr(refs, "slab%d" % i) for i in range(len(self.arrays))]
        every = [getattr(refs, "every%d" % i) for i in range(len(self.arrays))]
        self.jobs, at = [], 0
        for k, (which, row, rows, column, columns_, order) in enumerate(self.pieces):
            window = (pl.ds(row, rows), pl.ds(column, columns_))
            number = self.number(which)
            self.jobs.append(
                Gather(
                    slabs[which].at[window],
                    lambda p, which=which, window=window, number=number: every[which].at[(number(p),) + window],
                    number, order, self.depth, refs.g_send, refs.g_recv.at[k], at,
                )
            )
            at += Gather.sends(order, self.depth)
        for job in self.jobs:
            job.begin()
        me = place()
        self.own = [
            pltpu.make_async_copy(slab, all_.at[self.number(i)(me)], refs.g_local.at[i])
            for i, (slab, all_) in enumerate(zip(slabs, every))
        ]
        for copy in self.own:
            copy.start()

    def hurry(self, refs, arrays):
        for (which, *_), job in zip(self.pieces, self.jobs):
            if which in arrays:
                job.siblings()
        for i in arrays:
            self.own[i].wait()
        self.early = arrays

    def end(self):
        for (which, *_), job in zip(self.pieces, self.jobs):
            if which not in self.early:
                job.siblings()
        for job in self.jobs:
            job.drain()
        for i, copy in enumerate(self.own):
            if i not in self.early:
                copy.wait()

    def results(self, got):
        return [getattr(got, "every%d" % i) for i in range(len(self.arrays))]


def to_helpers(source, target, send, recv):
    seq, z = lax.axis_index(SEQ), lax.axis_index(BATCH)

    def copy(j):
        return pltpu.make_async_remote_copy(
            src_ref=source.at[pl.ds(j * SHARE, SHARE)], dst_ref=target, send_sem=send.at[j],
            recv_sem=recv, device_id=(j, z), device_id_type=MESH,
        )

    def begin():
        for j in range(1, HELPERS):
            copy(j).start()

    def own():
        pltpu.sync_copy(source.at[pl.ds(0, SHARE)], target)
        for j in range(1, HELPERS):
            copy(j).wait_send()

    def end():
        pl.when(seq == 0)(own)
        pl.when(seq != 0)(lambda: copy(1).wait_recv())

    pl.when(seq == 0)(begin)
    return end


def to_first(source, target, send, recv):
    seq, z = lax.axis_index(SEQ), lax.axis_index(BATCH)

    def copy(j):
        return pltpu.make_async_remote_copy(
            src_ref=source, dst_ref=target.at[pl.ds(j * SHARE, SHARE)], send_sem=send,
            recv_sem=recv.at[j], device_id=(0, z), device_id_type=MESH,
        )

    for j in range(1, HELPERS):
        pl.when(seq == j)(copy(j).start)

    def end():
        def mine():
            pltpu.sync_copy(source, target.at[pl.ds(0, SHARE)])
            for j in range(1, HELPERS):
                copy(j).wait_recv()

        pl.when(seq == 0)(mine)
        pl.when(seq != 0)(lambda: copy(1).wait_send())

    return end


def from_slabs(ref):
    def get(at):
        slabs = ref[:, :, at]
        return slabs.astype(jnp.float32).reshape(-1, slabs.shape[2]).astype(ref.dtype)

    return get


def project(low, w, bias, q, kv):
    def queries(i):
        at = span(i, 256)
        q[:, at] = (product(low[...], w(at)) + bias[0:1, at]).astype(q.dtype)

    def keys(i):
        keep(2 * i, product(low[...], w(span(i, 256, D))))

    def values(i):
        keep(PAIRS + 2 * i, product(low[...], w(span(i, 256, 2 * D))) + bias[1:2, span(i, 256)])

    def keep(pair, acc):
        kv[pair] = acc[:, :WIDE].astype(kv.dtype)
        kv[pair + 1] = acc[:, WIDE:].astype(kv.dtype)

    for act in (keys, values, queries):
        over(D // 256, act)


class Sequence:
    def __init__(self, rows, seq_count, depth, dtype):
        self.rows, self.seq_count, self.depth, self.dtype = rows, seq_count, depth, dtype

    def outs(self):
        return dict(
            q=((self.rows, D), self.dtype, IN_VMEM),
            every=((self.seq_count, 2 * PAIRS, self.rows, WIDE), self.dtype, ANYWHERE),
            part=((SHARE, D), self.dtype, ANYWHERE),
        )

    def scratch(self):
        return dict(
            kv=pltpu.VMEM((2 * PAIRS, self.rows, WIDE), self.dtype), send=dma(4 * Gather.sends(Y_X, self.depth)),
            recv=dma(4, self.seq_count), local=dma(), give=dma(HELPERS), take=dma(),
        )

    def prepare(self, refs):
        count, at = PAIRS // 2, 0
        self.jobs = []
        for i in range(4):
            window = pl.ds(i * count, count)
            self.jobs.append(
                Gather(
                    refs.kv.at[window],
                    lambda p, window=window: refs.every.at[number_in_sequence(p), window],
                    number_in_sequence, (X_Y, Y_X)[i % 2], self.depth, refs.send, refs.recv.at[i], at,
                )
            )
            at += Gather.sends(Y_X, self.depth)

    def begin(self, refs):
        for job in self.jobs:
            job.begin()
        self.finish = to_helpers(refs.q, refs.part, refs.give, refs.take)
        self.own = pltpu.make_async_copy(refs.kv, refs.every.at[number_in_sequence(place())], refs.local)
        self.own.start()

    def end(self):
        end_gathers(self.jobs)
        self.own.wait()
        self.finish()


def project_and_send(refs, gathering, sequence, low, which):
    def act():
        gathering.hurry(refs, [which])
        w = from_slabs(getattr(refs, "every%d" % which))
        project(low, w, refs.bias, refs.q, refs.kv)
        sequence.begin(refs)

    return act


def timed_events(jobs, places):
    return [pair for job, at in zip(jobs, places, strict=True) for pair in job.events(at)]


def first_head(low, small, segs, weights, seq_count, depth, cid):
    rows = low.shape[0]
    pieces = [(0, 0, small.shape[0], 0, 128, Z_Y_X), (1, 0, 8, 0, 128, Y_X)]
    pieces += layer_pieces(small.shape[0], weights[3].shape[0], 2)
    gathering = Gathering([small, segs] + weights, pieces, seq_count, depth, (0, 2))
    sequence = Sequence(rows, seq_count, depth, low.dtype)

    def body(refs):
        greet(("y", "x", "z"), depth, spread=True)
        gathering.begin(refs)
        sequence.prepare(refs)
        refs.bias = refs.vectors.at[0]

        def vectors():
            gathering.hurry(refs, [0])
            table = refs.every0[...].astype(jnp.float32).reshape(D, 128).T
            for layer in range(L):
                refs.vectors[layer, 0:6] = table[6 * layer : 6 * layer + 6]
                refs.vectors[layer, 6:8] = table[6 * L + 2 * layer : 6 * L + 2 * layer + 2]
            refs.table[...] = table[8 * L : 12 * L]

        def project_now():
            project_and_send(refs, gathering, sequence, refs.low, 2)()
            gathering.early = [0, 2]

        at = HEAD_PLACES
        run_in_order(
            timed_events(gathering.jobs + sequence.jobs, at.arrivals) + [(at.project, vectors), (at.project + 0.1, project_now)]
        )
        sequence.end()
        gathering.end()

    got = call(
        body, "first_head", cid,
        {"low": (low, IN_VMEM), **gathering.ins()},
        {
            **dict(vectors=((L, 8, D), jnp.float32, IN_VMEM), table=((4 * L, D), jnp.float32, IN_VMEM)),
            **sequence.outs(), **gathering.outs(),
        },
        {**sequence.scratch(), **gathering.scratch()},
    )
    results = gathering.results(got)
    return got, results[1], results[2:]


def norm_block(resid, gain, shift):
    center = resid - jnp.mean(resid, axis=1, keepdims=True)
    inv_std = lax.rsqrt(jnp.mean(center * center, axis=1, keepdims=True) + layer_eps)
    normed = center * inv_std
    return normed * gain + shift, normed, inv_std


ROW_BLOCK = 64


def tail_steps(refs, w_out, w_up, w_down, waits):
    rows, hidden = refs.resid.shape[0], refs.shifts.shape[1]

    def out():
        waits[0]()

        def act(i):
            at = span(i, 256)
            refs.sum[:, at] = refs.resid[:, at].astype(jnp.float32) + product(refs.mixed[...], w_out[:, at]) + refs.bias[2:3, at]

        over(D // 256, act)

    def norm_one():
        def act(i):
            at = span(i, ROW_BLOCK)
            y, normed, inv = norm_block(refs.sum[at], refs.bias[6:7], refs.bias[3:4])
            refs.n1[at], refs.inv1[at], refs.sum[at] = normed, inv, y
            refs.y_low[at] = y.astype(jnp.bfloat16)

        over(rows // ROW_BLOCK, act)
        waits[1]()

    def up(first, count):
        def act(i):
            at = span(first + i, 256)
            u = product(refs.y_low[...], w_up[:, at]) + refs.shifts[0:1, at]
            share = 0.5 + 0.5 * lax.erf(u * (0.5 ** 0.5))
            refs.a_low[:, at] = (u * share).astype(jnp.bfloat16)
            slope = share + u * jnp.exp(-0.5 * u * u) * ((2.0 * jnp.pi) ** -0.5)
            refs.slope[:, at] = slope.astype(jnp.bfloat16)

        over(count, act)

    def down():
        waits[2]()

        def act(i):
            at = span(i, 256)
            refs.sum[:, at] = refs.sum[:, at] + product(refs.a_low[...], w_down[:, at]) + refs.bias[4:5, at]

        over(D // 256, act)

    def norm_two():
        def act(i):
            at = span(i, ROW_BLOCK)
            z, normed, inv = norm_block(refs.sum[at], refs.bias[7:8], refs.bias[5:6])
            refs.n2[at], refs.inv2[at] = normed, inv
            if hasattr(refs, "z"):
                refs.z[at] = z
            refs.z_low[at] = z.astype(jnp.bfloat16)

        over(rows // ROW_BLOCK, act)

    quarter = hidden // 256 // 4
    return [out, norm_one] + [partial(up, k * quarter, quarter) for k in range(4)] + [down, norm_two]


def tail_ins(mixed, part, resid, vectors, shifts, weights):
    return {
        "generic": (mixed, IN_VMEM), "own_part": (part, ANYWHERE), "resid": (resid, IN_VMEM), "vectors": (vectors, IN_VMEM),
        "shifts": (shifts, IN_VMEM), "w_out": (weights[1], ANYWHERE), "w_up": (weights[2], ANYWHERE), "w_down": (weights[3], ANYWHERE),
    }


def tail_outs(rows, hidden):
    f32, low = jnp.float32, jnp.bfloat16
    return {
        "mixed": ((rows, D), low, IN_VMEM), "n1": ((rows, D), f32, IN_VMEM), "inv1": ((rows, 1), f32, IN_VMEM),
        "y_low": ((rows, D), low, IN_VMEM), "a_low": ((rows, hidden), low, IN_VMEM), "slope": ((rows, hidden), low, IN_VMEM),
        "n2": ((rows, D), f32, IN_VMEM), "inv2": ((rows, 1), f32, IN_VMEM), "z_low": ((rows, D), low, IN_VMEM),
    }


def tail_scratch(rows, hidden):
    low = jnp.bfloat16
    return {
        "sum": pltpu.VMEM((rows, D), jnp.float32), "v_out": pltpu.VMEM((D, D), low),
        "v_up": pltpu.VMEM((D, hidden), low), "v_down": pltpu.VMEM((hidden, D), low),
        "load": dma(3), "t_send": dma(), "t_recv": dma(HELPERS),
    }


def start_loads(refs):
    loads = [
        pltpu.make_async_copy(refs.w_out, refs.v_out, refs.load.at[0]),
        pltpu.make_async_copy(refs.w_up, refs.v_up, refs.load.at[1]),
        pltpu.make_async_copy(refs.w_down, refs.v_down, refs.load.at[2]),
    ]
    for copy in loads:
        copy.start()
    return [copy.wait for copy in loads]


def tail(mixed, part, resid, vectors, shifts, weights, next_weights, seq_count, depth, cid):
    rows, hidden = resid.shape[0], shifts.shape[1]
    pieces = layer_pieces(next_weights[0].shape[0], next_weights[3].shape[0], 0)
    gathering = Gathering(next_weights, pieces, seq_count, depth, (0,))
    sequence = Sequence(rows, seq_count, depth, mixed.dtype)

    def body(refs):
        waits = start_loads(refs)
        refs.mixed[...] = refs.generic[...]
        greet(("y", "x", "z"), depth, spread=True, collect=True)
        finish = to_first(refs.own_part, refs.mixed, refs.t_send, refs.t_recv)
        gathering.begin(refs)
        sequence.prepare(refs)
        refs.bias = refs.vectors.at[0]
        steps = [finish] + tail_steps(refs, refs.v_out, refs.v_up, refs.v_down, waits)

        def project_now():
            refs.bias = refs.vectors.at[1]
            project_and_send(refs, gathering, sequence, refs.z_low, 0)()

        at = TAIL_PLACES
        run_in_order(
            timed_events(gathering.jobs + sequence.jobs, at.arrivals)
            + list(zip(at.steps, steps, strict=True)) + [(at.project, project_now)]
        )
        sequence.end()
        gathering.end()

    outs = tail_outs(rows, hidden)
    outs.update(z=((rows, D), jnp.float32, IN_VMEM))
    got = call(
        body, "tail", cid,
        {**tail_ins(mixed, part, resid, vectors, shifts, weights), **gathering.ins()},
        {**outs, **sequence.outs(), **gathering.outs()},
        {**tail_scratch(rows, hidden), **sequence.scratch(), **gathering.scratch()},
    )
    return got, gathering.results(got)


def folded(block):
    return jnp.sum(block.reshape(-1, 8, block.shape[1]), axis=0)


def norm_block_back(grad, normed, inv_std, gain):
    scaled = grad * gain
    return (
        scaled
        - jnp.mean(scaled, axis=1, keepdims=True)
        - normed * jnp.mean(scaled * normed, axis=1, keepdims=True)
    ) * inv_std


def back_steps(refs, dz, w_down, w_up, w_out, waits):
    rows, hidden = refs.n2.shape[0], refs.slope.shape[1]
    zero = jnp.zeros((8, D), jnp.float32)

    def row(k, total):
        refs.totals[k : k + 1] = jnp.sum(total, axis=0, keepdims=True)

    def norm_two():
        def act(i, sums):
            at = span(i, ROW_BLOCK)
            grad, normed = dz(at), refs.n2[at]
            back = norm_block_back(grad, normed, refs.inv2[at], refs.bias[7:8])
            refs.work[at] = back
            refs.dr2_low[at] = back.astype(jnp.bfloat16)
            return sums[0] + folded(back), sums[1] + folded(grad), sums[2] + folded(grad * normed)

        sums = lax.fori_loop(0, rows // ROW_BLOCK, act, (zero,) * 3)
        row(4, sums[0]), row(5, sums[1]), row(7, sums[2])
        waits[0]()

    def down(first, count):
        def act(i):
            at = span(first + i, 256)
            du = product_nt(refs.dr2_low[...], w_down[at]) * refs.slope[:, at].astype(jnp.float32)
            refs.du_low[:, at] = du.astype(jnp.bfloat16)
            refs.hidden_totals[0:1, at] = jnp.sum(du, axis=0, keepdims=True)

        over(count, act)

    def up():
        waits[1]()

        def act(i):
            at = span(i, 256)
            refs.work[:, at] = refs.work[:, at] + product_nt(refs.du_low[...], w_up[at])

        over(D // 256, act)

    def norm_one():
        def act(i, sums):
            at = span(i, ROW_BLOCK)
            grad, normed = refs.work[at], refs.n1[at]
            back = norm_block_back(grad, normed, refs.inv1[at], refs.bias[6:7])
            refs.dr1[at] = back
            refs.dr1_low[at] = back.astype(jnp.bfloat16)
            return sums[0] + folded(back), sums[1] + folded(grad), sums[2] + folded(grad * normed)

        sums = lax.fori_loop(0, rows // ROW_BLOCK, act, (zero,) * 3)
        row(2, sums[0]), row(3, sums[1]), row(6, sums[2])

    def out():
        waits[2]()

        def act(i):
            at = span(i, 256)
            refs.cot[:, at] = product_nt(refs.dr1_low[...], w_out[at]).astype(jnp.bfloat16)

        over(D // 256, act)

    half = hidden // 256 // 2
    return [norm_two, partial(down, 0, half), partial(down, half, half), up, norm_one, out]


def back_outs(rows, hidden):
    f32, low = jnp.float32, jnp.bfloat16
    return {
        "dr2_low": ((rows, D), low, IN_VMEM), "du_low": ((rows, hidden), low, IN_VMEM), "dr1": ((rows, D), f32, IN_VMEM),
        "dr1_low": ((rows, D), low, IN_VMEM), "cot": ((rows, D), low, IN_VMEM), "totals": ((8, D), f32, IN_VMEM),
        "hidden_totals": ((1, hidden), f32, IN_VMEM), "part_cot": ((SHARE, D), low, ANYWHERE),
    }


def turn(mixed, part, resid, vectors, shifts, weights, d_out, depth, cid):
    rows, hidden = resid.shape[0], shifts.shape[1]

    def body(refs):
        waits = start_loads(refs)
        refs.mixed[...] = refs.generic[...]
        refs.bias = refs.vectors.at[1]
        greet((), depth, spread=True, collect=True)
        to_first(refs.own_part, refs.mixed, refs.t_send, refs.t_recv)()
        for step in tail_steps(refs, refs.v_out, refs.v_up, refs.v_down, waits):
            step()
        done = [lambda: None] * 3
        refs.totals[...] = jnp.zeros_like(refs.totals)
        for step in back_steps(
            refs, lambda at: refs.d_out[at].astype(jnp.float32), refs.v_down, refs.v_up, refs.v_out, done
        ):
            step()
        to_helpers(refs.cot, refs.part_cot, refs.give, refs.take)()

    return call(
        body, "turn", cid,
        {**tail_ins(mixed, part, resid, vectors, shifts, weights), "d_out": (d_out, IN_VMEM)},
        {**tail_outs(rows, hidden), **back_outs(rows, hidden)},
        {
            **tail_scratch(rows, hidden), "work": pltpu.VMEM((rows, D), jnp.float32), "give": dma(HELPERS), "take": dma(),
        },
    )


def chunked(shape):
    rows, columns = shape
    width = columns
    while rows * width > 24 * 1024 and width % 256 == 0:
        width //= 2
    if rows * width > 24 * 1024 and width % 384 == 0:
        width //= 3
    return width, columns // width


def total_of(own, kids, window):
    total = own[window].astype(jnp.float32)
    for ref, cond in kids:
        if cond is None:
            total = total + ref[window].astype(jnp.float32)
        else:
            total = total + lax.cond(
                cond,
                lambda ref=ref: ref[window].astype(jnp.float32),
                lambda total=total: jnp.zeros_like(total),
            )
    return total


def over_chunks(shape, act):
    if len(shape) == 3:
        size = shape[1] // 2

        def part(i, carry):
            act((i // 2, span(i % 2, size)))
            return carry

        lax.fori_loop(0, 2 * shape[0], part, 0)
        return
    width, count = chunked(shape)

    def step(i, carry):
        act((slice(None), pl.ds(pl.multiple_of(i * width, width), width)))
        return carry

    lax.fori_loop(0, count, step, 0)


def add_up(own, kids, into):
    def act(window):
        into[window] = total_of(own, kids, window).astype(into.dtype)

    over_chunks(into.shape, act)


def write_total(target):
    def finish(own, kids):
        def act(window):
            target[window] = total_of(own, kids, window).astype(target.dtype)

        over_chunks(target.shape, act)

    return finish


def weight_grad(left, right, into, first=0):
    share = into.shape[1]
    count = 384 // share

    def act(i):
        across = into.shape[2] // 256
        rows, at = i // across, span(i % across, 256)
        acc = product_tn(left[:, span(rows, 384)], right[:, span(i % across, 256, first)])
        for k in range(count):
            into[rows * count + k, :, at] = acc[k * share : (k + 1) * share].astype(into.dtype)

    over(left.shape[1] // 384 * (into.shape[2] // 256), act)


class Sums:
    def __init__(self, tag, pieces, depth):
        self.tag, self.pieces, self.depth = tag, pieces, depth

    def name(self, what, k):
        return "%s_%s%d" % (self.tag, what, k)

    def scratch(self):
        made = {}
        for k, (_, shape, _, order, dtype) in enumerate(self.pieces):
            edges = Reduce.slots(order, self.depth)[1]
            made[self.name("box", k)] = pltpu.VMEM((edges,) + shape, dtype)
            made[self.name("send", k)] = dma(2 * len(offsets(order, self.depth)))
            made[self.name("recv", k)] = dma(edges)
        return made

    def prepare(self, refs):
        self.jobs = []
        for k, (source, _, target, order, _) in enumerate(self.pieces):
            box, send, recv = (getattr(refs, self.name(what, k)) for what in ("box", "send", "recv"))
            job = Reduce(partial(source, refs), box, order, self.depth, send, recv)
            self.jobs.append((job, target(refs)))

    def start(self, k):
        job, _ = self.jobs[k]
        for t in job.marks:
            job.start(t)

    def timed(self, places):
        timed = []
        for k, ((job, finish), at) in enumerate(zip(self.jobs, places, strict=True)):
            timed.append((at[0], partial(self.start, k)))
            acts = [partial(job.handle, t, add_up, finish) for t in job.marks]
            timed += zip(at[1:], acts, strict=True)
        return timed

    def end(self):
        for job, _ in self.jobs:
            job.drain()


def weight_sums(windows, depth, n_dev, dtypes):
    number = number_in(depth)

    def piece(which, row, rows, column, columns_, order):
        window = (pl.ds(row, rows), pl.ds(column, columns_))
        return (
            lambda refs, p: getattr(refs, "grad%d" % which).at[(number(p),) + window],
            (rows, columns_),
            lambda refs: write_total(getattr(refs, "owned%d" % which).at[window]),
            order,
            dtypes[which],
        )

    return Sums("w", [piece(*w) for w in windows], depth)


def sum_rows(dk, dv, dq, part_dq, held, grads, seq_count, depth, cid):
    rows, hidden, n_dev = dq.shape[0], grads.du_low.shape[1], seq_count * depth
    low, f32 = dk.dtype, jnp.float32
    share, count = D // n_dev, PAIRS // 2

    def piece(i):
        window = pl.ds(i % 2 * count, count)

        def target(refs):
            def finish(own, kids):
                def act(at):
                    lanes = pl.ds(pl.multiple_of((PAIRS + i * count + at[0]) * WIDE, WIDE), WIDE)
                    refs.proj[at[1], lanes] = total_of(own, kids, at).astype(low)

                over_chunks((count, rows, WIDE), act)

            return finish

        return (
            lambda refs, p: (refs.dk, refs.dv)[i // 2].at[number_in_sequence(p), window],
            (count, rows, WIDE),
            target,
            (X_Y, Y_X)[i % 2],
            low,
        )

    by_rows = Sums("r", [piece(i) for i in range(4)], depth)
    windows = [(1, 0, share, 0, D, X_Y_Z), (2, 0, share, 0, hidden // 2, Y_X_Z)]
    by_weights = weight_sums(windows, depth, n_dev, {1: low, 2: low})

    def body(refs):
        refs.proj[:, 0:D] = refs.dq[...]
        greet(("y", "x", "z"), depth, collect=True)
        by_rows.prepare(refs)
        by_weights.prepare(refs)
        ends = [to_first(refs.part, refs.proj.at[:, pl.ds(0, D)], refs.t_send, refs.t_recv)]
        at = ROWS_PLACES
        run_in_order(
            by_rows.timed(at.rows) + by_weights.timed(at.weights)
            + [
                (at.grads[0], lambda: weight_grad(refs.mixed, refs.dr1_low, refs.grad1)),
                (at.grads[1], lambda: weight_grad(refs.y_low, refs.du_low, refs.grad2)),
                (at.collect, ends[0]),
            ]
        )
        by_rows.end()
        by_weights.end()

        def act(i, sums):
            at = span(i, ROW_BLOCK)
            return tuple(
                total + folded(refs.proj[at, pl.ds(first, D)].astype(f32)) for total, first in zip(sums, (0, 2 * D))
            )

        zero = jnp.zeros((8, D), f32)
        sums = lax.fori_loop(0, rows // ROW_BLOCK, act, (zero, zero))
        refs.totals[...] = jnp.zeros_like(refs.totals)
        for k in range(2):
            refs.totals[k : k + 1] = jnp.sum(sums[k], axis=0, keepdims=True)

    return call(
        body, "sum_rows", cid,
        dict(
            dk=(dk, IN_VMEM), dv=(dv, IN_VMEM), dq=(dq, IN_VMEM), part=(part_dq, ANYWHERE),
            mixed=(held.mixed, IN_VMEM), y_low=(held.y_low, IN_VMEM), dr1_low=(grads.dr1_low, IN_VMEM),
            du_low=(grads.du_low, IN_VMEM),
        ),
        dict(
            proj=((rows, 3 * D), low, IN_VMEM), totals=((8, D), f32, IN_VMEM), owned1=((share, D), f32, IN_VMEM),
            owned2=((share, hidden // 2), f32, IN_VMEM),
        ),
        {
            **dict(
                grad1=pltpu.VMEM((n_dev, share, D), low), grad2=pltpu.VMEM((n_dev, share, hidden // 2), low),
                t_send=dma(), t_recv=dma(HELPERS),
            ),
            **by_rows.scratch(), **by_weights.scratch(),
        },
    )


def sum_weights(held, low_in, proj, vectors, w_qkv, small, below, n_dev, depth, cid):
    rows, hidden = proj.shape[0], held.du_low.shape[1]
    low, f32 = jnp.bfloat16, jnp.float32
    share, tall = D // n_dev, hidden // n_dev
    shapes = {0: (share, 3 * D), 2: (share, hidden // 2), 3: (tall, D)}
    cut = tall * 2 // 3
    windows = [
        (3, 0, cut, 0, D, Z_X_Y),
        (3, cut, tall - cut, 0, D, Z_Y_X),
        (2, 0, share, 0, hidden // 2, Y_X_Z),
        (0, 0, share, 0, 3 * D, Z_Y_X),
    ]
    ins = {k: (getattr(held, k), IN_VMEM) for k in ("y_low", "du_low", "a_low", "dr2_low", "dr1")}
    ins = {"up_" + k: v for k, v in ins.items()}
    ins.update(low_in=(low_in, IN_VMEM), proj=(proj, IN_VMEM), w_qkv=(w_qkv, ANYWHERE))
    outs = {"owned%d" % i: (s, f32, IN_VMEM) for i, s in shapes.items()}
    scratch = {"grad%d" % i: pltpu.VMEM((n_dev,) + s, low) for i, s in shapes.items()}
    if small is not None:
        windows.append((4, 0, small.shape[1], 0, small.shape[2], Z_Y_X))
        ins.update(grad4=(small, IN_VMEM))
        outs.update(owned4=(small.shape[1:], f32, IN_VMEM))
    by_weights = weight_sums(windows, depth, n_dev, {0: low, 2: low, 3: low, 4: f32})
    scratch.update(by_weights.scratch())
    scratch.update(load=dma(4), wide=pltpu.VMEM((D, hidden), low))
    if below is not None:
        below_weights, below_held = below
        ins.update({k: (getattr(below_held, k), IN_VMEM) for k in ("n1", "inv1", "n2", "inv2", "slope")})
        ins.update(
            vectors=(vectors, IN_VMEM), w_out=(below_weights[1], ANYWHERE), w_up=(below_weights[2], ANYWHERE),
            w_down=(below_weights[3], ANYWHERE),
        )
        outs.update(back_outs(rows, hidden))
        scratch.update(
            tall=pltpu.VMEM((hidden, D), low), work=pltpu.VMEM((rows, D), f32), give=dma(HELPERS), take=dma()
        )
    outs.update(dx=((rows, D), f32, IN_VMEM))

    def body(refs):
        v_qkv = refs.wide.at[:, pl.ds(0, 3 * D)]
        load_qkv = pltpu.make_async_copy(refs.w_qkv, v_qkv, refs.load.at[0])
        load_qkv.start()
        if below is not None:
            refs.bias = refs.vectors.at[0]
            refs.totals[...] = jnp.zeros_like(refs.totals)
            load_down = pltpu.make_async_copy(refs.w_down, refs.tall, refs.load.at[1])
            load_down.start()
            load_up = pltpu.make_async_copy(refs.w_up, refs.wide, refs.load.at[2])
            load_out = pltpu.make_async_copy(refs.w_out, refs.tall.at[pl.ds(0, D)], refs.load.at[3])
        greet(("y", "x", "z"), depth, spread=below is not None)
        by_weights.prepare(refs)
        def dx():
            load_qkv.wait()

            def act(i):
                at = span(i, 256)
                refs.dx[:, at] = refs.up_dr1[:, at] + product_nt(refs.proj[...], v_qkv[at])

            over(D // 256, act)
            if below is not None:
                load_up.start()

        steps = [dx]
        if below is not None:

            def up_ready():
                load_out.start()
                load_up.wait()

            steps += back_steps(
                refs, lambda at: refs.dx[at], refs.tall, refs.wide, refs.tall, [load_down.wait, up_ready, load_out.wait]
            )
            ends = []
            steps.append(lambda: ends.append(to_helpers(refs.cot, refs.part_cot, refs.give, refs.take)))
        at = LAST_PLACES if below is None else BELOW_PLACES
        run_in_order(
            by_weights.timed(at.weights)
            + [
                (at.grads[0], lambda: weight_grad(refs.up_a_low, refs.up_dr2_low, refs.grad3)),
                (at.grads[1], lambda: weight_grad(refs.up_y_low, refs.up_du_low, refs.grad2, hidden // 2)),
                (at.grads[2], lambda: weight_grad(refs.low_in, refs.proj, refs.grad0)),
            ]
            + list(zip(at.steps, steps, strict=True))
        )
        by_weights.end()
        if below is not None:
            ends[0]()

    return call(body, "sum_weights", cid, ins, outs, scratch)


def norm_rows(resid, gain, shift):
    center = resid - jnp.mean(resid, axis=-1, keepdims=True)
    inv_std = lax.rsqrt(jnp.mean(center * center, axis=-1, keepdims=True) + layer_eps)
    normed = center * inv_std
    return (normed * gain + shift, normed, inv_std)


def norm_back(grad_rows, normed, inv_std, gain):
    scaled = grad_rows * gain
    return (
        scaled
        - jnp.mean(scaled, axis=-1, keepdims=True)
        - normed * jnp.mean(scaled * normed, axis=-1, keepdims=True)
    ) * inv_std


def dot32(a, b):
    return jnp.dot(a, b, preferred_element_type=jnp.float32)


def small_vectors(small, n_dev):
    small = small.astype(jnp.float32).T
    vectors = jnp.concatenate(
        [small[: 6 * L].reshape(L, 6, D), small[6 * L : 8 * L].reshape(L, 2, D)], axis=1
    )
    hidden_shifts = small[8 * L : 12 * L].reshape(L, 4, n_dev, D // n_dev)
    return vectors, jnp.swapaxes(hidden_shifts, 1, 2).reshape(L, -1)


def shut_keys(segs_all, segments, first, blocks_here):
    length = segs_all.shape[0]
    padding = jnp.full((BLK,), -1, jnp.int32)
    segs_all = jnp.concatenate([padding, segs_all, padding]).reshape(-1, BLK)
    segs_near = lax.dynamic_slice_in_dim(segs_all, first, blocks_here + 2, axis=0)
    seg_window = jnp.concatenate([segs_near[j : j + blocks_here] for j in range(3)], axis=1)
    spot = (first - 1 + jnp.arange(blocks_here)[:, None]) * BLK + jnp.arange(3 * BLK)[None, :]
    inside = (spot >= SHARED) & (spot < length)
    own = segments.reshape(blocks_here, 1, BLK)
    allowed = inside[:, :, None] & (seg_window[:, :, None] == jnp.concatenate([own, own], axis=2))
    return jnp.where(allowed, 0.0, masked_score)


def small_by_owner(vectors, hidden, n_dev):
    rows = jnp.moveaxis(vectors.reshape(8, n_dev, -1), 1, 0)
    rows = jnp.concatenate([rows, hidden.reshape(n_dev, 8, -1)], axis=2)
    return jnp.pad(rows, ((0, 0), (0, 0), (0, 128 - rows.shape[2])))


def small_outputs(narrow, piece, hidden):
    return (
        narrow[:, 6:8, :piece],
        narrow[:, 0:6, :piece],
        narrow[:, :, piece : piece + hidden // 8].reshape(L, -1),
    )


def share_of(rows):
    first = lax.all_gather(rows[:SHARED], SEQ, axis=0)[0]
    own = jnp.minimum(lax.axis_index(SEQ), HELPERS - 1) * SHARE
    return lax.dynamic_slice_in_dim(first, own, SHARE, axis=0)


def rows_of_all(kv, queries):
    kv = jnp.moveaxis(kv.reshape(-1, 2 * PAIRS, WIDE), 1, 0)
    return lax.all_gather(kv, SEQ, axis=0), share_of(queries)


def with_shared_rows(part, rows):
    first = lax.all_gather(part, SEQ, axis=0)[:HELPERS].reshape(SHARED, D)
    head_rows = jnp.where(lax.axis_index(SEQ) == 0, first.astype(rows.dtype), rows[:SHARED])
    return jnp.concatenate([head_rows, rows[SHARED:]], axis=0)


def on_any_slice(
    layer_input, segments, rand_blocks, w_qkv, w_out, w_up, w_down, gains, biases, up_bias, d_out
):
    seq_count, depth = lax.axis_size(SEQ), lax.axis_size(BATCH)
    n_dev = seq_count * depth
    own_index = lax.axis_index(SEQ)
    rows = layer_input.shape[1]
    blocks_here, length = rows // BLK, rows * seq_count
    picks = rand_blocks.reshape(-1)
    first = (own_index * blocks_here).reshape(1)

    piece = D // n_dev
    small = jnp.concatenate(
        [biases.reshape(-1, piece), gains.reshape(-1, piece), up_bias.reshape(-1, piece)], axis=0
    ).T
    small = lax.all_gather(small, (SEQ, BATCH), axis=0, tiled=True)
    segs_all = lax.all_gather(segments[0], SEQ, axis=0, tiled=True)
    weights = [
        [lax.all_gather(w[layer], (SEQ, BATCH), axis=0, tiled=True) for w in (w_qkv, w_out, w_up, w_down)]
        for layer in range(L)
    ]
    vectors, hidden_shifts = small_vectors(small, n_dev)
    shut = shut_keys(segs_all, segments, first[0], blocks_here)

    resid = layer_input[0].astype(jnp.float32)
    low = layer_input[0]
    saved = []
    for layer in range(L):
        mat_qkv, mat_out, mat_up, mat_down = weights[layer]
        bias = vectors[layer]
        proj = dot32(low, mat_qkv)
        queries = (proj[:, :D] + bias[0]).astype(jnp.bfloat16)
        kv = jnp.concatenate([proj[:, D : 2 * D], proj[:, 2 * D :] + bias[1]], axis=1).astype(jnp.bfloat16)
        kv_all, part = rows_of_all(kv, queries)
        mixed, part_mixed, *logs = attend(picks, first, queries, kv_all, shut, part)
        mixed = with_shared_rows(part_mixed, mixed)
        resid_one = resid + dot32(mixed, mat_out) + bias[2]
        middle, normed_one, inv_one = norm_rows(resid_one, bias[6], bias[3])
        middle_low = middle.astype(jnp.bfloat16)
        hidden = dot32(middle_low, mat_up) + hidden_shifts[layer]
        active = jax.nn.gelu(hidden, approximate=False).astype(jnp.bfloat16)
        resid_two = middle + dot32(active, mat_down) + bias[4]
        result, normed_two, inv_two = norm_rows(resid_two, bias[7], bias[5])
        saved.append(
            (low, queries, kv_all, part, logs, mixed, normed_one, inv_one, middle_low, hidden, active, normed_two, inv_two)
        )
        resid = result
        low = resid.astype(jnp.bfloat16)

    grad = d_out[0].astype(jnp.float32)
    owned = [None] * L
    for layer in reversed(range(L)):
        (low_in, queries, kv_all, part, logs, mixed, normed_one, inv_one, middle_low, hidden, active, normed_two, inv_two) = saved[layer]
        mat_qkv, mat_out, mat_up, mat_down = weights[layer]
        bias = vectors[layer]
        gain_two_grad = jnp.sum(grad * normed_two, axis=0)
        shift_two_grad = jnp.sum(grad, axis=0)
        grad_two = norm_back(grad, normed_two, inv_two, bias[7])
        grad_two_low = grad_two.astype(jnp.bfloat16)
        down_grad = product_tn(active, grad_two_low)
        active_grad = product_nt(grad_two_low, mat_down)
        hidden_grad = jax.vjp(partial(jax.nn.gelu, approximate=False), hidden)[1](active_grad)[0]
        hidden_grad_low = hidden_grad.astype(jnp.bfloat16)
        up_grad = product_tn(middle_low, hidden_grad_low)
        middle_grad = grad_two + product_nt(hidden_grad_low, mat_up)
        gain_one_grad = jnp.sum(middle_grad * normed_one, axis=0)
        shift_one_grad = jnp.sum(middle_grad, axis=0)
        grad_one = norm_back(middle_grad, normed_one, inv_one, bias[6])
        grad_one_low = grad_one.astype(jnp.bfloat16)
        out_grad = product_tn(mixed, grad_one_low)
        cot = product_nt(grad_one_low, mat_out).astype(jnp.bfloat16)
        part_cot = share_of(cot)
        part_cot = jnp.where(own_index < HELPERS, part_cot, 0)
        dq, dk, dv, part_dq = attend_back(picks, first, queries, kv_all, shut, cot, part, part_cot, *logs)
        dq = with_shared_rows(part_dq, dq)
        dkv = jnp.concatenate([dk, dv], axis=1).astype(jnp.float32)
        dkv = lax.psum_scatter(dkv, SEQ, scatter_dimension=0)
        dkv = jnp.moveaxis(dkv, 0, 1).reshape(rows, 2 * D)
        proj_grad = jnp.concatenate([dq, dkv.astype(jnp.bfloat16)], axis=1)
        qkv_grad = product_tn(low_in, proj_grad)
        small_rows = jnp.stack(
            [
                jnp.sum(dq.astype(jnp.float32), axis=0),
                jnp.sum(dkv[:, D:], axis=0),
                jnp.sum(grad_one, axis=0),
                shift_one_grad,
                jnp.sum(grad_two, axis=0),
                shift_two_grad,
                gain_one_grad,
                gain_two_grad,
            ]
        )
        small_rows = small_by_owner(small_rows, jnp.sum(hidden_grad, axis=0), n_dev)
        owned[layer] = [
            lax.psum_scatter(a, (SEQ, BATCH), scatter_dimension=0, tiled=True)
            for a in (qkv_grad, out_grad, up_grad, down_grad, small_rows)
        ]
        owned[layer][4] = owned[layer][4][0]
        grad = grad_one + product_nt(proj_grad, mat_qkv)
    stacked = [jnp.stack([owned[layer][i] for layer in range(L)]) for i in range(5)]
    return (low[None], grad[None], *stacked[:4], *small_outputs(stacked[4], piece, up_bias.shape[1]))


def on_pairs(
    layer_input, segments, rand_blocks, w_qkv, w_out, w_up, w_down, gains, biases, up_bias, d_out
):
    seq_count, depth = lax.axis_size(SEQ), lax.axis_size(BATCH)
    n_dev = seq_count * depth
    rows, hidden = layer_input.shape[1], up_bias.shape[1] * n_dev
    blocks_here = rows // BLK
    picks = rand_blocks.reshape(-1)
    first = (lax.axis_index(SEQ) * blocks_here).reshape(1)
    piece = D // n_dev

    small = jnp.concatenate(
        [biases.reshape(-1, piece), gains.reshape(-1, piece), up_bias.reshape(-1, piece)], axis=0
    ).T
    small = jnp.pad(small, ((0, 0), (0, 128 - small.shape[1])))
    segs = jnp.pad(segments.reshape(-1, 128), ((0, 8 - rows // 128), (0, 0)))

    def flat(slabs):
        return [w.reshape(-1, w.shape[2]) for w in slabs]

    def attention(got):
        return attend(picks, first, got.q, got.every, shut, got.part)

    def attention_back(got, back, logs):
        return attend_back(
            picks, first, got.q, got.every, shut, back.cot, got.part, back.part_cot, *logs
        )

    x = layer_input[0]
    layers = [[w[layer] for w in (w_qkv, w_out, w_up, w_down)] for layer in range(L)]
    head_one, segs_all, weights_one = first_head(x, small, segs, layers[0], seq_count, depth, 0)
    weights_one = flat(weights_one)
    vectors = head_one.vectors
    shifts = head_one.table.reshape(L, 4, n_dev, piece)
    shifts = jnp.swapaxes(shifts, 1, 2).reshape(L, 1, hidden)
    shut = shut_keys(segs_all[:, : rows // 128].reshape(-1), segments, first[0], blocks_here)
    mixed, part, *logs_one = attention(head_one)
    rows_one, weights_two = tail(
        mixed, part, x, vectors, shifts[0], weights_one, layers[1], seq_count, depth, 1
    )
    weights_two = flat(weights_two)
    middle = rows_one.z_low
    mixed, part, *logs_two = attention(rows_one)
    rows_two = turn(mixed, part, rows_one.z, vectors, shifts[1], weights_two, d_out[0], depth, 2)
    dq, dk, dv, part = attention_back(rows_one, rows_two, logs_two)
    sums_two = sum_rows(dk, dv, dq, part, rows_two, rows_two, seq_count, depth, 3)
    back_one = sum_weights(
        rows_two, middle, sums_two.proj, vectors, weights_two[0], None, (weights_one, rows_one), n_dev, depth, 4
    )
    dq, dk, dv, part = attention_back(head_one, back_one, logs_one)
    sums_one = sum_rows(dk, dv, dq, part, rows_one, back_one, seq_count, depth, 5)
    small = jnp.concatenate(
        [
            small_by_owner(back.totals + sums.totals, back.hidden_totals[0], n_dev)
            for back, sums in ((back_one, sums_one), (rows_two, sums_two))
        ],
        axis=1,
    )
    last = sum_weights(
        SimpleNamespace(**{**vars(rows_one), **vars(back_one)}),
        x, sums_one.proj, None, weights_one[0], small, None, n_dev, depth, 6,
    )
    by_layer = [(sums_one, last), (sums_two, back_one)]
    stacked = [
        jnp.stack([one.owned0 for _, one in by_layer]),
        jnp.stack([one.owned1 for one, _ in by_layer]),
        jnp.stack([jnp.concatenate([one.owned2, two.owned2], axis=1) for one, two in by_layer]),
        jnp.stack([one.owned3 for _, one in by_layer]),
    ]
    return (
        rows_two.z_low[None],
        last.dx[None],
        *stacked,
        *small_outputs(last.owned4.reshape(L, 8, 128), piece, up_bias.shape[1]),
    )


def solution(mesh):
    placed = (
        P(BATCH, SEQ, None),
        P(BATCH, SEQ),
        P(BATCH, SEQ, None, None),
        P(None, (SEQ, BATCH), None),
        P(None, (SEQ, BATCH), None),
        P(None, (SEQ, BATCH), None),
        P(None, (SEQ, BATCH), None),
        P(None, None, (SEQ, BATCH)),
        P(None, None, (SEQ, BATCH)),
        P(None, (SEQ, BATCH)),
        P(BATCH, SEQ, None),
    )
    return jax.shard_map(
        on_pairs if mesh.shape[SEQ] == 8 and mesh.shape[BATCH] == 4 else on_any_slice,
        mesh=mesh,
        in_specs=placed,
        out_specs=(
            P(BATCH, SEQ, None),
            P(BATCH, SEQ, None),
            P(None, (SEQ, BATCH), None),
            P(None, (SEQ, BATCH), None),
            P(None, (SEQ, BATCH), None),
            P(None, (SEQ, BATCH), None),
            P(None, None, (SEQ, BATCH)),
            P(None, None, (SEQ, BATCH)),
            P(None, (SEQ, BATCH)),
        ),
        check_vma=False,
    )
```

time: 723 us -> 563 us (0.78)
  matrix products: 89.6 us -> 0 us
  other arithmetic: 36.9 us -> 10.9 us
  Pallas kernels: 547 us -> 524 us
  local copies, waits for them, and re-layouts: 38.5 us -> 19.5 us
    dot_general x24 -> x0, matrix products: 89.6 us -> none  [the longest x8 38.7 us: dot32(): return jnp.dot(a, b, preferred_element_type=jnp.float32)]
    pallas_call x2, Pallas kernels: 76.7 us -> 43.8 us  [attend_back(): pl.pallas_call(attend_back_kernel, grid_spec=pltpu.PrefetchScalarGridSpec...]
    pallas_call x14 -> x7, Pallas kernels: 424 us -> 453 us  [call(): pl.pallas_call(lambda *refs: body(SimpleNamespace(**dict(zip(names, refs)...]
    pallas_call x2, Pallas kernels: 46.7 us -> 26.7 us  [attend(): pl.pallas_call(attend_kernel, grid_spec=pltpu.PrefetchScalarGridSpec(num_...]
    another operation x18 -> x2, local copies, waits for them, and re-layouts: 18.1 us -> 0.28 us  [small_by_owner(): rows = jnp.concatenate([rows, hidden.reshape(n_dev, 8, -1)], axis=2)]
    reduce_sum x14 -> x0, other arithmetic: 10.1 us -> none  [the longest x2 2.59 us: on_device(): jnp.sum(grad_two, axis=0)]
where the time goes in v3:
time: 563 us; the launch traced here: 555 us
  Pallas kernels  524 us (93%)
  local copies, waits for them, and re-layouts  19.5 us (3%)
  other arithmetic  10.9 us (2%)
    pallas_call x7, Pallas kernels, call(): pl.pallas_call(lambda *refs: body(SimpleNamespace(**dict(zip(names, refs)...  453 us
    pallas_call x2, Pallas kernels, attend_back(): pl.pallas_call(attend_back_kernel, grid_spec=pltpu.PrefetchScalarGridSpec...  43.8 us
    pallas_call x2, Pallas kernels, attend(): pl.pallas_call(attend_kernel, grid_spec=pltpu.PrefetchScalarGridSpec(num_...  26.7 us

profile of v3, /device:TPU:0, one launch (start us, length us, event | category | flops | bytes accessed | tf_op | source)
XLA Modules:
  0.0 555.4 jit_solution(8572688611206379238)
XLA Ops:
  0.7 1.7 slice_bitcast_fusion
  2.4 1.7 slice_bitcast_fusion.1
  4.1 1.6 slice_bitcast_fusion.4
  5.7 1.4 slice_bitcast_fusion.6
  7.1 0.7 copy.25
  7.9 0.7 reshape.124
  8.8 0.8 copy.27
  10.2 1.3 pad.16.refs_2_
  11.5 97.8 %first_head.1 = (f32[2,8,768]{2,1,0:T(8,128)}, f32[8,768]{1,0:T(8,128)}, bf16[256,768]{1,0:T(8,128)(2,1)}, bf16[8,12,256,128]{3,2,1,0:T(8,128)(2,1)}, bf16[16,76...) custom-call(bf16[256,768]{1,0:T(8,128)(2,1)} %bitcast.63, ...), custom_call_target="tpu_custom_call" | custom-call | tf_op jit(solution)/shard_map/first_head/pallas_call | solution.py:607
  109.3 0.8 slice.57
  110.9 1.3 reduce.9
  112.4 1.0 and_select_fusion.shut_ref
  114.2 13.4 %attend.2 = (bf16[256,768]{1,0:T(8,128)(2,1)}, bf16[16,768]{1,0:T(8,128)(2,1)}, f32[6,4,128]{2,1,0:T(4,128)}, f32[6,1,32]{2,1,0:T(1,128)}) custom-call(s32[144]{0:T(256)} %reshape.120.picks_ref, s32[1]{0:T(128)} %bitcast.first_ref, bf16[256,768]{1,0:T(8,128)(2,1)} %get-tuple-element.88.q_ref, bf16[8,12,256,128]{3,2,1,0:T(8,128)(2,1)} %get-tuple-element.89.k_ref.v_ref, ...), custom_call_target="tpu_custom_call" | custom-call | tf_op jit(solution)/shard_map/attend/pallas_call | solution.py:499
  127.8 0.7 squeeze.41.refs_4_
  128.5 91.0 %tail.1 = (bf16[256,768]{1,0:T(8,128)(2,1)}, f32[256,768]{1,0:T(8,128)}, f32[256,1]{1,0:T(8,128)}, bf16[256,768]{1,0:T(8,128)(2,1)}, bf16[256,3072]{1,0:T(8,128)...) custom-call(bf16[256,768]{1,0:T(8,128)(2,1)} %get-tuple-element.92.r, ...), custom_call_target="tpu_custom_call" | custom-call | tf_op jit(solution)/shard_map/tail/pallas_call | solution.py:607
  219.5 13.3 %attend.3 = (bf16[256,768]{1,0:T(8,128)(2,1)}, bf16[16,768]{1,0:T(8,128)(2,1)}, f32[6,4,128]{2,1,0:T(4,128)}, f32[6,1,32]{2,1,0:T(1,128)}) custom-call(s32[144]{0:T(256)} %reshape.120.picks_ref, s32[1]{0:T(128)} %bitcast.first_ref, bf16[256,768]{1,0:T(8,128)(2,1)} %get-tuple-element.99.q_ref, bf16[8,12,256,128]{3,2,1,0:T(8,128)(2,1)} %get-tuple-element.100.k_ref.v_ref, ...), custom_call_target="tpu_custom_call" | custom-call | tf_op jit(solution)/shard_map/attend/pallas_call | solution.py:499
  232.9 0.7 squeeze.46.refs_4_
  233.6 29.2 %turn.1 = (bf16[256,768]{1,0:T(8,128)(2,1)}, f32[256,768]{1,0:T(8,128)}, f32[256,1]{1,0:T(8,128)}, bf16[256,768]{1,0:T(8,128)(2,1)}, bf16[256,3072]{1,0:T(8,128)...) custom-call(bf16[256,768]{1,0:T(8,128)(2,1)} %get-tuple-element.102., ...), custom_call_target="tpu_custom_call" | custom-call | tf_op jit(solution)/shard_map/turn/pallas_call | solution.py:607
  262.8 21.9 %attend_back.2 = (bf16[256,768]{1,0:T(8,128)(2,1)}, bf16[8,6,256,128]{3,2,1,0:T(8,128)(2,1)}, bf16[8,6,256,128]{3,2,1,0:T(8,128)(2,1)}, bf16[16,768]{1,0:T(8,128)(2,1)}) custom-call(s32[144]{0:T(256)} %reshape.120.picks_ref, s32[1]{0:T(128)} %bitcast.first_ref, bf16[256,768]{1,0:T(8,128)(2,1)} %get-tuple-element.99.q_ref, ...), custom_call_target="tpu_custom_call" | custom-call | tf_op jit(solution)/shard_map/attend_back/pallas_call | solution.py:579
  284.7 51.1 %sum_rows.2 = (bf16[256,2304]{1,0:T(8,128)(2,1)}, f32[8,768]{1,0:T(8,128)}, f32[24,768]{1,0:T(8,128)}, f32[24,1536]{1,0:T(8,128)}) custom-call(bf16[8,6,256,128]{3,2,1,0:T(8,128)(2,1)} %get-tuple-element.120.refs_0_, bf16[8,6,256,128]{3,2,1,0:T(8,128)(2,1)} %get-tuple-element.121.refs_1_, bf16[256,768]{1,0:T(8,128)(2,1)} %get-tuple-element.122.refs_2_, ...), custom_call_target="tpu_custom_call" | custom-call | tf_op jit(solution)/shard_map/sum_rows/pallas_call | solution.py:607
  335.8 69.4 %sum_weights.2 = (f32[24,2304]{1,0:T(8,128)}, f32[24,1536]{1,0:T(8,128)}, f32[96,768]{1,0:T(8,128)}, bf16[256,768]{1,0:T(8,128)(2,1)}, bf16[256,3072]{1,0:T(8,12...) custom-call(bf16[256,768]{1,0:T(8,128)(2,1)} %get-tuple-element.110., ...), custom_call_target="tpu_custom_call" | custom-call | tf_op jit(solution)/shard_map/sum_weights/pallas_call | solution.py:607
  405.2 21.9 %attend_back.3 = (bf16[256,768]{1,0:T(8,128)(2,1)}, bf16[8,6,256,128]{3,2,1,0:T(8,128)(2,1)}, bf16[8,6,256,128]{3,2,1,0:T(8,128)(2,1)}, bf16[16,768]{1,0:T(8,128)(2,1)}) custom-call(s32[144]{0:T(256)} %reshape.120.picks_ref, s32[1]{0:T(128)} %bitcast.first_ref, bf16[256,768]{1,0:T(8,128)(2,1)} %get-tuple-element.88.q_ref, ...), custom_call_target="tpu_custom_call" | custom-call | tf_op jit(solution)/shard_map/attend_back/pallas_call | solution.py:579
  427.2 46.2 %sum_rows.3 = (bf16[256,2304]{1,0:T(8,128)(2,1)}, f32[8,768]{1,0:T(8,128)}, f32[24,768]{1,0:T(8,128)}, f32[24,1536]{1,0:T(8,128)}) custom-call(bf16[8,6,256,128]{3,2,1,0:T(8,128)(2,1)} %get-tuple-element.141.refs_0_, bf16[8,6,256,128]{3,2,1,0:T(8,128)(2,1)} %get-tuple-element.142.refs_1_, bf16[256,768]{1,0:T(8,128)(2,1)} %get-tuple-element.143.refs_2_, ...), custom_call_target="tpu_custom_call" | custom-call | tf_op jit(solution)/shard_map/sum_rows/pallas_call | solution.py:607
  473.4 0.7 add.52
  476.9 0.7 pad_maximum_fusion.3.refs_8_
  477.6 68.4 %sum_weights.3 = (f32[24,2304]{1,0:T(8,128)}, f32[24,1536]{1,0:T(8,128)}, f32[96,768]{1,0:T(8,128)}, f32[16,128]{1,0:T(8,128)}, f32[256,768]{1,0:T(8,128)}) custom-call(bf16[256,768]{1,0:T(8,128)(2,1)} %get-tuple-element.109.refs_5_.refs_0_, bf16[256,3072]{1,0:T(8,128)(2,1)} %get-tuple-element.133.refs_7_.refs_1_, ...), custom_call_target="tpu_custom_call" | custom-call | tf_op jit(solution)/shard_map/sum_weights/pallas_call | solution.py:607
  546.2 1.9 pad_maximum_fusion.1
  548.1 0.9 maximum_bitcast_fusion
  549.1 0.9 pad_maximum_fusion
  550.6 0.8 pad_maximum_fusion.2
  553.3 0.7 copy.41
  554.1 0.9 copy.42
  (75 shorter events, 8.2 us)
Async XLA Ops:
  0.6 112.8 %copy-start.17 = (s32[1,4,12,3]{2,1,3,0:T(4,128)S(1)}, s32[1,4,12,3]{2,1,3,0:T(4,128)}, u32[]{:S(2)}) copy-start(s32[1,4,12,3]{2,1,3,0:T(4,128)} %param.13) | copy-start | bytes 1732
  114.2 13.4 %copy-start.11 = (f32[8,768]{1,0:T(8,128)S(1)}, f32[8,768]{1,0:T(8,128)}, u32[]{:S(2)}) copy-start(f32[8,768]{1,0:T(8,128)} %get-tuple-element.95) | copy-start | bytes 73732
  427.1 46.2 %copy-start.14 = (f32[8,768]{1,0:T(8,128)S(1)}, f32[8,768]{1,0:T(8,128)}, u32[]{:S(2)}) copy-start(f32[8,768]{1,0:T(8,128)} %get-tuple-element.149) | copy-start | bytes 73732
  427.2 47.2 %copy-start.12 = (f32[8,768]{1,0:T(8,128)S(1)}, f32[8,768]{1,0:T(8,128)}, u32[]{:S(2)}) copy-start(f32[8,768]{1,0:T(8,128)} %get-tuple-element.152) | copy-start | bytes 73732
  427.2 47.2 %copy-start.13 = (f32[8,768]{1,0:T(8,128)S(1)}, f32[8,768]{1,0:T(8,128)}, u32[]{:S(2)}) copy-start(f32[8,768]{1,0:T(8,128)} %get-tuple-element.153) | copy-start | bytes 73732
  427.2 47.9 %copy-start.16 = (f32[1,3072]{1,0:T(1,128)S(1)}, f32[1,3072]{1,0:T(1,128)}, u32[]{:S(2)}) copy-start(f32[1,3072]{1,0:T(1,128)} %get-tuple-element.151) | copy-start | bytes 36868
  427.2 48.7 %copy-start.15 = (f32[1,3072]{1,0:T(1,128)S(1)}, f32[1,3072]{1,0:T(1,128)}, u32[]{:S(2)}) copy-start(f32[1,3072]{1,0:T(1,128)} %get-tuple-element.154) | copy-start | bytes 36868
  477.6 68.5 %copy-start.2 = (f32[96,768]{1,0:T(8,128)S(1)}, f32[96,768]{1,0:T(8,128)}, u32[]{:S(2)}) copy-start(f32[96,768]{1,0:T(8,128)} %get-tuple-element.165) | copy-start | bytes 884740
  477.6 70.5 %copy-start.7 = (f32[24,1536]{1,0:T(8,128)S(1)}, f32[24,1536]{1,0:T(8,128)}, u32[]{:S(2)}) copy-start(f32[24,1536]{1,0:T(8,128)} %get-tuple-element.160) | copy-start | bytes 442372
  477.6 71.4 %copy-start.5 = (f32[24,1536]{1,0:T(8,128)S(1)}, f32[24,1536]{1,0:T(8,128)}, u32[]{:S(2)}) copy-start(f32[24,1536]{1,0:T(8,128)} %get-tuple-element.162) | copy-start | bytes 442372
  477.6 71.4 %copy-start.6 = (f32[24,1536]{1,0:T(8,128)S(1)}, f32[24,1536]{1,0:T(8,128)}, u32[]{:S(2)}) copy-start(f32[24,1536]{1,0:T(8,128)} %get-tuple-element.163) | copy-start | bytes 442372
  546.1 3.9 copy-start.8
  546.1 3.9 copy-start.9
  546.1 4.5 copy-start.3
  546.1 4.5 copy-start.4
  546.1 5.3 copy-start.10
  546.1 7.2 %copy-start.1 = (bf16[256,768]{1,0:T(8,128)(2,1)S(1)}, bf16[256,768]{1,0:T(8,128)(2,1)}, u32[]{:S(2)}) copy-start(bf16[256,768]{1,0:T(8,128)(2,1)} %get-tuple-element.108) | copy-start | bytes 1179652
  546.1 7.9 %copy-start = (f32[256,768]{1,0:T(8,128)S(1)}, f32[256,768]{1,0:T(8,128)}, u32[]{:S(2)}) copy-start(f32[256,768]{1,0:T(8,128)} %get-tuple-element.155) | copy-start | bytes 2359300

commit v4 on v3

--- a/solution.py
+++ b/solution.py
@@ -14,39 +14,43 @@
 
 
 HEAD_PLACES = SimpleNamespace(
+    begins=(0, 3, 1, 2, 16, 28, 46, 15, 31),
     arrivals=(
-        (13, 14, 32, 23, 53, 40, 88, 31, 59, 61, 74, 67, 81, 87, 107),
-        (11, 12, 29),
-        (21, 15, 41, 25, 42, 50, 90, 34, 58, 64, 79, 68, 101, 92, 105),
-        (18, 33, 46, 17, 43, 66, 96, 45, 97, 65, 104, 71, 106, 89, 108),
-        (30, 20, 49, 10, 62, 63, 115, 48, 77, 69, 111, 82, 120, 110, 125),
-        (27, 24, 57, 22, 60, 52, 94, 39, 78, 80, 100, 76, 91, 103, 114),
-        (38, 26, 51, 35, 70, 73, 95, 37, 84, 85, 117, 93, 123, 109, 128),
-        (16, 28, 83, 19, 47, 99, 118, 4, 36, 75, 126, 72, 122, 134, 131),
-        (55, 54, 127, 56, 86, 132, 142, 44, 98, 137, 140, 102, 135, 143, 145),
-        (129, 124, 146),
-        (133, 130, 141),
-        (138, 136, 147),
-        (144, 139, 148),
+        (5, 4, 17, 6, 18, 19, 32, 20, 33, 30, 54, 34, 55, 56, 77),
+        (12, 13, 29),
+        (7, 14, 21, 8, 22, 23, 35, 24, 36, 37, 57, 38, 58, 59, 78),
+        (9, 10, 50, 11, 25, 26, 39, 27, 40, 41, 60, 42, 62, 61, 79),
+        (47, 48, 72, 49, 73, 74, 102, 75, 103, 104, 125, 105, 126, 127, 143),
+        (51, 52, 80, 53, 83, 81, 106, 82, 93, 107, 128, 108, 129, 130, 142),
+        (76, 70, 98, 71, 99, 100, 119, 101, 120, 121, 140, 122, 144, 141, 150),
+        (43, 66, 94, 44, 67, 95, 117, 45, 68, 91, 118, 69, 96, 133, 139),
+        (64, 87, 115, 65, 88, 109, 136, 63, 89, 114, 137, 90, 116, 138, 147),
+        (112, 113, 134),
+        (123, 124, 145),
+        (131, 132, 146),
+        (110, 111, 135),
     ),
-    project=112,
+    project=84,
+    attention=(148, 149, 151),
 )
 TAIL_PLACES = SimpleNamespace(
+    begins=(0, 2, 5, 11, 29, 22, 3),
     arrivals=(
-        (9, 8, 48, 19, 39, 31, 73, 26, 62, 57, 75, 65, 86, 83, 93),
-        (36, 5, 32, 6, 17, 38, 68, 13, 67, 50, 72, 56, 69, 70, 87),
-        (28, 10, 61, 11, 47, 46, 80, 20, 60, 64, 82, 74, 91, 89, 110),
-        (34, 23, 44, 24, 49, 51, 78, 43, 81, 88, 107, 77, 92, 99, 104),
-        (33, 29, 66, 30, 59, 71, 95, 45, 76, 79, 102, 84, 119, 98, 114),
-        (53, 55, 90, 35, 52, 96, 103, 40, 58, 106, 115, 63, 112, 123, 122),
-        (37, 105, 120, 42, 85, 117, 129, 54, 94, 121, 131, 97, 130, 133, 135),
-        (116, 113, 132),
-        (118, 126, 134),
-        (125, 124, 136),
-        (127, 128, 137),
+        (6, 7, 17, 8, 18, 19, 31, 20, 32, 33, 44, 34, 45, 46, 65),
+        (15, 10, 23, 14, 26, 24, 37, 28, 38, 39, 52, 40, 53, 54, 64),
+        (27, 36, 59, 16, 60, 61, 86, 62, 113, 88, 115, 85, 123, 112, 133),
+        (51, 48, 74, 47, 68, 73, 90, 63, 95, 93, 120, 96, 129, 121, 134),
+        (57, 55, 81, 56, 82, 83, 107, 87, 108, 104, 124, 92, 126, 131, 137),
+        (49, 76, 102, 50, 105, 110, 119, 58, 77, 103, 118, 70, 99, 125, 138),
+        (41, 71, 98, 42, 78, 91, 114, 43, 79, 94, 128, 69, 97, 117, 135),
+        (100, 101, 127),
+        (122, 109, 130),
+        (116, 111, 132),
+        (80, 75, 106),
     ),
-    steps=(3, 4, 12, 15, 16, 21, 22, 27, 41),
-    project=100,
+    steps=(1, 4, 9, 12, 13, 21, 25, 30, 35),
+    project=66,
+    attention=(136, 139, 140),
 )
 ROWS_PLACES = SimpleNamespace(
     rows=(
@@ -243,16 +247,9 @@
             when(cond, copy.wait_send)
 
 
-def end_gathers(jobs):
-    for job in jobs:
-        job.siblings()
-    for job in jobs:
-        job.drain()
-
-
 class Reduce:
-    def __init__(self, partial_of, inbox, order, depth, send, recv):
-        self.partial_of, self.inbox = partial_of, inbox
+    def __init__(self, partial_of, far_partial_of, inbox, order, depth, send, recv):
+        self.partial_of, self.far_partial_of, self.inbox = partial_of, far_partial_of, inbox
         self.order, self.depth, self.send, self.recv = order, depth, send, recv
         self.me = place()
         self.base, _ = self.slots(order, depth)
@@ -305,7 +302,7 @@
         slot = self.marks.index(offset)
         edge = self.where_(key, "c", p["z"])
         peer = flipped(self.me, "c")
-        self.copy(self.partial_of(flipped(p, "c")), edge, slot, peer).start()
+        self.copy(self.far_partial_of(flipped(p, "c")), edge, slot, peer).start()
         self.sent.append(slot)
 
     def kids(self, offset, p):
@@ -374,7 +371,9 @@
 Z_Y_X, Z_X_Y, X_Y_Z, Y_X_Z = ("z", "y", "x"), ("z", "x", "y"), ("x", "y", "z"), ("y", "x", "z")
 Y_X, X_Y = ("y", "x"), ("x", "y")
 ANYWHERE = pl.BlockSpec(memory_space=pl.ANY)
+IN_SMEM = pl.BlockSpec(memory_space=pltpu.SMEM)
 IN_VMEM = pl.BlockSpec(memory_space=pltpu.VMEM)
+LOAD, SAVE = pl.BlockSpec(memory_space=pl.ANY), pl.BlockSpec(memory_space=pl.ANY)
 
 
 def dma(*shape):
@@ -409,13 +408,27 @@
     return pl.multiple_of(block * BLK, BLK)
 
 
-def block_of(ref, block):
-    held = ref.shape[2] // BLK
-    return ref[block // held, 0, pl.ds(row_of(block % held), BLK)]
-
-
-def whole(ref):
-    return ref[...].reshape(-1, WIDE)
+class Keys:
+    def __init__(self, ref, pair=None):
+        self.ref, self.pair = ref, pair
+        self.held = ref.shape[2] // (BLK if pair is None else 1)
+        self.blocks_all = ref.shape[0] * self.held
+
+    def block(self, device, inner):
+        if self.pair is None:
+            return self.ref[device, 0, pl.ds(row_of(inner), BLK)]
+        return self.ref[device, self.pair, inner]
+
+    def whole(self):
+        held = self.ref[...] if self.pair is None else self.ref[:, self.pair]
+        return held.reshape(-1, WIDE)
+
+    def with_shared(self, near):
+        if self.pair is None:
+            shared = self.ref[0, 0, 0:SHARED]
+        else:
+            shared = self.ref[0, self.pair, 0:GLOB].reshape(SHARED, WIDE)
+        return jnp.concatenate([shared, near], axis=0)
 
 
 def window_blocks(first, block, blocks_all):
@@ -426,22 +439,18 @@
     return [picks_ref[(block * H + 2 * pair + side) * R + r] for side in range(2)]
 
 
-def bring(picks_ref, first, pair, pairs, blocks_here):
+def bring(drawn, first, pairs, blocks_here):
     low_lanes = lax.broadcasted_iota(jnp.int32, (1, WIDE), 1) < DH
     for block in range(blocks_here):
         for source, target in pairs:
-            blocks_all = source.shape[0] * source.shape[2] // BLK
-            for j, one in enumerate(window_blocks(first, block, blocks_all)):
-                target[block, j * BLK : (j + 1) * BLK] = block_of(source, one)
+            for j, one in enumerate(window_blocks(first, block, source.blocks_all)):
+                rows = source.block(one // source.held, one % source.held)
+                target[block, j * BLK : (j + 1) * BLK] = rows
             for r in range(R):
-                one, two = drawn_blocks(picks_ref, pair, block, r)
+                one, two = drawn(block, r)
                 target[block, (3 + r) * BLK : (4 + r) * BLK] = jnp.where(
-                    low_lanes, block_of(source, one), block_of(source, two)
+                    low_lanes, source.block(*one), source.block(*two)
                 )
-
-
-def with_shared(ref, near):
-    return jnp.concatenate([ref[0, 0, 0:SHARED], near], axis=0)
 
 
 def key_scores(keys, q_heads, shut):
@@ -457,24 +466,36 @@
     return weight * (1.0 / total), top + jnp.log(total)
 
 
-def attend_kernel(
-    picks_ref, first_ref, q_ref, k_ref, v_ref, shut_ref, part_ref, o_ref, po_ref, log_ref, plog_ref, near_k, near_v
+def attend_pair(
+    drawn, first, q_ref, keys, values, shut_ref, part_ref, o_ref, po_ref, log_ref, plog_ref, near_k, near_v
 ):
-    pair = pl.program_id(0)
     blocks_here = q_ref.shape[0] // BLK
-    bring(picks_ref, first_ref[0], pair, [(k_ref, near_k), (v_ref, near_v)], blocks_here)
+    bring(drawn, first, [(keys, near_k), (values, near_v)], blocks_here)
     scale = jnp.bfloat16(DH ** (-0.5))
-    weight, logs = soft(product_nt(whole(k_ref), split_heads(part_ref[...] * scale)))
-    mixed = product_tn(weight.astype(jnp.bfloat16), whole(v_ref))
+    weight, logs = soft(product_nt(keys.whole(), split_heads(part_ref[...] * scale)))
+    mixed = product_tn(weight.astype(jnp.bfloat16), values.whole())
     po_ref[...] = join_heads(mixed).astype(po_ref.dtype)
     plog_ref[0] = logs
     for block in range(blocks_here):
         here = slice(block * BLK, (block + 1) * BLK)
         q_heads = split_heads(q_ref[here] * scale)
-        weight, logs = soft(key_scores(with_shared(k_ref, near_k[block]), q_heads, shut_ref[block]))
-        mixed = product_tn(weight.astype(jnp.bfloat16), with_shared(v_ref, near_v[block]))
+        weight, logs = soft(key_scores(keys.with_shared(near_k[block]), q_heads, shut_ref[block]))
+        mixed = product_tn(weight.astype(jnp.bfloat16), values.with_shared(near_v[block]))
         o_ref[here] = join_heads(mixed).astype(o_ref.dtype)
         log_ref[0, block : block + 1] = logs
+
+
+def drawn_places(picks_ref, pair, held):
+    def drawn(block, r):
+        return [(one // held, one % held) for one in drawn_blocks(picks_ref, pair, block, r)]
+
+    return drawn
+
+
+def attend_kernel(picks_ref, first_ref, q_ref, k_ref, v_ref, *refs):
+    keys, values = Keys(k_ref), Keys(v_ref)
+    drawn = drawn_places(picks_ref, pl.program_id(0), keys.held)
+    attend_pair(drawn, first_ref[0], q_ref, keys, values, *refs)
 
 
 def near_rows(rows, dtype):
@@ -532,14 +553,16 @@
     pair = pl.program_id(0)
     first = first_ref[0]
     blocks_here, blocks_all = q_ref.shape[0] // BLK, sum_k.shape[0] // BLK
-    bring(picks_ref, first, pair, [(k_ref, near_k), (v_ref, near_v)], blocks_here)
+    all_keys, all_values = Keys(k_ref), Keys(v_ref)
+    drawn = drawn_places(picks_ref, pair, all_keys.held)
+    bring(drawn, first, [(all_keys, near_k), (all_values, near_v)], blocks_here)
     low_lanes = lax.broadcasted_iota(jnp.int32, (1, WIDE), 1) < DH
     step = DH ** (-0.5)
     scale = jnp.bfloat16(step)
     part, cot = split_heads(part_ref[...] * scale), split_heads(pdo_ref[...])
-    weight = jnp.exp(product_nt(whole(k_ref), part) - plog_ref[0])
-    grads = score_grads(weight, whole(v_ref), cot)
-    pdq_ref[...] = (join_heads(product_tn(grads, whole(k_ref))) * step).astype(pdq_ref.dtype)
+    weight = jnp.exp(product_nt(all_keys.whole(), part) - plog_ref[0])
+    grads = score_grads(weight, all_values.whole(), cot)
+    pdq_ref[...] = (join_heads(product_tn(grads, all_keys.whole())) * step).astype(pdq_ref.dtype)
     sum_k[...] = product(grads, part)
     sum_v[...] = product(weight.astype(jnp.bfloat16), cot)
     shared_k = jnp.zeros((SHARED, WIDE), jnp.float32)
@@ -548,7 +571,7 @@
         here = slice(block * BLK, (block + 1) * BLK)
         do = jnp.where(first + block < GLOB, jnp.bfloat16(0), do_ref[here])
         q_heads, do_heads = split_heads(q_ref[here] * scale), split_heads(do)
-        keys, values = with_shared(k_ref, near_k[block]), with_shared(v_ref, near_v[block])
+        keys, values = all_keys.with_shared(near_k[block]), all_values.with_shared(near_v[block])
         weight = jnp.exp(key_scores(keys, q_heads, shut_ref[block]) - log_ref[0, block : block + 1])
         grads = score_grads(weight, values, do_heads)
         dq_ref[here] = (join_heads(product_tn(grads, keys)) * step).astype(dq_ref.dtype)
@@ -603,15 +626,53 @@
 
 
 def call(body, name, cid, ins, outs, scratch):
-    names = list(ins) + list(outs) + list(scratch)
+    loads = [k for k, (_, where) in ins.items() if where is LOAD]
+    saves = [k for k, (_, _, where) in outs.items() if where is SAVE]
+    names = ["far_" + k if k in loads or k in saves else k for k in (*ins, *outs)]
+    scratch = {
+        **scratch,
+        **{k: pltpu.VMEM(ins[k][0].shape, ins[k][0].dtype) for k in loads},
+        **{k: pltpu.VMEM(outs[k][0], outs[k][1]) for k in saves},
+        **dict(moves=dma(len(loads) + len(saves) + 1)),
+    }
+
+    def run(*given):
+        refs = SimpleNamespace(**dict(zip(names + list(scratch), given)))
+        copies = {}
+        for i, k in enumerate(loads + saves):
+            pair = (getattr(refs, "far_" + k), getattr(refs, k))
+            copies[k] = pltpu.make_async_copy(*(pair if k in loads else pair[::-1]), refs.moves.at[i])
+        coming, going = list(loads), []
+        for k in loads:
+            copies[k].start()
+
+        def ready(*wanted):
+            for k in wanted:
+                if k in coming:
+                    coming.remove(k)
+                    copies[k].wait()
+
+        def save(*given):
+            for k in given:
+                if k in saves:
+                    going.append(k)
+                    copies[k].start()
+
+        refs.ready, refs.save = ready, save
+        body(refs)
+        ready(*loads)
+        save(*[k for k in saves if k not in going])
+        for k in saves:
+            copies[k].wait()
+
     got = pl.pallas_call(
-        lambda *refs: body(SimpleNamespace(**dict(zip(names, refs)))),
+        run,
         out_shape=[jax.ShapeDtypeStruct(shape, dtype) for shape, dtype, _ in outs.values()],
         in_specs=[where for _, where in ins.values()],
         out_specs=[where for _, _, where in outs.values()],
         scratch_shapes=list(scratch.values()),
         compiler_params=pltpu.CompilerParams(
-            collective_id=cid, has_side_effects=cid is not None, vmem_limit_bytes=VMEM_LIMIT
+            collective_id=cid, has_side_effects=True, vmem_limit_bytes=VMEM_LIMIT
         ),
         name=name,
     )(*[array for array, _ in ins.values()])
@@ -650,7 +711,10 @@
 
 class Gathering:
     def __init__(self, arrays, pieces, seq_count, depth, near):
-        self.near = near
+        self.near, self.layers = near, [layer for _, layer in arrays]
+        shapes = [a.shape if layer is None else a.shape[1:] for a, layer in arrays]
+        self.shapes = [jax.ShapeDtypeStruct(shape, a.dtype) for shape, (a, _) in zip(shapes, arrays)]
+        arrays = [a for a, _ in arrays]
         self.arrays, self.pieces, self.depth, self.n_dev = arrays, pieces, depth, seq_count * depth
         flat_only = {which for which, *_, order in pieces if "z" not in order}
         self.counts = [seq_count if i in flat_only else self.n_dev for i in range(len(arrays))]
@@ -660,8 +724,8 @@
 
     def outs(self):
         return {
-            "every%d" % i: ((n,) + a.shape, a.dtype, IN_VMEM if i in self.near else ANYWHERE)
-            for i, (n, a) in enumerate(zip(self.counts, self.arrays))
+            "every%d" % i: ((n,) + a.shape, a.dtype, SAVE if i in self.near else ANYWHERE)
+            for i, (n, a) in enumerate(zip(self.counts, self.shapes))
         }
 
     def scratch(self):
@@ -677,6 +741,7 @@
 
     def begin(self, refs):
         slabs = [getattr(refs, "slab%d" % i) for i in range(len(self.arrays))]
+        slabs = [ref if layer is None else ref.at[layer] for ref, layer in zip(slabs, self.layers)]
         every = [getattr(refs, "every%d" % i) for i in range(len(self.arrays))]
         self.jobs, at = [], 0
         for k, (which, row, rows, column, columns_, order) in enumerate(self.pieces):
@@ -690,8 +755,6 @@
                 )
             )
             at += Gather.sends(order, self.depth)
-        for job in self.jobs:
-            job.begin()
         me = place()
         self.own = [
             pltpu.make_async_copy(slab, all_.at[self.number(i)(me)], refs.g_local.at[i])
@@ -706,6 +769,7 @@
                 job.siblings()
         for i in arrays:
             self.own[i].wait()
+            refs.save("every%d" % i)
         self.early = arrays
 
     def end(self):
@@ -792,8 +856,9 @@
         keep(PAIRS + 2 * i, product(low[...], w(span(i, 256, 2 * D))) + bias[1:2, span(i, 256)])
 
     def keep(pair, acc):
-        kv[pair] = acc[:, :WIDE].astype(kv.dtype)
-        kv[pair + 1] = acc[:, WIDE:].astype(kv.dtype)
+        for half in range(2):
+            lanes = acc[:, half * WIDE : (half + 1) * WIDE].astype(kv.dtype)
+            kv[pair + half] = lanes.reshape(kv.shape[1:])
 
     for act in (keys, values, queries):
         over(D // 256, act)
@@ -804,16 +869,20 @@
         self.rows, self.seq_count, self.depth, self.dtype = rows, seq_count, depth, dtype
 
     def outs(self):
+        blocks, f32 = self.rows // BLK, jnp.float32
         return dict(
-            q=((self.rows, D), self.dtype, IN_VMEM),
-            every=((self.seq_count, 2 * PAIRS, self.rows, WIDE), self.dtype, ANYWHERE),
-            part=((SHARE, D), self.dtype, ANYWHERE),
+            q=((self.rows, D), self.dtype, SAVE),
+            every=((self.seq_count, 2 * PAIRS, blocks, BLK, WIDE), self.dtype, SAVE),
+            part=((SHARE, D), self.dtype, SAVE),
+            o=((self.rows, D), self.dtype, SAVE), po=((SHARE, D), self.dtype, SAVE),
+            log=((PAIRS, blocks, WIDE), f32, SAVE), plog=((PAIRS, 1, 2 * SHARE), f32, SAVE),
         )
 
     def scratch(self):
         return dict(
-            kv=pltpu.VMEM((2 * PAIRS, self.rows, WIDE), self.dtype), send=dma(4 * Gather.sends(Y_X, self.depth)),
+            kv=pltpu.VMEM((2 * PAIRS, self.rows // BLK, BLK, WIDE), self.dtype), send=dma(4 * Gather.sends(Y_X, self.depth)),
             recv=dma(4, self.seq_count), local=dma(), give=dma(HELPERS), take=dma(),
+            near_k=near_rows(self.rows, self.dtype), near_v=near_rows(self.rows, self.dtype),
         )
 
     def prepare(self, refs):
@@ -837,18 +906,53 @@
         self.own = pltpu.make_async_copy(refs.kv, refs.every.at[number_in_sequence(place())], refs.local)
         self.own.start()
 
-    def end(self):
-        end_gathers(self.jobs)
+    def arrived(self, refs):
+        for job in self.jobs:
+            job.siblings()
         self.own.wait()
         self.finish()
+        refs.save("every", "part")
+
+    def attention(self, refs, steps):
+        first = lax.axis_index(SEQ) * (self.rows // BLK)
+        count = PAIRS // steps
+
+        def pair_of(pair):
+            at, one = span(pair, WIDE), pl.ds(pair, 1)
+
+            def drawn(block, r):
+                first_one = (block * H + 2 * pair) * R + r
+                return [(refs.picks[0, i], refs.picks[1, i]) for i in (first_one, first_one + R)]
+
+            attend_pair(
+                drawn, first, refs.q.at[:, at], Keys(refs.every, pair), Keys(refs.every, PAIRS + pair), refs.shut,
+                refs.part.at[:, at], refs.o.at[:, at], refs.po.at[:, at], refs.log.at[one], refs.plog.at[one],
+                refs.near_k, refs.near_v,
+            )
+
+        def step(k):
+            if k == 0:
+                self.arrived(refs)
+                refs.ready("shut")
+            over(count, lambda i: pair_of(k * count + i))
+            if k == steps - 1:
+                refs.save("o", "po", "log", "plog")
+
+        return [partial(step, k) for k in range(steps)]
+
+    def end(self):
+        for job in self.jobs:
+            job.drain()
 
 
 def project_and_send(refs, gathering, sequence, low, which):
     def act():
         gathering.hurry(refs, [which])
         w = from_slabs(getattr(refs, "every%d" % which))
+        refs.ready("low")
         project(low, w, refs.bias, refs.q, refs.kv)
         sequence.begin(refs)
+        refs.save("q")
 
     return act
 
@@ -857,11 +961,28 @@
     return [pair for job, at in zip(jobs, places, strict=True) for pair in job.events(at)]
 
 
-def first_head(low, small, segs, weights, seq_count, depth, cid):
+def shut_keys_here(segs, own_segs, shut):
+    me, count = lax.axis_index(SEQ), segs.shape[0]
+    blocks = shut.shape[0]
+    rows = blocks * BLK
+
+    def column(device):
+        held = segs[device].astype(jnp.float32).T
+        return [held[:, r : r + 1] for r in range(rows // WIDE)]
+
+    before, here, after = column((me + count - 1) % count), column(me), column((me + 1) % count)
+    near = jnp.concatenate([before[-1][WIDE - BLK :]] + here + [after[0][:BLK]], axis=0)
+    for block in range(blocks):
+        spot = (me * blocks + block - 1) * BLK + lax.broadcasted_iota(jnp.int32, (3 * BLK, WIDE), 0)
+        same = near[block * BLK : (block + 3) * BLK] == own_segs[block : block + 1]
+        shut[block] = jnp.where(same & (spot >= SHARED) & (spot < count * rows), 0.0, masked_score)
+
+
+def first_head(low, small, segs, own_segs, picks, weights, seq_count, depth, cid):
     rows = low.shape[0]
     pieces = [(0, 0, small.shape[0], 0, 128, Z_Y_X), (1, 0, 8, 0, 128, Y_X)]
-    pieces += layer_pieces(small.shape[0], weights[3].shape[0], 2)
-    gathering = Gathering([small, segs] + weights, pieces, seq_count, depth, (0, 2))
+    pieces += layer_pieces(small.shape[0], weights[3][0].shape[1], 2)
+    gathering = Gathering([(small, None), (segs, None)] + weights, pieces, seq_count, depth, (0, 1, 2))
     sequence = Sequence(rows, seq_count, depth, low.dtype)
 
     def body(refs):
@@ -871,7 +992,9 @@
         refs.bias = refs.vectors.at[0]
 
         def vectors():
-            gathering.hurry(refs, [0])
+            gathering.hurry(refs, [0, 1])
+            shut_keys_here(refs.every1, refs.own_segs, refs.shut)
+            refs.save("shut")
             table = refs.every0[...].astype(jnp.float32).reshape(D, 128).T
             for layer in range(L):
                 refs.vectors[layer, 0:6] = table[6 * layer : 6 * layer + 6]
@@ -880,26 +1003,33 @@
 
         def project_now():
             project_and_send(refs, gathering, sequence, refs.low, 2)()
-            gathering.early = [0, 2]
+            gathering.early = [0, 1, 2]
 
         at = HEAD_PLACES
         run_in_order(
-            timed_events(gathering.jobs + sequence.jobs, at.arrivals) + [(at.project, vectors), (at.project + 0.1, project_now)]
+            [(place_, job.begin) for place_, job in zip(at.begins, gathering.jobs, strict=True)]
+            + timed_events(gathering.jobs + sequence.jobs, at.arrivals)
+            + [(at.project, vectors), (at.project + 0.1, project_now)]
+            + list(zip(at.attention, sequence.attention(refs, len(at.attention)), strict=True))
         )
         sequence.end()
         gathering.end()
 
     got = call(
         body, "first_head", cid,
-        {"low": (low, IN_VMEM), **gathering.ins()},
         {
-            **dict(vectors=((L, 8, D), jnp.float32, IN_VMEM), table=((4 * L, D), jnp.float32, IN_VMEM)),
+            **dict(low=(low, LOAD), own_segs=(own_segs, IN_VMEM), picks=(picks, IN_SMEM)), **gathering.ins(),
+        },
+        {
+            **dict(
+                vectors=((L, 8, D), jnp.float32, IN_VMEM), table=((4 * L, D), jnp.float32, IN_VMEM),
+                shut=((rows // BLK, 3 * BLK, WIDE), jnp.float32, SAVE),
+            ),
             **sequence.outs(), **gathering.outs(),
         },
         {**sequence.scratch(), **gathering.scratch()},
     )
-    results = gathering.results(got)
-    return got, results[1], results[2:]
+    return got, gathering.results(got)[2:]
 
 
 def norm_block(resid, gain, shift):
@@ -912,17 +1042,19 @@
 ROW_BLOCK = 64
 
 
-def tail_steps(refs, w_out, w_up, w_down, waits):
+def tail_steps(refs):
     rows, hidden = refs.resid.shape[0], refs.shifts.shape[1]
 
     def out():
-        waits[0]()
+        refs.ready("resid", "w_out")
 
         def act(i):
             at = span(i, 256)
-            refs.sum[:, at] = refs.resid[:, at].astype(jnp.float32) + product(refs.mixed[...], w_out[:, at]) + refs.bias[2:3, at]
+            own = refs.resid[:, at].astype(jnp.float32)
+            refs.sum[:, at] = own + product(refs.mixed[...], refs.w_out[:, at]) + refs.bias[2:3, at]
 
         over(D // 256, act)
+        refs.save("mixed")
 
     def norm_one():
         def act(i):
@@ -932,12 +1064,13 @@
             refs.y_low[at] = y.astype(jnp.bfloat16)
 
         over(rows // ROW_BLOCK, act)
-        waits[1]()
+        refs.save("n1", "inv1", "y_low")
+        refs.ready("w_up")
 
     def up(first, count):
         def act(i):
             at = span(first + i, 256)
-            u = product(refs.y_low[...], w_up[:, at]) + refs.shifts[0:1, at]
+            u = product(refs.y_low[...], refs.w_up[:, at]) + refs.shifts[0:1, at]
             share = 0.5 + 0.5 * lax.erf(u * (0.5 ** 0.5))
             refs.a_low[:, at] = (u * share).astype(jnp.bfloat16)
             slope = share + u * jnp.exp(-0.5 * u * u) * ((2.0 * jnp.pi) ** -0.5)
@@ -946,11 +1079,12 @@
         over(count, act)
 
     def down():
-        waits[2]()
+        refs.ready("w_down")
+        refs.save("a_low", "slope")
 
         def act(i):
             at = span(i, 256)
-            refs.sum[:, at] = refs.sum[:, at] + product(refs.a_low[...], w_down[:, at]) + refs.bias[4:5, at]
+            refs.sum[:, at] = refs.sum[:, at] + product(refs.a_low[...], refs.w_down[:, at]) + refs.bias[4:5, at]
 
         over(D // 256, act)
 
@@ -964,62 +1098,51 @@
             refs.z_low[at] = z.astype(jnp.bfloat16)
 
         over(rows // ROW_BLOCK, act)
+        refs.save("n2", "inv2", "z", "z_low")
 
     quarter = hidden // 256 // 4
     return [out, norm_one] + [partial(up, k * quarter, quarter) for k in range(4)] + [down, norm_two]
 
 
 def tail_ins(mixed, part, resid, vectors, shifts, weights):
-    return {
-        "generic": (mixed, IN_VMEM), "own_part": (part, ANYWHERE), "resid": (resid, IN_VMEM), "vectors": (vectors, IN_VMEM),
-        "shifts": (shifts, IN_VMEM), "w_out": (weights[1], ANYWHERE), "w_up": (weights[2], ANYWHERE), "w_down": (weights[3], ANYWHERE),
-    }
-
-
-def tail_outs(rows, hidden):
+    return dict(
+        generic=(mixed, LOAD), own_part=(part, ANYWHERE), resid=(resid, LOAD), vectors=(vectors, IN_VMEM),
+        shifts=(shifts, IN_VMEM), w_out=(weights[1], LOAD), w_up=(weights[2], LOAD), w_down=(weights[3], LOAD),
+    )
+
+
+def tail_results(rows, hidden):
     f32, low = jnp.float32, jnp.bfloat16
-    return {
-        "mixed": ((rows, D), low, IN_VMEM), "n1": ((rows, D), f32, IN_VMEM), "inv1": ((rows, 1), f32, IN_VMEM),
-        "y_low": ((rows, D), low, IN_VMEM), "a_low": ((rows, hidden), low, IN_VMEM), "slope": ((rows, hidden), low, IN_VMEM),
-        "n2": ((rows, D), f32, IN_VMEM), "inv2": ((rows, 1), f32, IN_VMEM), "z_low": ((rows, D), low, IN_VMEM),
-    }
-
-
-def tail_scratch(rows, hidden):
-    low = jnp.bfloat16
-    return {
-        "sum": pltpu.VMEM((rows, D), jnp.float32), "v_out": pltpu.VMEM((D, D), low),
-        "v_up": pltpu.VMEM((D, hidden), low), "v_down": pltpu.VMEM((hidden, D), low),
-        "load": dma(3), "t_send": dma(), "t_recv": dma(HELPERS),
-    }
-
-
-def start_loads(refs):
-    loads = [
-        pltpu.make_async_copy(refs.w_out, refs.v_out, refs.load.at[0]),
-        pltpu.make_async_copy(refs.w_up, refs.v_up, refs.load.at[1]),
-        pltpu.make_async_copy(refs.w_down, refs.v_down, refs.load.at[2]),
-    ]
-    for copy in loads:
-        copy.start()
-    return [copy.wait for copy in loads]
-
-
-def tail(mixed, part, resid, vectors, shifts, weights, next_weights, seq_count, depth, cid):
+    kept = dict(mixed=((rows, D), low), y_low=((rows, D), low), a_low=((rows, hidden), low), z_low=((rows, D), low))
+    norms = dict(
+        n1=((rows, D), f32), inv1=((rows, 1), f32), slope=((rows, hidden), low), n2=((rows, D), f32), inv2=((rows, 1), f32)
+    )
+    return kept, norms
+
+
+def saved(shapes):
+    return {k: (*v, SAVE) for k, v in shapes.items()}
+
+
+def tail_scratch(rows):
+    return dict(sum=pltpu.VMEM((rows, D), jnp.float32), t_send=dma(), t_recv=dma(HELPERS))
+
+
+def tail(mixed, part, resid, vectors, shifts, weights, next_weights, shut, picks, seq_count, depth, cid):
     rows, hidden = resid.shape[0], shifts.shape[1]
-    pieces = layer_pieces(next_weights[0].shape[0], next_weights[3].shape[0], 0)
+    pieces = layer_pieces(next_weights[0][0].shape[1], next_weights[3][0].shape[1], 0)
     gathering = Gathering(next_weights, pieces, seq_count, depth, (0,))
     sequence = Sequence(rows, seq_count, depth, mixed.dtype)
 
     def body(refs):
-        waits = start_loads(refs)
+        refs.ready("generic")
         refs.mixed[...] = refs.generic[...]
         greet(("y", "x", "z"), depth, spread=True, collect=True)
         finish = to_first(refs.own_part, refs.mixed, refs.t_send, refs.t_recv)
         gathering.begin(refs)
         sequence.prepare(refs)
         refs.bias = refs.vectors.at[0]
-        steps = [finish] + tail_steps(refs, refs.v_out, refs.v_up, refs.v_down, waits)
+        steps = [finish] + tail_steps(refs)
 
         def project_now():
             refs.bias = refs.vectors.at[1]
@@ -1027,19 +1150,26 @@
 
         at = TAIL_PLACES
         run_in_order(
-            timed_events(gathering.jobs + sequence.jobs, at.arrivals)
+            [(place_, job.begin) for place_, job in zip(at.begins, gathering.jobs, strict=True)]
+            + timed_events(gathering.jobs + sequence.jobs, at.arrivals)
             + list(zip(at.steps, steps, strict=True)) + [(at.project, project_now)]
+            + list(zip(at.attention, sequence.attention(refs, len(at.attention)), strict=True))
         )
         sequence.end()
         gathering.end()
 
-    outs = tail_outs(rows, hidden)
-    outs.update(z=((rows, D), jnp.float32, IN_VMEM))
+    kept, norms = tail_results(rows, hidden)
     got = call(
         body, "tail", cid,
-        {**tail_ins(mixed, part, resid, vectors, shifts, weights), **gathering.ins()},
-        {**outs, **sequence.outs(), **gathering.outs()},
-        {**tail_scratch(rows, hidden), **sequence.scratch(), **gathering.scratch()},
+        {
+            **tail_ins(mixed, part, resid, vectors, shifts, weights),
+            **dict(shut=(shut, LOAD), picks=(picks, IN_SMEM)), **gathering.ins(),
+        },
+        {
+            **saved(kept), **saved(norms), **dict(z=((rows, D), jnp.float32, SAVE)), **sequence.outs(),
+            **gathering.outs(),
+        },
+        {**tail_scratch(rows), **sequence.scratch(), **gathering.scratch()},
     )
     return got, gathering.results(got)
 
@@ -1057,7 +1187,7 @@
     ) * inv_std
 
 
-def back_steps(refs, dz, w_down, w_up, w_out, waits):
+def back_steps(refs, dz, w_down, w_up, w_out, waits=(lambda: None,) * 3):
     rows, hidden = refs.n2.shape[0], refs.slope.shape[1]
     zero = jnp.zeros((8, D), jnp.float32)
 
@@ -1065,6 +1195,8 @@
         refs.totals[k : k + 1] = jnp.sum(total, axis=0, keepdims=True)
 
     def norm_two():
+        refs.ready("n2", "inv2", "d_out")
+
         def act(i, sums):
             at = span(i, ROW_BLOCK)
             grad, normed = dz(at), refs.n2[at]
@@ -1075,6 +1207,8 @@
 
         sums = lax.fori_loop(0, rows // ROW_BLOCK, act, (zero,) * 3)
         row(4, sums[0]), row(5, sums[1]), row(7, sums[2])
+        refs.save("dr2_low")
+        refs.ready("slope")
         waits[0]()
 
     def down(first, count):
@@ -1087,6 +1221,7 @@
         over(count, act)
 
     def up():
+        refs.save("du_low")
         waits[1]()
 
         def act(i):
@@ -1096,6 +1231,8 @@
         over(D // 256, act)
 
     def norm_one():
+        refs.ready("n1", "inv1")
+
         def act(i, sums):
             at = span(i, ROW_BLOCK)
             grad, normed = refs.work[at], refs.n1[at]
@@ -1106,6 +1243,7 @@
 
         sums = lax.fori_loop(0, rows // ROW_BLOCK, act, (zero,) * 3)
         row(2, sums[0]), row(3, sums[1]), row(6, sums[2])
+        refs.save("dr1", "dr1_low")
 
     def out():
         waits[2]()
@@ -1115,6 +1253,7 @@
             refs.cot[:, at] = product_nt(refs.dr1_low[...], w_out[at]).astype(jnp.bfloat16)
 
         over(D // 256, act)
+        refs.save("cot")
 
     half = hidden // 256 // 2
     return [norm_two, partial(down, 0, half), partial(down, half, half), up, norm_one, out]
@@ -1122,38 +1261,37 @@
 
 def back_outs(rows, hidden):
     f32, low = jnp.float32, jnp.bfloat16
-    return {
-        "dr2_low": ((rows, D), low, IN_VMEM), "du_low": ((rows, hidden), low, IN_VMEM), "dr1": ((rows, D), f32, IN_VMEM),
-        "dr1_low": ((rows, D), low, IN_VMEM), "cot": ((rows, D), low, IN_VMEM), "totals": ((8, D), f32, IN_VMEM),
-        "hidden_totals": ((1, hidden), f32, IN_VMEM), "part_cot": ((SHARE, D), low, ANYWHERE),
-    }
+    return dict(
+        dr2_low=((rows, D), low, SAVE), du_low=((rows, hidden), low, SAVE), dr1=((rows, D), f32, SAVE),
+        dr1_low=((rows, D), low, SAVE), cot=((rows, D), low, SAVE), totals=((8, D), f32, IN_VMEM),
+        hidden_totals=((1, hidden), f32, IN_VMEM), part_cot=((SHARE, D), low, ANYWHERE),
+    )
 
 
 def turn(mixed, part, resid, vectors, shifts, weights, d_out, depth, cid):
     rows, hidden = resid.shape[0], shifts.shape[1]
 
     def body(refs):
-        waits = start_loads(refs)
+        refs.ready("generic")
         refs.mixed[...] = refs.generic[...]
         refs.bias = refs.vectors.at[1]
         greet((), depth, spread=True, collect=True)
         to_first(refs.own_part, refs.mixed, refs.t_send, refs.t_recv)()
-        for step in tail_steps(refs, refs.v_out, refs.v_up, refs.v_down, waits):
+        for step in tail_steps(refs):
             step()
-        done = [lambda: None] * 3
         refs.totals[...] = jnp.zeros_like(refs.totals)
-        for step in back_steps(
-            refs, lambda at: refs.d_out[at].astype(jnp.float32), refs.v_down, refs.v_up, refs.v_out, done
-        ):
+        for step in back_steps(refs, lambda at: refs.d_out[at].astype(jnp.float32), refs.w_down, refs.w_up, refs.w_out):
             step()
         to_helpers(refs.cot, refs.part_cot, refs.give, refs.take)()
 
+    kept, norms = tail_results(rows, hidden)
     return call(
         body, "turn", cid,
-        {**tail_ins(mixed, part, resid, vectors, shifts, weights), "d_out": (d_out, IN_VMEM)},
-        {**tail_outs(rows, hidden), **back_outs(rows, hidden)},
+        {**tail_ins(mixed, part, resid, vectors, shifts, weights), **dict(d_out=(d_out, LOAD))},
+        {**saved(kept), **back_outs(rows, hidden)},
         {
-            **tail_scratch(rows, hidden), "work": pltpu.VMEM((rows, D), jnp.float32), "give": dma(HELPERS), "take": dma(),
+            **tail_scratch(rows), **{k: pltpu.VMEM(*v) for k, v in norms.items()},
+            **dict(work=pltpu.VMEM((rows, D), jnp.float32), give=dma(HELPERS), take=dma()),
         },
     )
 
@@ -1241,7 +1379,7 @@
 
     def scratch(self):
         made = {}
-        for k, (_, shape, _, order, dtype) in enumerate(self.pieces):
+        for k, (_, _, shape, _, order, dtype) in enumerate(self.pieces):
             edges = Reduce.slots(order, self.depth)[1]
             made[self.name("box", k)] = pltpu.VMEM((edges,) + shape, dtype)
             made[self.name("send", k)] = dma(2 * len(offsets(order, self.depth)))
@@ -1250,9 +1388,9 @@
 
     def prepare(self, refs):
         self.jobs = []
-        for k, (source, _, target, order, _) in enumerate(self.pieces):
+        for k, (source, far, _, target, order, _) in enumerate(self.pieces):
             box, send, recv = (getattr(refs, self.name(what, k)) for what in ("box", "send", "recv"))
-            job = Reduce(partial(source, refs), box, order, self.depth, send, recv)
+            job = Reduce(partial(source, refs), partial(far, refs), box, order, self.depth, send, recv)
             self.jobs.append((job, target(refs)))
 
     def start(self, k):
@@ -1278,8 +1416,13 @@
 
     def piece(which, row, rows, column, columns_, order):
         window = (pl.ds(row, rows), pl.ds(column, columns_))
+
+        def source(refs, p):
+            return getattr(refs, "grad%d" % which).at[(number(p),) + window]
+
         return (
-            lambda refs, p: getattr(refs, "grad%d" % which).at[(number(p),) + window],
+            source,
+            source,
             (rows, columns_),
             lambda refs: write_total(getattr(refs, "owned%d" % which).at[window]),
             order,
@@ -1309,6 +1452,7 @@
 
         return (
             lambda refs, p: (refs.dk, refs.dv)[i // 2].at[number_in_sequence(p), window],
+            lambda refs, p: (refs.far_dk, refs.far_dv)[i // 2].at[number_in_sequence(p), window],
             (count, rows, WIDE),
             target,
             (X_Y, Y_X)[i % 2],
@@ -1320,17 +1464,25 @@
     by_weights = weight_sums(windows, depth, n_dev, {1: low, 2: low})
 
     def body(refs):
+        refs.ready("dq")
         refs.proj[:, 0:D] = refs.dq[...]
         greet(("y", "x", "z"), depth, collect=True)
         by_rows.prepare(refs)
         by_weights.prepare(refs)
         ends = [to_first(refs.part, refs.proj.at[:, pl.ds(0, D)], refs.t_send, refs.t_recv)]
         at = ROWS_PLACES
+
+        def grad(left, right, into):
+            refs.ready(left, right)
+            weight_grad(getattr(refs, left), getattr(refs, right), into)
+
+        first_block = min(place for places in at.rows for place in places[1:])
         run_in_order(
             by_rows.timed(at.rows) + by_weights.timed(at.weights)
             + [
-                (at.grads[0], lambda: weight_grad(refs.mixed, refs.dr1_low, refs.grad1)),
-                (at.grads[1], lambda: weight_grad(refs.y_low, refs.du_low, refs.grad2)),
+                (at.grads[0], partial(grad, "mixed", "dr1_low", refs.grad1)),
+                (at.grads[1], partial(grad, "y_low", "du_low", refs.grad2)),
+                (first_block - 0.5, partial(refs.ready, "dk", "dv")),
                 (at.collect, ends[0]),
             ]
         )
@@ -1352,9 +1504,8 @@
     return call(
         body, "sum_rows", cid,
         dict(
-            dk=(dk, IN_VMEM), dv=(dv, IN_VMEM), dq=(dq, IN_VMEM), part=(part_dq, ANYWHERE),
-            mixed=(held.mixed, IN_VMEM), y_low=(held.y_low, IN_VMEM), dr1_low=(grads.dr1_low, IN_VMEM),
-            du_low=(grads.du_low, IN_VMEM),
+            dq=(dq, LOAD), part=(part_dq, ANYWHERE), mixed=(held.mixed, LOAD), dr1_low=(grads.dr1_low, LOAD),
+            dk=(dk, LOAD), dv=(dv, LOAD), y_low=(held.y_low, LOAD), du_low=(grads.du_low, LOAD),
         ),
         dict(
             proj=((rows, 3 * D), low, IN_VMEM), totals=((8, D), f32, IN_VMEM), owned1=((share, D), f32, IN_VMEM),
@@ -1382,9 +1533,9 @@
         (2, 0, share, 0, hidden // 2, Y_X_Z),
         (0, 0, share, 0, 3 * D, Z_Y_X),
     ]
-    ins = {k: (getattr(held, k), IN_VMEM) for k in ("y_low", "du_low", "a_low", "dr2_low", "dr1")}
-    ins = {"up_" + k: v for k, v in ins.items()}
-    ins.update(low_in=(low_in, IN_VMEM), proj=(proj, IN_VMEM), w_qkv=(w_qkv, ANYWHERE))
+    ins = dict(low_in=(low_in, LOAD), proj=(proj, LOAD))
+    ins.update({"up_" + k: (getattr(held, k), LOAD) for k in ("y_low", "du_low", "a_low", "dr2_low")})
+    ins.update(up_dr1=(held.dr1, LOAD), w_qkv=(w_qkv, ANYWHERE))
     outs = {"owned%d" % i: (s, f32, IN_VMEM) for i, s in shapes.items()}
     scratch = {"grad%d" % i: pltpu.VMEM((n_dev,) + s, low) for i, s in shapes.items()}
     if small is not None:
@@ -1396,7 +1547,7 @@
     scratch.update(load=dma(4), wide=pltpu.VMEM((D, hidden), low))
     if below is not None:
         below_weights, below_held = below
-        ins.update({k: (getattr(below_held, k), IN_VMEM) for k in ("n1", "inv1", "n2", "inv2", "slope")})
+        ins.update({k: (getattr(below_held, k), LOAD) for k in ("n2", "inv2", "slope", "n1", "inv1")})
         ins.update(
             vectors=(vectors, IN_VMEM), w_out=(below_weights[1], ANYWHERE), w_up=(below_weights[2], ANYWHERE),
             w_down=(below_weights[3], ANYWHERE),
@@ -1405,7 +1556,10 @@
         scratch.update(
             tall=pltpu.VMEM((hidden, D), low), work=pltpu.VMEM((rows, D), f32), give=dma(HELPERS), take=dma()
         )
-    outs.update(dx=((rows, D), f32, IN_VMEM))
+    if below is None:
+        outs.update(dx=((rows, D), f32, SAVE))
+    else:
+        scratch.update(dx=pltpu.VMEM((rows, D), f32))
 
     def body(refs):
         v_qkv = refs.wide.at[:, pl.ds(0, 3 * D)]
@@ -1422,12 +1576,14 @@
         by_weights.prepare(refs)
         def dx():
             load_qkv.wait()
+            refs.ready("proj", "up_dr1")
 
             def act(i):
                 at = span(i, 256)
                 refs.dx[:, at] = refs.up_dr1[:, at] + product_nt(refs.proj[...], v_qkv[at])
 
             over(D // 256, act)
+            refs.save("dx")
             if below is not None:
                 load_up.start()
 
@@ -1444,12 +1600,17 @@
             ends = []
             steps.append(lambda: ends.append(to_helpers(refs.cot, refs.part_cot, refs.give, refs.take)))
         at = LAST_PLACES if below is None else BELOW_PLACES
+
+        def grad(left, right, into, column=0):
+            refs.ready(left, right)
+            weight_grad(getattr(refs, left), getattr(refs, right), into, column)
+
         run_in_order(
             by_weights.timed(at.weights)
             + [
-                (at.grads[0], lambda: weight_grad(refs.up_a_low, refs.up_dr2_low, refs.grad3)),
-                (at.grads[1], lambda: weight_grad(refs.up_y_low, refs.up_du_low, refs.grad2, hidden // 2)),
-                (at.grads[2], lambda: weight_grad(refs.low_in, refs.proj, refs.grad0)),
+                (at.grads[0], partial(grad, "up_a_low", "up_dr2_low", refs.grad3)),
+                (at.grads[1], partial(grad, "up_y_low", "up_du_low", refs.grad2, hidden // 2)),
+                (at.grads[2], partial(grad, "low_in", "proj", refs.grad0)),
             ]
             + list(zip(at.steps, steps, strict=True))
         )
@@ -1636,6 +1797,25 @@
     return (low[None], grad[None], *stacked[:4], *small_outputs(stacked[4], piece, up_bias.shape[1]))
 
 
+def assemble(wanted):
+    parts = [part for _, parts in wanted for part in parts]
+
+    def body(*refs):
+        sources, targets = list(refs[: len(parts)]), refs[len(parts) :]
+        for target, (_, held) in zip(targets, wanted):
+            for array, layer, column in held:
+                target[layer, :, column : column + array.shape[1]] = sources.pop(0)[...]
+
+    return pl.pallas_call(
+        body,
+        out_shape=[jax.ShapeDtypeStruct(shape, jnp.float32) for shape, _ in wanted],
+        in_specs=[IN_VMEM] * len(parts),
+        out_specs=[IN_VMEM] * len(wanted),
+        compiler_params=pltpu.CompilerParams(vmem_limit_bytes=VMEM_LIMIT),
+        name="assemble",
+    )(*[array for array, _, _ in parts])
+
+
 def on_pairs(
     layer_input, segments, rand_blocks, w_qkv, w_out, w_up, w_down, gains, biases, up_bias, d_out
 ):
@@ -1656,36 +1836,35 @@
     def flat(slabs):
         return [w.reshape(-1, w.shape[2]) for w in slabs]
 
-    def attention(got):
-        return attend(picks, first, got.q, got.every, shut, got.part)
-
-    def attention_back(got, back, logs):
+    places = jnp.stack([picks // blocks_here, picks % blocks_here])
+
+    def attention_back(got, back):
         return attend_back(
-            picks, first, got.q, got.every, shut, back.cot, got.part, back.part_cot, *logs
+            picks, first, got.q, got.every.reshape(seq_count, 2 * PAIRS, rows, WIDE), shut, back.cot, got.part, back.part_cot, got.log, got.plog
         )
 
     x = layer_input[0]
-    layers = [[w[layer] for w in (w_qkv, w_out, w_up, w_down)] for layer in range(L)]
-    head_one, segs_all, weights_one = first_head(x, small, segs, layers[0], seq_count, depth, 0)
+    layers = [[(w, layer) for w in (w_qkv, w_out, w_up, w_down)] for layer in range(L)]
+    own_segs = segments.reshape(blocks_here, BLK).astype(jnp.float32)
+    own_segs = jnp.concatenate([own_segs, own_segs], axis=1)
+    head_one, weights_one = first_head(x, small, segs, own_segs, places, layers[0], seq_count, depth, 0)
     weights_one = flat(weights_one)
     vectors = head_one.vectors
     shifts = head_one.table.reshape(L, 4, n_dev, piece)
     shifts = jnp.swapaxes(shifts, 1, 2).reshape(L, 1, hidden)
-    shut = shut_keys(segs_all[:, : rows // 128].reshape(-1), segments, first[0], blocks_here)
-    mixed, part, *logs_one = attention(head_one)
+    shut = head_one.shut
     rows_one, weights_two = tail(
-        mixed, part, x, vectors, shifts[0], weights_one, layers[1], seq_count, depth, 1
+        head_one.o, head_one.po, x, vectors, shifts[0], weights_one, layers[1], shut, places, seq_count, depth, 1
     )
     weights_two = flat(weights_two)
     middle = rows_one.z_low
-    mixed, part, *logs_two = attention(rows_one)
-    rows_two = turn(mixed, part, rows_one.z, vectors, shifts[1], weights_two, d_out[0], depth, 2)
-    dq, dk, dv, part = attention_back(rows_one, rows_two, logs_two)
+    rows_two = turn(rows_one.o, rows_one.po, rows_one.z, vectors, shifts[1], weights_two, d_out[0], depth, 2)
+    dq, dk, dv, part = attention_back(rows_one, rows_two)
     sums_two = sum_rows(dk, dv, dq, part, rows_two, rows_two, seq_count, depth, 3)
     back_one = sum_weights(
         rows_two, middle, sums_two.proj, vectors, weights_two[0], None, (weights_one, rows_one), n_dev, depth, 4
     )
-    dq, dk, dv, part = attention_back(head_one, back_one, logs_one)
+    dq, dk, dv, part = attention_back(head_one, back_one)
     sums_one = sum_rows(dk, dv, dq, part, rows_one, back_one, seq_count, depth, 5)
     small = jnp.concatenate(
         [
@@ -1698,17 +1877,25 @@
         SimpleNamespace(**{**vars(rows_one), **vars(back_one)}),
         x, sums_one.proj, None, weights_one[0], small, None, n_dev, depth, 6,
     )
-    by_layer = [(sums_one, last), (sums_two, back_one)]
-    stacked = [
-        jnp.stack([one.owned0 for _, one in by_layer]),
-        jnp.stack([one.owned1 for one, _ in by_layer]),
-        jnp.stack([jnp.concatenate([one.owned2, two.owned2], axis=1) for one, two in by_layer]),
-        jnp.stack([one.owned3 for _, one in by_layer]),
-    ]
+    whole_outputs = assemble(
+        [
+            ((L, piece, 3 * D), [(last.owned0, 0, 0), (back_one.owned0, 1, 0)]),
+            ((L, piece, D), [(sums_one.owned1, 0, 0), (sums_two.owned1, 1, 0)]),
+            (
+                (L, piece, hidden),
+                [
+                    (sums_one.owned2, 0, 0), (last.owned2, 0, hidden // 2),
+                    (sums_two.owned2, 1, 0), (back_one.owned2, 1, hidden // 2),
+                ],
+            ),
+            ((L, hidden // n_dev, D), [(last.owned3, 0, 0), (back_one.owned3, 1, 0)]),
+            ((1, rows, D), [(last.dx, 0, 0)]),
+        ]
+    )
     return (
         rows_two.z_low[None],
-        last.dx[None],
-        *stacked,
+        whole_outputs[4],
+        *whole_outputs[:4],
         *small_outputs(last.owned4.reshape(L, 8, 128), piece, up_bias.shape[1]),
     )
 

time: 563 us -> 527 us (0.936)
  Pallas kernels: 524 us -> 498 us
  other arithmetic: 10.9 us -> 5 us
    pallas_call x9 -> x8, Pallas kernels: 480 us -> 454 us  [the longest x7 451 us: call(): pl.pallas_call(run, out_shape=[jax.ShapeDtypeStruct(shape, dtype) for sha...]
    squeeze x4 -> x0, local copies, waits for them, and re-layouts: 6.48 us -> none  [on_pairs(): w[layer]]
where the time goes in v4:
time: 527 us; the launch traced here: 519 us
  Pallas kernels  498 us (94%)
  local copies, waits for them, and re-layouts  14.3 us (3%)
    pallas_call x7, Pallas kernels, call(): pl.pallas_call(run, out_shape=[jax.ShapeDtypeStruct(shape, dtype) for sha...  451 us
    pallas_call x2, Pallas kernels, attend_back(): pl.pallas_call(attend_back_kernel, grid_spec=pltpu.PrefetchScalarGridSpec...  43.8 us

profile of v4, /device:TPU:0, one launch (start us, length us, event | category | flops | bytes accessed | tf_op | source)
XLA Modules:
  0.0 518.7 jit_solution(18422407517739660083)
XLA Ops:
  0.6 0.7 convert_reduce_fusion
  1.4 0.7 pad_maximum_fusion.1.given_1_
  2.1 0.7 reshape.195
  2.9 0.7 copy.26
  3.7 1.3 pad.16.given_4_
  5.0 0.8 copy.28
  5.8 0.6 pad.15.given_3_
  6.5 0.8 copy.25
  7.2 0.7 reshape.204.picks_ref
  8.1 0.6 pad_add_fusion.given_2_.given_9_
  8.7 100.9 %first_head.1 = (f32[2,8,768]{2,1,0:T(8,128)}, f32[8,768]{1,0:T(8,128)}, f32[4,192,128]{2,1,0:T(8,128)}, bf16[256,768]{1,0:T(8,128)(2,1)}, bf16[8,12,4,64,128]{4...) custom-call(bf16[256,768]{1,0:T(8,128)(2,1)} %bitcast.39, ...), custom_call_target="tpu_custom_call" | custom-call | tf_op jit(solution)/shard_map/first_head/pallas_call | solution.py:668
  109.6 0.8 reshape.197
  110.5 0.7 squeeze.14.given_4_
  111.3 0.7 squeeze.13.given_4_
  112.0 103.5 %tail.1 = (bf16[256,768]{1,0:T(8,128)(2,1)}, bf16[256,768]{1,0:T(8,128)(2,1)}, bf16[256,3072]{1,0:T(8,128)(2,1)}, bf16[256,768]{1,0:T(8,128)(2,1)}, f32[256,768]...) custom-call(bf16[256,768]{1,0:T(8,128)(2,1)} %get-tuple-element.93.g, ...), custom_call_target="tpu_custom_call" | custom-call | tf_op jit(solution)/shard_map/tail/pallas_call | solution.py:668
  215.6 26.7 %turn.1 = (bf16[256,768]{1,0:T(8,128)(2,1)}, bf16[256,768]{1,0:T(8,128)(2,1)}, bf16[256,3072]{1,0:T(8,128)(2,1)}, bf16[256,768]{1,0:T(8,128)(2,1)}, bf16[256,768...) custom-call(bf16[256,768]{1,0:T(8,128)(2,1)} %get-tuple-element.101., ...), custom_call_target="tpu_custom_call" | custom-call | tf_op jit(solution)/shard_map/turn/pallas_call | solution.py:668
  242.3 21.9 %attend_back.2 = (bf16[256,768]{1,0:T(8,128)(2,1)}, bf16[8,6,256,128]{3,2,1,0:T(8,128)(2,1)}, bf16[8,6,256,128]{3,2,1,0:T(8,128)(2,1)}, bf16[16,768]{1,0:T(8,128)(2,1)}) custom-call(s32[144]{0:T(256)} %reshape.204.picks_ref, s32[1]{0:T(128)} %bitcast.13.first_ref, bf16[256,768]{1,0:T(8,128)(2,1)} %get-tuple-element.111.q_ref, ...), custom_call_target="tpu_custom_call" | custom-call | tf_op jit(solution)/shard_map/attend_back/pallas_call | solution.py:602
  264.2 44.8 %sum_rows.2 = (bf16[256,2304]{1,0:T(8,128)(2,1)}, f32[8,768]{1,0:T(8,128)}, f32[24,768]{1,0:T(8,128)}, f32[24,1536]{1,0:T(8,128)}) custom-call(bf16[256,768]{1,0:T(8,128)(2,1)} %get-tuple-element.118.given_0_, bf16[16,768]{1,0:T(8,128)(2,1)} %get-tuple-element.119.given_1_, bf16[256,768]{1,0:T(8,128)(2,1)} %get-tuple-element.120.given_2_, ...), custom_call_target="tpu_custom_call" | custom-call | tf_op jit(solution)/shard_map/sum_rows/pallas_call | solution.py:668
  309.0 65.0 %sum_weights.2 = (f32[24,2304]{1,0:T(8,128)}, f32[24,1536]{1,0:T(8,128)}, f32[96,768]{1,0:T(8,128)}, bf16[256,768]{1,0:T(8,128)(2,1)}, bf16[256,3072]{1,0:T(8,12...) custom-call(bf16[256,768]{1,0:T(8,128)(2,1)} %get-tuple-element.110., ...), custom_call_target="tpu_custom_call" | custom-call | tf_op jit(solution)/shard_map/sum_weights/pallas_call | solution.py:668
  374.0 21.9 %attend_back.3 = (bf16[256,768]{1,0:T(8,128)(2,1)}, bf16[8,6,256,128]{3,2,1,0:T(8,128)(2,1)}, bf16[8,6,256,128]{3,2,1,0:T(8,128)(2,1)}, bf16[16,768]{1,0:T(8,128)(2,1)}) custom-call(s32[144]{0:T(256)} %reshape.204.picks_ref, s32[1]{0:T(128)} %bitcast.13.first_ref, bf16[256,768]{1,0:T(8,128)(2,1)} %get-tuple-element.108.q_ref, ...), custom_call_target="tpu_custom_call" | custom-call | tf_op jit(solution)/shard_map/attend_back/pallas_call | solution.py:602
  396.0 43.7 %sum_rows.3 = (bf16[256,2304]{1,0:T(8,128)(2,1)}, f32[8,768]{1,0:T(8,128)}, f32[24,768]{1,0:T(8,128)}, f32[24,1536]{1,0:T(8,128)}) custom-call(bf16[256,768]{1,0:T(8,128)(2,1)} %get-tuple-element.141.given_0_, bf16[16,768]{1,0:T(8,128)(2,1)} %get-tuple-element.142.given_1_, bf16[256,768]{1,0:T(8,128)(2,1)} %get-tuple-element.143.given_2_, ...), custom_call_target="tpu_custom_call" | custom-call | tf_op jit(solution)/shard_map/sum_rows/pallas_call | solution.py:668
  439.7 0.7 add.36
  441.0 0.7 reduce.11
  441.7 0.7 reduce.10
  443.2 0.7 pad_maximum_fusion.given_8_
  443.9 66.3 %sum_weights.3 = (f32[24,2304]{1,0:T(8,128)}, f32[24,1536]{1,0:T(8,128)}, f32[96,768]{1,0:T(8,128)}, f32[16,128]{1,0:T(8,128)}, f32[256,768]{1,0:T(8,128)}) custom-call(bf16[256,768]{1,0:T(8,128)(2,1)} %bitcast.41, bf16[256,2304]{1,0:T(8,128)(2,1)} %get-tuple-element.149.given_1_, bf16[256,768]{1,0:T(8,128)(2,1)} %get-tuple-element.147.given_6_.given_2_, ...), custom_call_target="tpu_custom_call" | custom-call | tf_op jit(solution)/shard_map/sum_weights/pallas_call | solution.py:668
  510.2 3.3 assemble.1
  513.5 1.3 slice.24
  514.8 1.3 copy.36
  516.1 0.8 slice.26
  516.8 0.6 reshape.213
  517.5 0.7 copy.42
  (32 shorter events, 1.9 us)
Async XLA Ops:
  396.0 43.7 %copy-start.3 = (f32[8,768]{1,0:T(8,128)S(1)}, f32[8,768]{1,0:T(8,128)}, u32[]{:S(2)}) copy-start(f32[8,768]{1,0:T(8,128)} %get-tuple-element.154) | copy-start | bytes 73732
  396.0 44.5 %copy-start.1 = (f32[8,768]{1,0:T(8,128)S(1)}, f32[8,768]{1,0:T(8,128)}, u32[]{:S(2)}) copy-start(f32[8,768]{1,0:T(8,128)} %get-tuple-element.157) | copy-start | bytes 73732
  396.0 44.5 %copy-start.2 = (f32[8,768]{1,0:T(8,128)S(1)}, f32[8,768]{1,0:T(8,128)}, u32[]{:S(2)}) copy-start(f32[8,768]{1,0:T(8,128)} %get-tuple-element.158) | copy-start | bytes 73732
  396.0 45.0 %copy-start.5 = (f32[1,3072]{1,0:T(1,128)S(1)}, f32[1,3072]{1,0:T(1,128)}, u32[]{:S(2)}) copy-start(f32[1,3072]{1,0:T(1,128)} %get-tuple-element.156) | copy-start | bytes 36868
  396.0 45.7 %copy-start.4 = (f32[1,3072]{1,0:T(1,128)S(1)}, f32[1,3072]{1,0:T(1,128)}, u32[]{:S(2)}) copy-start(f32[1,3072]{1,0:T(1,128)} %get-tuple-element.159) | copy-start | bytes 36868
  443.9 73.6 %copy-start = (bf16[256,768]{1,0:T(8,128)(2,1)S(1)}, bf16[256,768]{1,0:T(8,128)(2,1)}, u32[]{:S(2)}) copy-start(bf16[256,768]{1,0:T(8,128)(2,1)} %get-tuple-element.107) | copy-start | bytes 1179652

commit v5 on v4

--- a/solution.py
+++ b/solution.py
@@ -14,43 +14,43 @@
 
 
 HEAD_PLACES = SimpleNamespace(
-    begins=(0, 3, 1, 2, 16, 28, 46, 15, 31),
+    begins=(1, 4, 3, 2, 0, 64, 61, 56, 14),
     arrivals=(
-        (5, 4, 17, 6, 18, 19, 32, 20, 33, 30, 54, 34, 55, 56, 77),
-        (12, 13, 29),
-        (7, 14, 21, 8, 22, 23, 35, 24, 36, 37, 57, 38, 58, 59, 78),
-        (9, 10, 50, 11, 25, 26, 39, 27, 40, 41, 60, 42, 62, 61, 79),
-        (47, 48, 72, 49, 73, 74, 102, 75, 103, 104, 125, 105, 126, 127, 143),
-        (51, 52, 80, 53, 83, 81, 106, 82, 93, 107, 128, 108, 129, 130, 142),
-        (76, 70, 98, 71, 99, 100, 119, 101, 120, 121, 140, 122, 144, 141, 150),
-        (43, 66, 94, 44, 67, 95, 117, 45, 68, 91, 118, 69, 96, 133, 139),
-        (64, 87, 115, 65, 88, 109, 136, 63, 89, 114, 137, 90, 116, 138, 147),
-        (112, 113, 134),
-        (123, 124, 145),
-        (131, 132, 146),
-        (110, 111, 135),
+        (8, 9, 21, 10, 22, 20, 36, 23, 37, 38, 55, 39, 51, 52, 62),
+        (15, 16, 27),
+        (19, 17, 29, 18, 30, 31, 45, 32, 57, 46, 58, 47, 59, 60, 69),
+        (11, 12, 44, 13, 24, 25, 40, 26, 41, 42, 53, 43, 75, 54, 63),
+        (5, 6, 28, 7, 33, 34, 65, 35, 66, 67, 86, 68, 87, 88, 106),
+        (81, 82, 136, 83, 107, 108, 131, 100, 130, 132, 143, 118, 144, 142, 150),
+        (78, 79, 103, 80, 104, 105, 127, 102, 128, 129, 145, 125, 140, 141, 149),
+        (76, 99, 119, 74, 96, 117, 135, 77, 97, 122, 126, 98, 120, 138, 146),
+        (48, 70, 111, 50, 71, 91, 121, 49, 72, 92, 114, 73, 90, 115, 133),
+        (113, 109, 134),
+        (123, 124, 139),
+        (94, 95, 116),
+        (110, 112, 137),
     ),
     project=84,
-    attention=(148, 149, 151),
+    attention=(147, 148, 151),
 )
 TAIL_PLACES = SimpleNamespace(
-    begins=(0, 2, 5, 11, 29, 22, 3),
+    begins=(1, 2, 0, 14, 38, 43, 4),
     arrivals=(
-        (6, 7, 17, 8, 18, 19, 31, 20, 32, 33, 44, 34, 45, 46, 65),
-        (15, 10, 23, 14, 26, 24, 37, 28, 38, 39, 52, 40, 53, 54, 64),
-        (27, 36, 59, 16, 60, 61, 86, 62, 113, 88, 115, 85, 123, 112, 133),
-        (51, 48, 74, 47, 68, 73, 90, 63, 95, 93, 120, 96, 129, 121, 134),
-        (57, 55, 81, 56, 82, 83, 107, 87, 108, 104, 124, 92, 126, 131, 137),
-        (49, 76, 102, 50, 105, 110, 119, 58, 77, 103, 118, 70, 99, 125, 138),
-        (41, 71, 98, 42, 78, 91, 114, 43, 79, 94, 128, 69, 97, 117, 135),
-        (100, 101, 127),
-        (122, 109, 130),
-        (116, 111, 132),
-        (80, 75, 106),
+        (10, 11, 19, 12, 20, 21, 61, 22, 42, 33, 47, 34, 49, 48, 70),
+        (32, 13, 23, 17, 26, 24, 46, 25, 35, 36, 52, 37, 53, 54, 71),
+        (6, 7, 27, 8, 28, 29, 62, 31, 50, 56, 74, 51, 72, 75, 92),
+        (39, 40, 63, 41, 64, 65, 93, 66, 86, 87, 108, 88, 129, 110, 128),
+        (55, 59, 80, 60, 111, 89, 105, 79, 118, 98, 122, 101, 123, 124, 137),
+        (67, 81, 95, 68, 82, 106, 125, 69, 83, 112, 126, 84, 107, 127, 136),
+        (57, 78, 100, 73, 96, 102, 120, 58, 99, 113, 121, 91, 103, 119, 132),
+        (97, 104, 130),
+        (114, 115, 135),
+        (133, 117, 134),
+        (116, 109, 131),
     ),
-    steps=(1, 4, 9, 12, 13, 21, 25, 30, 35),
-    project=66,
-    attention=(136, 139, 140),
+    steps=(3, 5, 9, 15, 16, 18, 30, 44, 45),
+    project=76,
+    attention=(138, 139, 140),
 )
 ROWS_PLACES = SimpleNamespace(
     rows=(
@@ -1042,6 +1042,9 @@
 ROW_BLOCK = 64
 
 
+WIDE_D, WIDE_FF = 384, 512
+
+
 def tail_steps(refs):
     rows, hidden = refs.resid.shape[0], refs.shifts.shape[1]
 
@@ -1049,11 +1052,11 @@
         refs.ready("resid", "w_out")
 
         def act(i):
-            at = span(i, 256)
+            at = span(i, WIDE_D)
             own = refs.resid[:, at].astype(jnp.float32)
             refs.sum[:, at] = own + product(refs.mixed[...], refs.w_out[:, at]) + refs.bias[2:3, at]
 
-        over(D // 256, act)
+        over(D // WIDE_D, act)
         refs.save("mixed")
 
     def norm_one():
@@ -1069,7 +1072,7 @@
 
     def up(first, count):
         def act(i):
-            at = span(first + i, 256)
+            at = span(first + i, WIDE_FF)
             u = product(refs.y_low[...], refs.w_up[:, at]) + refs.shifts[0:1, at]
             share = 0.5 + 0.5 * lax.erf(u * (0.5 ** 0.5))
             refs.a_low[:, at] = (u * share).astype(jnp.bfloat16)
@@ -1083,10 +1086,10 @@
         refs.save("a_low", "slope")
 
         def act(i):
-            at = span(i, 256)
+            at = span(i, WIDE_D)
             refs.sum[:, at] = refs.sum[:, at] + product(refs.a_low[...], refs.w_down[:, at]) + refs.bias[4:5, at]
 
-        over(D // 256, act)
+        over(D // WIDE_D, act)
 
     def norm_two():
         def act(i):
@@ -1100,8 +1103,9 @@
         over(rows // ROW_BLOCK, act)
         refs.save("n2", "inv2", "z", "z_low")
 
-    quarter = hidden // 256 // 4
-    return [out, norm_one] + [partial(up, k * quarter, quarter) for k in range(4)] + [down, norm_two]
+    ends = [hidden // WIDE_FF * k // 4 for k in range(5)]
+    ups = [partial(up, a, b - a) for a, b in zip(ends, ends[1:])]
+    return [out, norm_one] + ups + [down, norm_two]
 
 
 def tail_ins(mixed, part, resid, vectors, shifts, weights):
@@ -1213,7 +1217,7 @@
 
     def down(first, count):
         def act(i):
-            at = span(first + i, 256)
+            at = span(first + i, WIDE_FF)
             du = product_nt(refs.dr2_low[...], w_down[at]) * refs.slope[:, at].astype(jnp.float32)
             refs.du_low[:, at] = du.astype(jnp.bfloat16)
             refs.hidden_totals[0:1, at] = jnp.sum(du, axis=0, keepdims=True)
@@ -1225,10 +1229,10 @@
         waits[1]()
 
         def act(i):
-            at = span(i, 256)
+            at = span(i, WIDE_D)
             refs.work[:, at] = refs.work[:, at] + product_nt(refs.du_low[...], w_up[at])
 
-        over(D // 256, act)
+        over(D // WIDE_D, act)
 
     def norm_one():
         refs.ready("n1", "inv1")
@@ -1249,13 +1253,13 @@
         waits[2]()
 
         def act(i):
-            at = span(i, 256)
+            at = span(i, WIDE_D)
             refs.cot[:, at] = product_nt(refs.dr1_low[...], w_out[at]).astype(jnp.bfloat16)
 
-        over(D // 256, act)
+        over(D // WIDE_D, act)
         refs.save("cot")
 
-    half = hidden // 256 // 2
+    half = hidden // WIDE_FF // 2
     return [norm_two, partial(down, 0, half), partial(down, half, half), up, norm_one, out]
 
 
@@ -1358,16 +1362,17 @@
 
 def weight_grad(left, right, into, first=0):
     share = into.shape[1]
+    width = WIDE_FF if into.shape[2] % WIDE_FF == 0 else WIDE_D
     count = 384 // share
 
     def act(i):
-        across = into.shape[2] // 256
-        rows, at = i // across, span(i % across, 256)
-        acc = product_tn(left[:, span(rows, 384)], right[:, span(i % across, 256, first)])
+        across = into.shape[2] // width
+        rows, at = i // across, span(i % across, width)
+        acc = product_tn(left[:, span(rows, 384)], right[:, pl.ds(pl.multiple_of(first + i % across * width, WIDE), width)])
         for k in range(count):
             into[rows * count + k, :, at] = acc[k * share : (k + 1) * share].astype(into.dtype)
 
-    over(left.shape[1] // 384 * (into.shape[2] // 256), act)
+    over(left.shape[1] // 384 * (into.shape[2] // width), act)
 
 
 class Sums:
@@ -1579,10 +1584,10 @@
             refs.ready("proj", "up_dr1")
 
             def act(i):
-                at = span(i, 256)
+                at = span(i, WIDE_D)
                 refs.dx[:, at] = refs.up_dr1[:, at] + product_nt(refs.proj[...], v_qkv[at])
 
-            over(D // 256, act)
+            over(D // WIDE_D, act)
             refs.save("dx")
             if below is not None:
                 load_up.start()

time: 527 us -> 520 us (0.987)
  no operation moved by 1% of the time
where the time goes in v5:
time: 520 us; the launch traced here: 515 us
  Pallas kernels  495 us (95%)
  local copies, waits for them, and re-layouts  14.3 us (3%)
    pallas_call x7, Pallas kernels, call(): pl.pallas_call(run, out_shape=[jax.ShapeDtypeStruct(shape, dtype) for sha...  448 us
    pallas_call x2, Pallas kernels, attend_back(): pl.pallas_call(attend_back_kernel, grid_spec=pltpu.PrefetchScalarGridSpec...  43.8 us

profile of v5, /device:TPU:0, one launch (start us, length us, event | category | flops | bytes accessed | tf_op | source)
XLA Modules:
  0.0 515.4 jit_solution(18234317707838478472)
XLA Ops:
  0.6 0.7 convert_reduce_fusion
  1.4 0.7 pad_maximum_fusion.1.given_1_
  2.1 0.7 reshape.195
  2.9 0.7 copy.26
  3.7 1.3 pad.16.given_4_
  5.0 0.8 copy.28
  5.8 0.6 pad.15.given_3_
  6.5 0.8 copy.25
  7.2 0.7 reshape.204.picks_ref
  8.1 0.6 pad_add_fusion.given_2_.given_9_
  8.7 103.9 %first_head.1 = (f32[2,8,768]{2,1,0:T(8,128)}, f32[8,768]{1,0:T(8,128)}, f32[4,192,128]{2,1,0:T(8,128)}, bf16[256,768]{1,0:T(8,128)(2,1)}, bf16[8,12,4,64,128]{4...) custom-call(bf16[256,768]{1,0:T(8,128)(2,1)} %bitcast.39, ...), custom_call_target="tpu_custom_call" | custom-call | tf_op jit(solution)/shard_map/first_head/pallas_call | solution.py:668
  112.6 0.8 reshape.197
  113.5 0.7 squeeze.14.given_4_
  114.3 0.7 squeeze.13.given_4_
  115.0 108.5 %tail.1 = (bf16[256,768]{1,0:T(8,128)(2,1)}, bf16[256,768]{1,0:T(8,128)(2,1)}, bf16[256,3072]{1,0:T(8,128)(2,1)}, bf16[256,768]{1,0:T(8,128)(2,1)}, f32[256,768]...) custom-call(bf16[256,768]{1,0:T(8,128)(2,1)} %get-tuple-element.93.g, ...), custom_call_target="tpu_custom_call" | custom-call | tf_op jit(solution)/shard_map/tail/pallas_call | solution.py:668
  223.5 24.7 %turn.1 = (bf16[256,768]{1,0:T(8,128)(2,1)}, bf16[256,768]{1,0:T(8,128)(2,1)}, bf16[256,3072]{1,0:T(8,128)(2,1)}, bf16[256,768]{1,0:T(8,128)(2,1)}, bf16[256,768...) custom-call(bf16[256,768]{1,0:T(8,128)(2,1)} %get-tuple-element.101., ...), custom_call_target="tpu_custom_call" | custom-call | tf_op jit(solution)/shard_map/turn/pallas_call | solution.py:668
  248.2 21.9 %attend_back.2 = (bf16[256,768]{1,0:T(8,128)(2,1)}, bf16[8,6,256,128]{3,2,1,0:T(8,128)(2,1)}, bf16[8,6,256,128]{3,2,1,0:T(8,128)(2,1)}, bf16[16,768]{1,0:T(8,128)(2,1)}) custom-call(s32[144]{0:T(256)} %reshape.204.picks_ref, s32[1]{0:T(128)} %bitcast.13.first_ref, bf16[256,768]{1,0:T(8,128)(2,1)} %get-tuple-element.111.q_ref, ...), custom_call_target="tpu_custom_call" | custom-call | tf_op jit(solution)/shard_map/attend_back/pallas_call | solution.py:602
  270.1 44.5 %sum_rows.2 = (bf16[256,2304]{1,0:T(8,128)(2,1)}, f32[8,768]{1,0:T(8,128)}, f32[24,768]{1,0:T(8,128)}, f32[24,1536]{1,0:T(8,128)}) custom-call(bf16[256,768]{1,0:T(8,128)(2,1)} %get-tuple-element.118.given_0_, bf16[16,768]{1,0:T(8,128)(2,1)} %get-tuple-element.119.given_1_, bf16[256,768]{1,0:T(8,128)(2,1)} %get-tuple-element.120.given_2_, ...), custom_call_target="tpu_custom_call" | custom-call | tf_op jit(solution)/shard_map/sum_rows/pallas_call | solution.py:668
  314.7 61.3 %sum_weights.2 = (f32[24,2304]{1,0:T(8,128)}, f32[24,1536]{1,0:T(8,128)}, f32[96,768]{1,0:T(8,128)}, bf16[256,768]{1,0:T(8,128)(2,1)}, bf16[256,3072]{1,0:T(8,12...) custom-call(bf16[256,768]{1,0:T(8,128)(2,1)} %get-tuple-element.110., ...), custom_call_target="tpu_custom_call" | custom-call | tf_op jit(solution)/shard_map/sum_weights/pallas_call | solution.py:668
  376.0 21.9 %attend_back.3 = (bf16[256,768]{1,0:T(8,128)(2,1)}, bf16[8,6,256,128]{3,2,1,0:T(8,128)(2,1)}, bf16[8,6,256,128]{3,2,1,0:T(8,128)(2,1)}, bf16[16,768]{1,0:T(8,128)(2,1)}) custom-call(s32[144]{0:T(256)} %reshape.204.picks_ref, s32[1]{0:T(128)} %bitcast.13.first_ref, bf16[256,768]{1,0:T(8,128)(2,1)} %get-tuple-element.108.q_ref, ...), custom_call_target="tpu_custom_call" | custom-call | tf_op jit(solution)/shard_map/attend_back/pallas_call | solution.py:602
  397.9 42.6 %sum_rows.3 = (bf16[256,2304]{1,0:T(8,128)(2,1)}, f32[8,768]{1,0:T(8,128)}, f32[24,768]{1,0:T(8,128)}, f32[24,1536]{1,0:T(8,128)}) custom-call(bf16[256,768]{1,0:T(8,128)(2,1)} %get-tuple-element.141.given_0_, bf16[16,768]{1,0:T(8,128)(2,1)} %get-tuple-element.142.given_1_, bf16[256,768]{1,0:T(8,128)(2,1)} %get-tuple-element.143.given_2_, ...), custom_call_target="tpu_custom_call" | custom-call | tf_op jit(solution)/shard_map/sum_rows/pallas_call | solution.py:668
  440.5 0.7 add.36
  441.8 0.7 reduce.11
  442.5 0.7 reduce.10
  444.0 0.7 pad_maximum_fusion.given_8_
  444.7 62.5 %sum_weights.3 = (f32[24,2304]{1,0:T(8,128)}, f32[24,1536]{1,0:T(8,128)}, f32[96,768]{1,0:T(8,128)}, f32[16,128]{1,0:T(8,128)}, f32[256,768]{1,0:T(8,128)}) custom-call(bf16[256,768]{1,0:T(8,128)(2,1)} %bitcast.41, bf16[256,2304]{1,0:T(8,128)(2,1)} %get-tuple-element.149.given_1_, bf16[256,768]{1,0:T(8,128)(2,1)} %get-tuple-element.147.given_6_.given_2_, ...), custom_call_target="tpu_custom_call" | custom-call | tf_op jit(solution)/shard_map/sum_weights/pallas_call | solution.py:668
  507.2 3.3 assemble.1
  510.5 1.3 slice.24
  511.7 1.3 copy.36
  513.0 0.8 slice.26
  513.8 0.6 reshape.213
  514.5 0.7 copy.42
  (32 shorter events, 1.9 us)
Async XLA Ops:
  397.9 42.6 %copy-start.3 = (f32[8,768]{1,0:T(8,128)S(1)}, f32[8,768]{1,0:T(8,128)}, u32[]{:S(2)}) copy-start(f32[8,768]{1,0:T(8,128)} %get-tuple-element.154) | copy-start | bytes 73732
  397.9 43.4 %copy-start.1 = (f32[8,768]{1,0:T(8,128)S(1)}, f32[8,768]{1,0:T(8,128)}, u32[]{:S(2)}) copy-start(f32[8,768]{1,0:T(8,128)} %get-tuple-element.157) | copy-start | bytes 73732
  397.9 43.4 %copy-start.2 = (f32[8,768]{1,0:T(8,128)S(1)}, f32[8,768]{1,0:T(8,128)}, u32[]{:S(2)}) copy-start(f32[8,768]{1,0:T(8,128)} %get-tuple-element.158) | copy-start | bytes 73732
  397.9 43.9 %copy-start.5 = (f32[1,3072]{1,0:T(1,128)S(1)}, f32[1,3072]{1,0:T(1,128)}, u32[]{:S(2)}) copy-start(f32[1,3072]{1,0:T(1,128)} %get-tuple-element.156) | copy-start | bytes 36868
  397.9 44.6 %copy-start.4 = (f32[1,3072]{1,0:T(1,128)S(1)}, f32[1,3072]{1,0:T(1,128)}, u32[]{:S(2)}) copy-start(f32[1,3072]{1,0:T(1,128)} %get-tuple-element.159) | copy-start | bytes 36868
  444.7 69.7 %copy-start = (bf16[256,768]{1,0:T(8,128)(2,1)S(1)}, bf16[256,768]{1,0:T(8,128)(2,1)}, u32[]{:S(2)}) copy-start(bf16[256,768]{1,0:T(8,128)(2,1)} %get-tuple-element.107) | copy-start | bytes 1179652

commit v6 on v5

--- a/solution.py
+++ b/solution.py
@@ -1045,18 +1045,18 @@
 WIDE_D, WIDE_FF = 384, 512
 
 
-def tail_steps(refs):
+def tail_steps(refs, wide_d, wide_ff):
     rows, hidden = refs.resid.shape[0], refs.shifts.shape[1]
 
     def out():
         refs.ready("resid", "w_out")
 
         def act(i):
-            at = span(i, WIDE_D)
+            at = span(i, wide_d)
             own = refs.resid[:, at].astype(jnp.float32)
             refs.sum[:, at] = own + product(refs.mixed[...], refs.w_out[:, at]) + refs.bias[2:3, at]
 
-        over(D // WIDE_D, act)
+        over(D // wide_d, act)
         refs.save("mixed")
 
     def norm_one():
@@ -1072,7 +1072,7 @@
 
     def up(first, count):
         def act(i):
-            at = span(first + i, WIDE_FF)
+            at = span(first + i, wide_ff)
             u = product(refs.y_low[...], refs.w_up[:, at]) + refs.shifts[0:1, at]
             share = 0.5 + 0.5 * lax.erf(u * (0.5 ** 0.5))
             refs.a_low[:, at] = (u * share).astype(jnp.bfloat16)
@@ -1086,10 +1086,10 @@
         refs.save("a_low", "slope")
 
         def act(i):
-            at = span(i, WIDE_D)
+            at = span(i, wide_d)
             refs.sum[:, at] = refs.sum[:, at] + product(refs.a_low[...], refs.w_down[:, at]) + refs.bias[4:5, at]
 
-        over(D // WIDE_D, act)
+        over(D // wide_d, act)
 
     def norm_two():
         def act(i):
@@ -1103,7 +1103,7 @@
         over(rows // ROW_BLOCK, act)
         refs.save("n2", "inv2", "z", "z_low")
 
-    ends = [hidden // WIDE_FF * k // 4 for k in range(5)]
+    ends = [hidden // wide_ff * k // 4 for k in range(5)]
     ups = [partial(up, a, b - a) for a, b in zip(ends, ends[1:])]
     return [out, norm_one] + ups + [down, norm_two]
 
@@ -1146,7 +1146,7 @@
         gathering.begin(refs)
         sequence.prepare(refs)
         refs.bias = refs.vectors.at[0]
-        steps = [finish] + tail_steps(refs)
+        steps = [finish] + tail_steps(refs, 256, 256)
 
         def project_now():
             refs.bias = refs.vectors.at[1]
@@ -1281,7 +1281,7 @@
         refs.bias = refs.vectors.at[1]
         greet((), depth, spread=True, collect=True)
         to_first(refs.own_part, refs.mixed, refs.t_send, refs.t_recv)()
-        for step in tail_steps(refs):
+        for step in tail_steps(refs, WIDE_D, WIDE_FF):
             step()
         refs.totals[...] = jnp.zeros_like(refs.totals)
         for step in back_steps(refs, lambda at: refs.d_out[at].astype(jnp.float32), refs.w_down, refs.w_up, refs.w_out):

time: 520 us -> 516 us (level)
  Pallas kernels: 495 us -> 486 us
    pallas_call x7, Pallas kernels: 448 us -> 439 us  [call(): pl.pallas_call(run, out_shape=[jax.ShapeDtypeStruct(shape, dtype) for sha...]
where the time goes in v6:
time: 516 us; the launch traced here: 507 us
  Pallas kernels  486 us (94%)
  local copies, waits for them, and re-layouts  14.3 us (3%)
    pallas_call x7, Pallas kernels, call(): pl.pallas_call(run, out_shape=[jax.ShapeDtypeStruct(shape, dtype) for sha...  439 us
    pallas_call x2, Pallas kernels, attend_back(): pl.pallas_call(attend_back_kernel, grid_spec=pltpu.PrefetchScalarGridSpec...  43.8 us

profile of v6, /device:TPU:0, one launch (start us, length us, event | category | flops | bytes accessed | tf_op | source)
XLA Modules:
  0.0 506.7 jit_solution(2855775713841060665)
XLA Ops:
  0.6 0.7 convert_reduce_fusion
  1.4 0.7 pad_maximum_fusion.1.given_1_
  2.1 0.7 reshape.195
  2.9 0.7 copy.26
  3.7 1.3 pad.16.given_4_
  5.0 0.8 copy.28
  5.8 0.6 pad.15.given_3_
  6.5 0.8 copy.25
  7.2 0.7 reshape.204.picks_ref
  8.1 0.6 pad_add_fusion.given_2_.given_9_
  8.7 103.9 %first_head.1 = (f32[2,8,768]{2,1,0:T(8,128)}, f32[8,768]{1,0:T(8,128)}, f32[4,192,128]{2,1,0:T(8,128)}, bf16[256,768]{1,0:T(8,128)(2,1)}, bf16[8,12,4,64,128]{4...) custom-call(bf16[256,768]{1,0:T(8,128)(2,1)} %bitcast.39, ...), custom_call_target="tpu_custom_call" | custom-call | tf_op jit(solution)/shard_map/first_head/pallas_call | solution.py:668
  112.6 0.8 reshape.197
  113.5 0.7 squeeze.14.given_4_
  114.3 0.7 squeeze.13.given_4_
  115.0 99.4 %tail.1 = (bf16[256,768]{1,0:T(8,128)(2,1)}, bf16[256,768]{1,0:T(8,128)(2,1)}, bf16[256,3072]{1,0:T(8,128)(2,1)}, bf16[256,768]{1,0:T(8,128)(2,1)}, f32[256,768]...) custom-call(bf16[256,768]{1,0:T(8,128)(2,1)} %get-tuple-element.93.g, ...), custom_call_target="tpu_custom_call" | custom-call | tf_op jit(solution)/shard_map/tail/pallas_call | solution.py:668
  214.5 24.5 %turn.1 = (bf16[256,768]{1,0:T(8,128)(2,1)}, bf16[256,768]{1,0:T(8,128)(2,1)}, bf16[256,3072]{1,0:T(8,128)(2,1)}, bf16[256,768]{1,0:T(8,128)(2,1)}, bf16[256,768...) custom-call(bf16[256,768]{1,0:T(8,128)(2,1)} %get-tuple-element.101., ...), custom_call_target="tpu_custom_call" | custom-call | tf_op jit(solution)/shard_map/turn/pallas_call | solution.py:668
  239.0 21.9 %attend_back.2 = (bf16[256,768]{1,0:T(8,128)(2,1)}, bf16[8,6,256,128]{3,2,1,0:T(8,128)(2,1)}, bf16[8,6,256,128]{3,2,1,0:T(8,128)(2,1)}, bf16[16,768]{1,0:T(8,128)(2,1)}) custom-call(s32[144]{0:T(256)} %reshape.204.picks_ref, s32[1]{0:T(128)} %bitcast.13.first_ref, bf16[256,768]{1,0:T(8,128)(2,1)} %get-tuple-element.111.q_ref, ...), custom_call_target="tpu_custom_call" | custom-call | tf_op jit(solution)/shard_map/attend_back/pallas_call | solution.py:602
  260.9 44.9 %sum_rows.2 = (bf16[256,2304]{1,0:T(8,128)(2,1)}, f32[8,768]{1,0:T(8,128)}, f32[24,768]{1,0:T(8,128)}, f32[24,1536]{1,0:T(8,128)}) custom-call(bf16[256,768]{1,0:T(8,128)(2,1)} %get-tuple-element.118.given_0_, bf16[16,768]{1,0:T(8,128)(2,1)} %get-tuple-element.119.given_1_, bf16[256,768]{1,0:T(8,128)(2,1)} %get-tuple-element.120.given_2_, ...), custom_call_target="tpu_custom_call" | custom-call | tf_op jit(solution)/shard_map/sum_rows/pallas_call | solution.py:668
  305.8 61.1 %sum_weights.2 = (f32[24,2304]{1,0:T(8,128)}, f32[24,1536]{1,0:T(8,128)}, f32[96,768]{1,0:T(8,128)}, bf16[256,768]{1,0:T(8,128)(2,1)}, bf16[256,3072]{1,0:T(8,12...) custom-call(bf16[256,768]{1,0:T(8,128)(2,1)} %get-tuple-element.110., ...), custom_call_target="tpu_custom_call" | custom-call | tf_op jit(solution)/shard_map/sum_weights/pallas_call | solution.py:668
  366.9 21.9 %attend_back.3 = (bf16[256,768]{1,0:T(8,128)(2,1)}, bf16[8,6,256,128]{3,2,1,0:T(8,128)(2,1)}, bf16[8,6,256,128]{3,2,1,0:T(8,128)(2,1)}, bf16[16,768]{1,0:T(8,128)(2,1)}) custom-call(s32[144]{0:T(256)} %reshape.204.picks_ref, s32[1]{0:T(128)} %bitcast.13.first_ref, bf16[256,768]{1,0:T(8,128)(2,1)} %get-tuple-element.108.q_ref, ...), custom_call_target="tpu_custom_call" | custom-call | tf_op jit(solution)/shard_map/attend_back/pallas_call | solution.py:602
  388.9 42.6 %sum_rows.3 = (bf16[256,2304]{1,0:T(8,128)(2,1)}, f32[8,768]{1,0:T(8,128)}, f32[24,768]{1,0:T(8,128)}, f32[24,1536]{1,0:T(8,128)}) custom-call(bf16[256,768]{1,0:T(8,128)(2,1)} %get-tuple-element.141.given_0_, bf16[16,768]{1,0:T(8,128)(2,1)} %get-tuple-element.142.given_1_, bf16[256,768]{1,0:T(8,128)(2,1)} %get-tuple-element.143.given_2_, ...), custom_call_target="tpu_custom_call" | custom-call | tf_op jit(solution)/shard_map/sum_rows/pallas_call | solution.py:668
  431.5 0.7 add.36
  432.8 0.7 reduce.11
  433.5 0.7 reduce.10
  435.0 0.7 pad_maximum_fusion.given_8_
  435.8 62.5 %sum_weights.3 = (f32[24,2304]{1,0:T(8,128)}, f32[24,1536]{1,0:T(8,128)}, f32[96,768]{1,0:T(8,128)}, f32[16,128]{1,0:T(8,128)}, f32[256,768]{1,0:T(8,128)}) custom-call(bf16[256,768]{1,0:T(8,128)(2,1)} %bitcast.41, bf16[256,2304]{1,0:T(8,128)(2,1)} %get-tuple-element.149.given_1_, bf16[256,768]{1,0:T(8,128)(2,1)} %get-tuple-element.147.given_6_.given_2_, ...), custom_call_target="tpu_custom_call" | custom-call | tf_op jit(solution)/shard_map/sum_weights/pallas_call | solution.py:668
  498.2 3.3 assemble.1
  501.5 1.3 slice.24
  502.8 1.3 copy.36
  504.1 0.8 slice.26
  504.8 0.6 reshape.213
  505.5 0.7 copy.42
  (32 shorter events, 1.9 us)
Async XLA Ops:
  388.9 42.6 %copy-start.3 = (f32[8,768]{1,0:T(8,128)S(1)}, f32[8,768]{1,0:T(8,128)}, u32[]{:S(2)}) copy-start(f32[8,768]{1,0:T(8,128)} %get-tuple-element.154) | copy-start | bytes 73732
  388.9 43.4 %copy-start.1 = (f32[8,768]{1,0:T(8,128)S(1)}, f32[8,768]{1,0:T(8,128)}, u32[]{:S(2)}) copy-start(f32[8,768]{1,0:T(8,128)} %get-tuple-element.157) | copy-start | bytes 73732
  388.9 43.4 %copy-start.2 = (f32[8,768]{1,0:T(8,128)S(1)}, f32[8,768]{1,0:T(8,128)}, u32[]{:S(2)}) copy-start(f32[8,768]{1,0:T(8,128)} %get-tuple-element.158) | copy-start | bytes 73732
  388.9 43.9 %copy-start.5 = (f32[1,3072]{1,0:T(1,128)S(1)}, f32[1,3072]{1,0:T(1,128)}, u32[]{:S(2)}) copy-start(f32[1,3072]{1,0:T(1,128)} %get-tuple-element.156) | copy-start | bytes 36868
  388.9 44.6 %copy-start.4 = (f32[1,3072]{1,0:T(1,128)S(1)}, f32[1,3072]{1,0:T(1,128)}, u32[]{:S(2)}) copy-start(f32[1,3072]{1,0:T(1,128)} %get-tuple-element.159) | copy-start | bytes 36868
  435.7 69.7 %copy-start = (bf16[256,768]{1,0:T(8,128)(2,1)S(1)}, bf16[256,768]{1,0:T(8,128)(2,1)}, u32[]{:S(2)}) copy-start(bf16[256,768]{1,0:T(8,128)(2,1)} %get-tuple-element.107) | copy-start | bytes 1179652

commit v7 on v6

--- a/solution.py
+++ b/solution.py
@@ -14,24 +14,24 @@
 
 
 HEAD_PLACES = SimpleNamespace(
-    begins=(1, 4, 3, 2, 0, 64, 61, 56, 14),
+    begins=(0, 3, 1, 2, 16, 28, 46, 15, 31),
     arrivals=(
-        (8, 9, 21, 10, 22, 20, 36, 23, 37, 38, 55, 39, 51, 52, 62),
-        (15, 16, 27),
-        (19, 17, 29, 18, 30, 31, 45, 32, 57, 46, 58, 47, 59, 60, 69),
-        (11, 12, 44, 13, 24, 25, 40, 26, 41, 42, 53, 43, 75, 54, 63),
-        (5, 6, 28, 7, 33, 34, 65, 35, 66, 67, 86, 68, 87, 88, 106),
-        (81, 82, 136, 83, 107, 108, 131, 100, 130, 132, 143, 118, 144, 142, 150),
-        (78, 79, 103, 80, 104, 105, 127, 102, 128, 129, 145, 125, 140, 141, 149),
-        (76, 99, 119, 74, 96, 117, 135, 77, 97, 122, 126, 98, 120, 138, 146),
-        (48, 70, 111, 50, 71, 91, 121, 49, 72, 92, 114, 73, 90, 115, 133),
-        (113, 109, 134),
-        (123, 124, 139),
-        (94, 95, 116),
-        (110, 112, 137),
+        (5, 4, 17, 6, 18, 19, 32, 20, 33, 30, 54, 34, 55, 56, 77),
+        (12, 13, 29),
+        (7, 14, 21, 8, 22, 23, 35, 24, 36, 37, 57, 38, 58, 59, 78),
+        (9, 10, 50, 11, 25, 26, 39, 27, 40, 41, 60, 42, 62, 61, 79),
+        (47, 48, 72, 49, 73, 74, 102, 75, 103, 104, 125, 105, 126, 127, 143),
+        (51, 52, 80, 53, 83, 81, 106, 82, 93, 107, 128, 108, 129, 130, 142),
+        (76, 70, 98, 71, 99, 100, 119, 101, 120, 121, 140, 122, 144, 141, 150),
+        (43, 66, 94, 44, 67, 95, 117, 45, 68, 91, 118, 69, 96, 133, 139),
+        (64, 87, 115, 65, 88, 109, 136, 63, 89, 114, 137, 90, 116, 138, 147),
+        (112, 113, 134),
+        (123, 124, 145),
+        (131, 132, 146),
+        (110, 111, 135),
     ),
     project=84,
-    attention=(147, 148, 151),
+    attention=(148, 149, 151),
 )
 TAIL_PLACES = SimpleNamespace(
     begins=(1, 2, 0, 14, 38, 43, 4),

time: 516 us -> 514 us (level)
  no operation moved by 1% of the time
where the time goes in v7:
time: 514 us; the launch traced here: 505 us
  Pallas kernels  484 us (94%)
  local copies, waits for them, and re-layouts  14.3 us (3%)
    pallas_call x7, Pallas kernels, call(): pl.pallas_call(run, out_shape=[jax.ShapeDtypeStruct(shape, dtype) for sha...  437 us
    pallas_call x2, Pallas kernels, attend_back(): pl.pallas_call(attend_back_kernel, grid_spec=pltpu.PrefetchScalarGridSpec...  43.8 us

profile of v7, /device:TPU:0, one launch (start us, length us, event | category | flops | bytes accessed | tf_op | source)
XLA Modules:
  0.0 504.6 jit_solution(8640977525537866248)
XLA Ops:
  0.6 0.7 convert_reduce_fusion
  1.4 0.7 pad_maximum_fusion.1.given_1_
  2.1 0.7 reshape.195
  2.9 0.7 copy.26
  3.7 1.3 pad.16.given_4_
  5.0 0.8 copy.28
  5.8 0.6 pad.15.given_3_
  6.5 0.8 copy.25
  7.2 0.7 reshape.204.picks_ref
  8.1 0.6 pad_add_fusion.given_2_.given_9_
  8.7 100.9 %first_head.1 = (f32[2,8,768]{2,1,0:T(8,128)}, f32[8,768]{1,0:T(8,128)}, f32[4,192,128]{2,1,0:T(8,128)}, bf16[256,768]{1,0:T(8,128)(2,1)}, bf16[8,12,4,64,128]{4...) custom-call(bf16[256,768]{1,0:T(8,128)(2,1)} %bitcast.39, ...), custom_call_target="tpu_custom_call" | custom-call | tf_op jit(solution)/shard_map/first_head/pallas_call | solution.py:668
  109.6 0.8 reshape.197
  110.5 0.7 squeeze.14.given_4_
  111.3 0.7 squeeze.13.given_4_
  112.0 99.9 %tail.1 = (bf16[256,768]{1,0:T(8,128)(2,1)}, bf16[256,768]{1,0:T(8,128)(2,1)}, bf16[256,3072]{1,0:T(8,128)(2,1)}, bf16[256,768]{1,0:T(8,128)(2,1)}, f32[256,768]...) custom-call(bf16[256,768]{1,0:T(8,128)(2,1)} %get-tuple-element.93.g, ...), custom_call_target="tpu_custom_call" | custom-call | tf_op jit(solution)/shard_map/tail/pallas_call | solution.py:668
  211.9 25.0 %turn.1 = (bf16[256,768]{1,0:T(8,128)(2,1)}, bf16[256,768]{1,0:T(8,128)(2,1)}, bf16[256,3072]{1,0:T(8,128)(2,1)}, bf16[256,768]{1,0:T(8,128)(2,1)}, bf16[256,768...) custom-call(bf16[256,768]{1,0:T(8,128)(2,1)} %get-tuple-element.101., ...), custom_call_target="tpu_custom_call" | custom-call | tf_op jit(solution)/shard_map/turn/pallas_call | solution.py:668
  236.9 21.9 %attend_back.2 = (bf16[256,768]{1,0:T(8,128)(2,1)}, bf16[8,6,256,128]{3,2,1,0:T(8,128)(2,1)}, bf16[8,6,256,128]{3,2,1,0:T(8,128)(2,1)}, bf16[16,768]{1,0:T(8,128)(2,1)}) custom-call(s32[144]{0:T(256)} %reshape.204.picks_ref, s32[1]{0:T(128)} %bitcast.13.first_ref, bf16[256,768]{1,0:T(8,128)(2,1)} %get-tuple-element.111.q_ref, ...), custom_call_target="tpu_custom_call" | custom-call | tf_op jit(solution)/shard_map/attend_back/pallas_call | solution.py:602
  258.8 44.9 %sum_rows.2 = (bf16[256,2304]{1,0:T(8,128)(2,1)}, f32[8,768]{1,0:T(8,128)}, f32[24,768]{1,0:T(8,128)}, f32[24,1536]{1,0:T(8,128)}) custom-call(bf16[256,768]{1,0:T(8,128)(2,1)} %get-tuple-element.118.given_0_, bf16[16,768]{1,0:T(8,128)(2,1)} %get-tuple-element.119.given_1_, bf16[256,768]{1,0:T(8,128)(2,1)} %get-tuple-element.120.given_2_, ...), custom_call_target="tpu_custom_call" | custom-call | tf_op jit(solution)/shard_map/sum_rows/pallas_call | solution.py:668
  303.7 61.1 %sum_weights.2 = (f32[24,2304]{1,0:T(8,128)}, f32[24,1536]{1,0:T(8,128)}, f32[96,768]{1,0:T(8,128)}, bf16[256,768]{1,0:T(8,128)(2,1)}, bf16[256,3072]{1,0:T(8,12...) custom-call(bf16[256,768]{1,0:T(8,128)(2,1)} %get-tuple-element.110., ...), custom_call_target="tpu_custom_call" | custom-call | tf_op jit(solution)/shard_map/sum_weights/pallas_call | solution.py:668
  364.9 21.9 %attend_back.3 = (bf16[256,768]{1,0:T(8,128)(2,1)}, bf16[8,6,256,128]{3,2,1,0:T(8,128)(2,1)}, bf16[8,6,256,128]{3,2,1,0:T(8,128)(2,1)}, bf16[16,768]{1,0:T(8,128)(2,1)}) custom-call(s32[144]{0:T(256)} %reshape.204.picks_ref, s32[1]{0:T(128)} %bitcast.13.first_ref, bf16[256,768]{1,0:T(8,128)(2,1)} %get-tuple-element.108.q_ref, ...), custom_call_target="tpu_custom_call" | custom-call | tf_op jit(solution)/shard_map/attend_back/pallas_call | solution.py:602
  386.9 42.6 %sum_rows.3 = (bf16[256,2304]{1,0:T(8,128)(2,1)}, f32[8,768]{1,0:T(8,128)}, f32[24,768]{1,0:T(8,128)}, f32[24,1536]{1,0:T(8,128)}) custom-call(bf16[256,768]{1,0:T(8,128)(2,1)} %get-tuple-element.141.given_0_, bf16[16,768]{1,0:T(8,128)(2,1)} %get-tuple-element.142.given_1_, bf16[256,768]{1,0:T(8,128)(2,1)} %get-tuple-element.143.given_2_, ...), custom_call_target="tpu_custom_call" | custom-call | tf_op jit(solution)/shard_map/sum_rows/pallas_call | solution.py:668
  429.5 0.7 add.36
  430.7 0.7 reduce.11
  431.4 0.7 reduce.10
  433.0 0.7 pad_maximum_fusion.given_8_
  433.7 62.5 %sum_weights.3 = (f32[24,2304]{1,0:T(8,128)}, f32[24,1536]{1,0:T(8,128)}, f32[96,768]{1,0:T(8,128)}, f32[16,128]{1,0:T(8,128)}, f32[256,768]{1,0:T(8,128)}) custom-call(bf16[256,768]{1,0:T(8,128)(2,1)} %bitcast.41, bf16[256,2304]{1,0:T(8,128)(2,1)} %get-tuple-element.149.given_1_, bf16[256,768]{1,0:T(8,128)(2,1)} %get-tuple-element.147.given_6_.given_2_, ...), custom_call_target="tpu_custom_call" | custom-call | tf_op jit(solution)/shard_map/sum_weights/pallas_call | solution.py:668
  496.2 3.3 assemble.1
  499.4 1.3 slice.24
  500.7 1.3 copy.36
  502.0 0.8 slice.26
  502.8 0.6 reshape.213
  503.4 0.7 copy.42
  (32 shorter events, 1.9 us)
Async XLA Ops:
  386.8 42.6 %copy-start.3 = (f32[8,768]{1,0:T(8,128)S(1)}, f32[8,768]{1,0:T(8,128)}, u32[]{:S(2)}) copy-start(f32[8,768]{1,0:T(8,128)} %get-tuple-element.154) | copy-start | bytes 73732
  386.8 43.4 %copy-start.1 = (f32[8,768]{1,0:T(8,128)S(1)}, f32[8,768]{1,0:T(8,128)}, u32[]{:S(2)}) copy-start(f32[8,768]{1,0:T(8,128)} %get-tuple-element.157) | copy-start | bytes 73732
  386.8 43.4 %copy-start.2 = (f32[8,768]{1,0:T(8,128)S(1)}, f32[8,768]{1,0:T(8,128)}, u32[]{:S(2)}) copy-start(f32[8,768]{1,0:T(8,128)} %get-tuple-element.158) | copy-start | bytes 73732
  386.8 43.9 %copy-start.5 = (f32[1,3072]{1,0:T(1,128)S(1)}, f32[1,3072]{1,0:T(1,128)}, u32[]{:S(2)}) copy-start(f32[1,3072]{1,0:T(1,128)} %get-tuple-element.156) | copy-start | bytes 36868
  386.8 44.6 %copy-start.4 = (f32[1,3072]{1,0:T(1,128)S(1)}, f32[1,3072]{1,0:T(1,128)}, u32[]{:S(2)}) copy-start(f32[1,3072]{1,0:T(1,128)} %get-tuple-element.159) | copy-start | bytes 36868
  433.7 69.7 %copy-start = (bf16[256,768]{1,0:T(8,128)(2,1)S(1)}, bf16[256,768]{1,0:T(8,128)(2,1)}, u32[]{:S(2)}) copy-start(bf16[256,768]{1,0:T(8,128)(2,1)} %get-tuple-element.107) | copy-start | bytes 1179652
